TPU v7x, 256 devices: a whole 4x4x8 slice. The times are simulated.
256 devices in a mesh: lat: 4 (over x_lo, core), lon: 64 (over y, x_hi, z).
Axes of the slice: x: 4 (x_hi: 2, x_lo: 2; x = x_hi * 2 + x_lo), y: 4, z: 8, core: 2. Of those that a mesh axis runs over, the one named last changes fastest.
Arguments:
- state: bfloat16 [64, 512, 256], P('lat', 'lon'), may hold values from -45 to 45
- cotangent: bfloat16 [64, 512, 256], P('lat', 'lon'), may hold values from -5 to 5
- land_sea: int32 [64, 512], P('lat', 'lon'), may hold values 0 or 1
- regime: int32 [4, 64, 16, 8, 1], P('lat', 'lon'), may hold values from 0 to 15; in each aligned block of 128 rows (0 to 127, 128 to 255, ..., all dimensions but the last counted through in order) at most 16 rows name the same one
- first_gain: float32 [256], replicated, may hold values from 0.1 to 1.9
- second_gain: float32 [256], replicated, may hold values from 0.1 to 1.9
- project_weight: bfloat16 [256, 768], replicated, may hold values from -0.375 to 0.375
- out_weight: bfloat16 [256, 256], replicated, may hold values from -0.375 to 0.375
- pos_bias: float32 [8, 49], replicated, may hold values from -3 to 315
- up_weight: bfloat16 [256, 16384], P(None, 'lon'), may hold values from -0.375 to 0.375
- down_weight: bfloat16 [16384, 256], P('lon'), may hold values from -0.1875 to 0.1875
Outputs:
- block_out: bfloat16 [64, 512, 256], P('lat', 'lon')
- grad_up: float32 [256, 16384], P(None, 'lon')
- grad_down: float32 [16384, 256], P('lon')
Inputs may be any that keep to these rules, and one draw needn't show every extreme that they name: Among the 16 x 8 cells of one tile at most 16 share a regime, and some tile has exactly 16 cells of one regime. Every regime occurs somewhere.
All inputs are finite; a program needn't handle non-finite values. No bound on the sum of `land_sea` on one device may be relied on, other than what follows from the above.
Results may differ from a plain program's by a relative error of at most 0.022.
Values may be sent and summed in bfloat16 or wider, within the bound.
No kernel may reach another device: no remote copies, remote signals or barrier semaphores. Data moves between devices by JAX's collectives and lax.ppermute only.
A program may use at most 64 MiB of HBM per device.

v0:
```python
import math

import jax
import jax.numpy as jnp
import numpy as np
from jax import lax
from jax.experimental import pallas as pl
from jax.experimental.pallas import tpu as pltpu
from jax.sharding import PartitionSpec as P

WINDOW = 7
REACH = WINDOW // 2
EXPERTS = 16
ROWS = 16
COLS = 8
CELLS = ROWS * COLS
D = 256
HEADS = 8
HD = 32
CAP = 16
SLOTS = EXPERTS * CAP
UNITS = 256
EXT = ROWS + 2 * REACH
LAND = 1024.0
FAR = -1e30
F32 = jnp.float32
BF = jnp.bfloat16
VMEM_LIMIT = 48 * 1024 * 1024


def vmem(count):
    return [pl.BlockSpec(memory_space=pltpu.VMEM)] * count


def dot(a, b):
    return lax.dot_general(a, b, (((1,), (0,)), ((), ())), preferred_element_type=F32)


def dot_t(a, b):
    return lax.dot_general(a, b, (((1,), (1,)), ((), ())), preferred_element_type=F32)


def t_dot(a, b):
    return lax.dot_general(a, b, (((0,), (0,)), ((), ())), preferred_element_type=F32)


def layer_norm(values, gain):
    mean_val = jnp.mean(values, axis=-1, keepdims=True)
    spread = jnp.mean(jnp.square(values - mean_val), axis=-1, keepdims=True)
    return ((values - mean_val) * lax.rsqrt(spread + 1e-05) * gain).astype(BF)


def tap_tables():
    column = np.concatenate([np.arange(8) + 3, np.arange(4) - 1, np.arange(4) + 11])
    table = np.zeros((WINDOW * WINDOW, 16, 8, 16), np.float32)
    for q in range(16):
        for a in range(8):
            for slot in range(16):
                da, db = a - q // 8, column[slot] - q % 8
                if 0 <= da < WINDOW and 0 <= db < WINDOW:
                    table[da * WINDOW + db, q, a, slot] = 1.0
    outside = (1.0 - table.sum(0)) * FAR
    return table.reshape(WINDOW * WINDOW, 2048), outside.reshape(1, 2048).astype(np.float32)


def prepare_kernel(pos_ref, taps_ref, outside_ref, labels_ref, cot_ref, land_ref, bias_ref, place_ref, sendc_ref):
    pos = pos_ref[...]
    high = pos.astype(BF)
    rest = pos - high.astype(F32)
    middle = rest.astype(BF)
    low = (rest - middle.astype(F32)).astype(BF)
    taps = taps_ref[...]
    bias = dot(high, taps) + dot(middle, taps) + dot(low, taps) + outside_ref[...]
    for q in range(16):
        bias_ref[q * 8 : q * 8 + 8, :] = bias[:, q * 128 : q * 128 + 128]
    labels = labels_ref[...]
    named = lax.broadcasted_iota(jnp.int32, (EXPERTS, CELLS), 0) == labels
    named = jnp.where(named, 1.0, 0.0)
    earlier = lax.broadcasted_iota(jnp.int32, (CELLS, CELLS), 0) < lax.broadcasted_iota(
        jnp.int32, (CELLS, CELLS), 1
    )
    before = dot(named.astype(BF), jnp.where(earlier, 1.0, 0.0).astype(BF))
    rank = jnp.sum(before * named, axis=0, keepdims=True)
    slot = labels * CAP + rank.astype(jnp.int32)
    place = lax.broadcasted_iota(jnp.int32, (SLOTS, CELLS), 0) == slot
    place = jnp.where(place, 1.0, 0.0).astype(BF)
    place_ref[...] = place
    tangent = cot_ref[...].astype(F32).reshape(CELLS, D) * land_ref[...].astype(F32)
    sendc_ref[...] = dot(place, tangent.astype(BF)).astype(BF)


def attention_kernel(
    own_ref,
    up_ref,
    down_ref,
    left_ref,
    right_ref,
    land_ref,
    gain1_ref,
    gain2_ref,
    project_ref,
    out_ref,
    bias_ref,
    place_ref,
    sendc_ref,
    residual_ref,
    send_ref,
    ext_ref,
    pen_ref,
):
    lat = lax.axis_index("lat")
    top = jnp.where(lat == 0, FAR, 0.0).astype(F32)
    bottom = jnp.where(lat == lax.axis_size("lat") - 1, FAR, 0.0).astype(F32)
    own3 = own_ref[...].astype(F32)
    up = up_ref[...].astype(F32)
    down = down_ref[...].astype(F32)
    left = left_ref[...].astype(F32)
    right = right_ref[...].astype(F32)

    def marked(piece):
        return jnp.where(piece[:, :, 0:128] > 0.5 * LAND, FAR, 0.0)

    ext_ref[0:REACH, 0:8, :] = up
    ext_ref[REACH : REACH + ROWS, 0:8, :] = own3
    ext_ref[REACH + ROWS : EXT, 0:8, :] = down
    ext_ref[:, 8:12, :] = left
    ext_ref[:, 12:16, :] = right
    land = land_ref[...].reshape(ROWS, COLS, 1)
    pen_ref[0:REACH, 0:8, :] = marked(up)
    pen_ref[REACH : REACH + ROWS, 0:8, :] = jnp.broadcast_to(
        jnp.where(land > 0, 0.0, FAR), (ROWS, COLS, 128)
    )
    pen_ref[REACH + ROWS : EXT, 0:8, :] = marked(down)
    pen_ref[:, 8:12, :] = marked(left)
    pen_ref[:, 12:16, :] = marked(right)
    pen_ref[0:REACH] = pen_ref[0:REACH] + top
    pen_ref[REACH + ROWS : EXT] = pen_ref[REACH + ROWS : EXT] + bottom
    own = own3.reshape(CELLS, D)
    gain1 = gain1_ref[...]
    normed = layer_norm(ext_ref[...].reshape(EXT * 16, D), gain1)
    keyvals = dot(normed, project_ref[:, D : 3 * D]).astype(BF)
    queries = dot(layer_norm(own, gain1), project_ref[:, 0:D]).astype(BF)
    pen = pen_ref[...].reshape(EXT * 16, 128).astype(BF)

    row = lax.broadcasted_iota(jnp.int32, (128, D), 0)
    lane = lax.broadcasted_iota(jnp.int32, (128, D), 1)
    head_mask = jnp.where(lane // HD == row % HEADS, 1.0, 0.0)
    spread = jnp.where(
        lax.broadcasted_iota(jnp.int32, (128, 16), 0) // HEADS
        == lax.broadcasted_iota(jnp.int32, (128, 16), 1),
        1.0,
        0.0,
    ).astype(BF)
    gather = jnp.where(
        lax.broadcasted_iota(jnp.int32, (16, 128), 1) // HEADS
        == lax.broadcasted_iota(jnp.int32, (16, 128), 0),
        1.0,
        0.0,
    ).astype(BF)
    row = lax.broadcasted_iota(jnp.int32, (128, 128), 0)
    lane = lax.broadcasted_iota(jnp.int32, (128, 128), 1)
    first_lane = jnp.where(lane == 0, 1.0, 0.0).astype(BF)
    query = row // HEADS
    centre = lane == (query // COLS + REACH) * 16 + query % COLS
    bias = bias_ref[...]
    scale = 1.0 / math.sqrt(HD)
    pieces = []
    for pair in range(ROWS // 2):
        keys = keyvals[32 * pair : 32 * pair + 128, 0:D]
        values = keyvals[32 * pair : 32 * pair + 128, D : 2 * D]
        wide = (dot(spread, queries[16 * pair : 16 * pair + 16]) * head_mask).astype(BF)
        closed = dot_t(first_lane, pen[32 * pair : 32 * pair + 128])
        scores = dot_t(wide, keys) * scale + bias + jnp.where(centre, 0.0, closed)
        raw = jnp.exp(scores - jnp.max(scores, axis=1, keepdims=True))
        weights = (raw / jnp.sum(raw, axis=1, keepdims=True)).astype(BF)
        taken = (dot(weights, values) * head_mask).astype(BF)
        pieces.append(dot(gather, taken))
    attended = jnp.concatenate(pieces, axis=0).astype(BF)
    residual = (own + dot(attended, out_ref[...])).astype(BF)
    residual_ref[...] = residual
    second = layer_norm(residual.astype(F32), gain2_ref[...])
    send_ref[:, 0:D] = dot(place_ref[...], second).astype(BF)
    send_ref[:, D : 2 * D] = sendc_ref[...]


def gelu_parts(hidden):
    half = 0.5 * (1.0 + lax.erf(hidden * 0.7071067811865476))
    slope = half + hidden * jnp.exp(-0.5 * hidden * hidden) * 0.3989422804014327
    return hidden * half, slope


def expert_kernel(got_ref, own_ref, *refs):
    weight_refs = (own_ref,) + refs[0:3]
    outputs_ref, keep_ref, give_ref, grad_ref = refs[3:]
    inputs = got_ref[:, 0:D]
    tangents = got_ref[:, D : 2 * D]
    outputs = jnp.zeros((SLOTS, D), F32)
    for member in range(4):
        up = weight_refs[member][0]
        down = weight_refs[member][1]
        active, slope = gelu_parts(dot(inputs, up))
        active = active.astype(BF)
        outputs = outputs + dot(active, down)
        pre_act = (dot_t(tangents, down) * slope).astype(BF)
        grad_ref[member, 0] = t_dot(inputs, pre_act)
        grad_ref[member, 1] = t_dot(active, tangents)
    outputs_ref[...] = outputs.astype(BF)
    lat = lax.axis_index("lat")
    for far in range(2):
        for other in range(2):
            start = pl.multiple_of(jnp.bitwise_xor(lat, 2 * far + other) * 64, 64)
            chunk = grad_ref[:, :, pl.ds(start, 64), :]
            if other:
                give_ref[far] = chunk.astype(BF)
            else:
                keep_ref[far] = chunk


def combine_kernel(returned_ref, place_ref, residual_ref, land_ref, block_ref):
    rows = lax.dot_general(
        place_ref[...],
        returned_ref[...],
        (((0,), (0,)), ((), ())),
        preferred_element_type=F32,
    )
    land = land_ref[...].astype(F32)
    block_ref[...] = (
        (land * (residual_ref[...].astype(F32) + rows)).astype(BF).reshape(ROWS, COLS, D)
    )


def gather_kernel(own_ref, a_ref, b_ref, c_ref, up_ref, down_ref):
    lat = lax.axis_index("lat")
    for mask, ref in enumerate((own_ref, a_ref, b_ref, c_ref)):
        start = pl.multiple_of(jnp.bitwise_xor(lat, mask) * 64, 64)
        up_ref[pl.ds(start, 64), :] = ref[0].astype(F32)
        down_ref[pl.ds(start, 64), :] = ref[1].astype(F32)


def call(kernel, outs, args, scratch=()):
    return pl.pallas_call(
        kernel,
        out_shape=[jax.ShapeDtypeStruct(shape, dtype) for shape, dtype in outs],
        in_specs=vmem(len(args)),
        out_specs=vmem(len(outs)),
        scratch_shapes=list(scratch),
        compiler_params=pltpu.CompilerParams(vmem_limit_bytes=VMEM_LIMIT),
    )(*args)


def shift(value, axis, step, closed):
    count = lax.axis_size(axis)
    pairs = [(i, (i + step) % count) for i in range(count) if closed or 0 <= i + step < count]
    return lax.ppermute(value, axis, pairs)


def swap(value, axis, mask):
    return lax.ppermute(value, axis, [(i, i ^ mask) for i in range(lax.axis_size(axis))])


def expert_groups():
    return [[8 * (e // 2) + (k if e % 2 == 0 else 7 - k) for e in range(EXPERTS)] for k in range(4)]


def exchange(value):
    return lax.all_to_all(
        value, "lon", 0, 0, axis_index_groups=expert_groups(), tiled=True
    )


def on_device(
    state,
    cotangent,
    land_sea,
    regime,
    first_gain,
    second_gain,
    project_weight,
    out_weight,
    pos_bias,
    up_weight,
    down_weight,
):
    marked = jnp.where(land_sea[:, :, None] > 0, state, jnp.asarray(LAND, BF))
    up = shift(marked[ROWS - REACH :], "lat", 1, False)
    down = shift(marked[:REACH], "lat", -1, False)
    tall = jnp.concatenate([up, marked, down], axis=0)
    left = shift(tall[:, COLS - 4 :], "lon", 1, True)
    right = shift(tall[:, :4], "lon", -1, True)

    land_column = land_sea.reshape(CELLS, 1)
    taps, outside = tap_tables()
    bias, place, sendc = call(
        prepare_kernel,
        [((128, 128), F32), ((SLOTS, CELLS), BF), ((SLOTS, D), BF)],
        (
            pos_bias,
            jnp.asarray(taps, BF),
            jnp.asarray(outside),
            regime.reshape(1, CELLS),
            cotangent,
            land_column,
        ),
    )
    weights = [jnp.stack([up_weight, down_weight])]
    for mask in (1, 2, 3):
        weights.append(swap(weights[0], "lon", mask))

    residual, send = call(
        attention_kernel,
        [((CELLS, D), BF), ((SLOTS, 2 * D), BF)],
        (
            state,
            up,
            down,
            left,
            right,
            land_column,
            first_gain.reshape(1, D),
            second_gain.reshape(1, D),
            project_weight,
            out_weight,
            bias,
            place,
            sendc,
        ),
        (pltpu.VMEM((EXT, 16, D), F32), pltpu.VMEM((EXT, 16, 128), F32)),
    )
    got = exchange(send.reshape(EXPERTS, CAP, 2 * D)).reshape(SLOTS, 2 * D)
    outputs, keep, give = call(
        expert_kernel,
        [((SLOTS, D), BF), ((2, 4, 2, 64, D), F32), ((2, 4, 2, 64, D), BF)],
        (got, *weights),
        (pltpu.VMEM((4, 2, 256, D), F32),),
    )
    returned = exchange(outputs.reshape(EXPERTS, CAP, D)).reshape(SLOTS, D)

    near = swap(give, "lat", 1)
    far = swap((keep[1] + near[1].astype(F32)).astype(BF), "lat", 2)
    part = keep[0] + near[0].astype(F32) + far.astype(F32)
    total = part[0]
    for mask in (1, 2, 3):
        total = total + swap(part[mask].astype(BF), "lon", mask).astype(F32)
    total = total.astype(BF)
    grad_up, grad_down = call(
        gather_kernel,
        [((D, UNITS), F32), ((UNITS, D), F32)],
        (total, *[swap(total, "lat", mask) for mask in (1, 2, 3)]),
    )
    (block,) = call(
        combine_kernel,
        [((ROWS, COLS, D), BF)],
        (returned, place, residual, land_column),
    )
    return block, grad_up, grad_down


def solution(mesh):
    placed = (
        P("lat", "lon", None),
        P("lat", "lon", None),
        P("lat", "lon"),
        P("lat", "lon", None, None, None),
        P(),
        P(),
        P(),
        P(),
        P(),
        P(None, "lon"),
        P("lon", None),
    )
    return jax.shard_map(
        on_device,
        mesh=mesh,
        in_specs=placed,
        out_specs=(P("lat", "lon", None), P(None, "lon"), P("lon", None)),
        check_vma=False,
    )
```

profile of v0, /device:TPU:32, one launch (start us, length us, event | category | flops | bytes accessed | tf_op | source)
XLA Modules:
  0.0 98.7 jit_solution(425317037630627496)
XLA Ops:
  0.6 0.7 broadcast_compare_fusion
  1.3 0.1 copy.22
  1.4 0.9 broadcast_select_fusion
  2.3 0.0 copy-start.11
  2.4 0.0 copy-start.12
  2.4 0.0 copy-start.4
  2.4 0.0 copy-start.5
  2.4 0.0 copy-start.6
  2.4 1.4 %collective-permute-start.1 = (bf16[3,8,256]{2,1,0:T(8,128)(2,1)S(1)}, bf16[3,8,256]{2,1,0:T(8,128)(2,1)S(1)}, u32[]{:S(2)}, u32[]{:S(2)}) collective-permute-start(bf16[3,8,256]{2,1,0:T(8,128)(2,1)S(1)} %get-tuple-element.30), channel_id=1, source_target_pairs={{64,0},{128,64},{192,128},{65,1},{129,65},{193,129},{66,2},{130,66... | collective-permute-start | bytes 36872 | tf_op jit(solution)/shard_map/ppermute | solution.py:254
  3.8 0.0 copy-start.2
  3.9 0.0 copy-start
  3.9 3.2 %collective-permute-start = (bf16[3,8,256]{2,1,0:T(8,128)(2,1)S(1)}, bf16[3,8,256]{2,1,0:T(8,128)(2,1)S(1)}, u32[]{:S(2)}, u32[]{:S(2)}) collective-permute-start(bf16[3,8,256]{2,1,0:T(8,128)(2,1)S(1)} %get-tuple-element.31), channel_id=1, source_target_pairs={{0,64},{64,128},{128,192},{1,65},{65,129},{129,193},{2,66},{66,130... | collective-permute-start | bytes 36872 | tf_op jit(solution)/shard_map/ppermute | solution.py:254
  7.0 0.0 collective-permute-done.1.down_ref
  7.1 0.8 collective-permute-done.up_ref
  7.9 1.9 %collective-permute-start.3 = (bf16[22,4,256]{2,1,0:T(4,128)(2,1)S(1)}, bf16[22,4,256]{2,1,0:T(4,128)(2,1)S(1)}, u32[]{:S(2)}, u32[]{:S(2)}) collective-permute-start(bf16[22,4,256]{2,1,0:T(4,128)(2,1)S(1)} %get-tuple-element.28), channel_id=1, source_target_pairs={{0,63},{1,0},{2,1},{3,2},{4,3},{5,4},{6,5},{7,6},{8,7},{9,8},{10,9... | collective-permute-start | bytes 135176 | tf_op jit(solution)/shard_map/ppermute | solution.py:254
  9.8 0.2 collective-permute-start.2
  10.0 0.0 copy-done.11
  10.0 0.1 copy.23
  10.1 0.0 copy-done.12
  10.1 0.1 copy.24
  10.2 0.1 reshape.43.labels_ref
  10.3 0.1 reshape.48.land_ref
  10.3 0.0 copy-done.4
  10.4 0.0 copy-start.1
  10.4 0.0 copy-start.3
  10.4 0.0 copy-start.8
  10.4 0.4 shard_map.148
  10.8 1.4 %collective-permute-done.3.right_ref = bf16[22,4,256]{2,1,0:T(4,128)(2,1)S(1)} collective-permute-done((bf16[22,4,256]{2,1,0:T(4,128)(2,1)S(1)}, bf16[22,4,256]{2,1,0:T(4,128)(2,1)S(1)}, u32[]{:S(2)}, u32[]{:S(2)}) %collective-permute-start.3) | collective-permute-done | bytes 45088 | tf_op jit(solution)/shard_map/ppermute | solution.py:254
  12.2 9.1 %collective-permute-done.2.left_ref = bf16[22,4,256]{2,1,0:T(4,128)(2,1)S(1)} collective-permute-done((bf16[22,4,256]{2,1,0:T(4,128)(2,1)S(1)}, bf16[22,4,256]{2,1,0:T(4,128)(2,1)S(1)}, u32[]{:S(2)}, u32[]{:S(2)}) %collective-permute-start.2) | collective-permute-done | bytes 45088 | tf_op jit(solution)/shard_map/ppermute | solution.py:254
  21.3 0.0 copy-done
  21.3 0.0 copy-done.3
  21.3 0.7 copy-done.7
  22.0 6.2 %shard_map.149 = (bf16[128,256]{1,0:T(8,128)(2,1)S(1)}, bf16[256,512]{1,0:T(8,128)(2,1)}) custom-call(bf16[16,8,256]{2,1,0:T(8,128)(2,1)S(1)} %copy-done.1, bf16[3,8,256]{2,1,0:T(8,128)(2,1)S(1)} %collective-permute-done.up_ref, bf16[3,8,256]{2,1,0:T(8,128)(2,1)S(1)} %collective-permute-done.1.down_ref, ...), custom_call_target="tpu_custom_call" | custom-call | tf_op jit(solution)/shard_map/pallas_call | solution.py:241
  28.2 4.5 %all-to-all-start = ((bf16[16,16,512]{2,1,0:T(8,128)(2,1)}), bf16[16,16,512]{2,1,0:T(8,128)(2,1)S(1)}, u32[]{:S(2)}, u32[]{:S(2)}) async-start(bf16[16,16,512]{2,1,0:T(8,128)(2,1)} %bitcast.2), calls=%async_computation | async-start | bytes 524288 | tf_op jit(solution)/shard_map/all_to_all | solution.py:266
  32.8 1.1 %collective-permute-start.6 = (bf16[2,256,256]{2,1,0:T(8,128)(2,1)S(1)}, bf16[2,256,256]{2,1,0:T(8,128)(2,1)S(1)}, u32[]{:S(2)}, u32[]{:S(2)}) collective-permute-start(bf16[2,256,256]{2,1,0:T(8,128)(2,1)S(1)} %pad_maximum_fusion.own_ref), channel_id=1, source_target_pairs={{0,3},{1,2},{2,1},{3,0},{4,7},{5,6},{6,5},{7,4},{8,11},{9,10},{10,... | collective-permute-start | bytes 786440 | tf_op jit(solution)/shard_map/ppermute | solution.py:258
  33.9 8.2 %collective-permute-start.5 = (bf16[2,256,256]{2,1,0:T(8,128)(2,1)S(1)}, bf16[2,256,256]{2,1,0:T(8,128)(2,1)S(1)}, u32[]{:S(2)}, u32[]{:S(2)}) collective-permute-start(bf16[2,256,256]{2,1,0:T(8,128)(2,1)S(1)} %pad_maximum_fusion.own_ref), channel_id=1, source_target_pairs={{0,2},{1,3},{2,0},{3,1},{4,6},{5,7},{6,4},{7,5},{8,10},{9,11},{10,... | collective-permute-start | bytes 786440 | tf_op jit(solution)/shard_map/ppermute | solution.py:258
  42.0 0.0 collective-permute-start.4
  42.0 0.0 collective-permute-done.6.refs_2_
  42.1 14.7 %collective-permute-done.5.refs_1_ = bf16[2,256,256]{2,1,0:T(8,128)(2,1)S(1)} collective-permute-done((bf16[2,256,256]{2,1,0:T(8,128)(2,1)S(1)}, bf16[2,256,256]{2,1,0:T(8,128)(2,1)S(1)}, u32[]{:S(2)}, u32[]{:S(2)}) %collective-permute-start.5) | collective-permute-done | bytes 262176 | tf_op jit(solution)/shard_map/ppermute | solution.py:258
  56.8 1.1 %collective-permute-done.4.refs_0_ = bf16[2,256,256]{2,1,0:T(8,128)(2,1)S(1)} collective-permute-done((bf16[2,256,256]{2,1,0:T(8,128)(2,1)S(1)}, bf16[2,256,256]{2,1,0:T(8,128)(2,1)S(1)}, u32[]{:S(2)}, u32[]{:S(2)}) %collective-permute-start.4) | collective-permute-done | bytes 262176 | tf_op jit(solution)/shard_map/ppermute | solution.py:258
  57.8 0.0 all-to-all-done
  57.8 2.1 %shard_map.150 = (bf16[256,256]{1,0:T(8,128)(2,1)}, f32[2,4,2,64,256]{4,3,2,1,0:T(8,128)S(1)}, bf16[2,4,2,64,256]{4,3,2,1,0:T(8,128)(2,1)S(1)}) custom-call(bf16[256,512]{1,0:T(8,128)(2,1)S(1)} %bitcast.33, bf16[2,256,256]{2,1,0:T(8,128)(2,1)S(1)} %pad_maximum_fusion.own_ref, bf16[2,256,256]{2,1,0:T(8,128)(2,1)S(1)} %collective-permute-done.4.refs_0_, ...), custom_call_target="tpu_custom_call" | custom-call | tf_op jit(solution)/shard_map/pallas_call | solution.py:241
  60.0 0.0 collective-permute-start.7
  60.0 1.9 %collective-permute-done.7 = bf16[2,4,2,64,256]{4,3,2,1,0:T(8,128)(2,1)S(1)} collective-permute-done((bf16[2,4,2,64,256]{4,3,2,1,0:T(8,128)(2,1)S(1)}, bf16[2,4,2,64,256]{4,3,2,1,0:T(8,128)(2,1)S(1)}, u32[]{:S(2)}, u32[]{:S(2)}) %collective-permute-start.7) | collective-permute-done | bytes 524320 | tf_op jit(solution)/shard_map/ppermute | solution.py:258
  61.9 0.1 fusion
  62.0 0.3 collective-permute-start.8
  62.3 8.1 %collective-permute-done.8 = bf16[4,2,64,256]{3,2,1,0:T(8,128)(2,1)S(1)} collective-permute-done((bf16[4,2,64,256]{3,2,1,0:T(8,128)(2,1)S(1)}, bf16[4,2,64,256]{3,2,1,0:T(8,128)(2,1)S(1)}, u32[]{:S(2)}, u32[]{:S(2)}) %collective-permute-start.8) | collective-permute-done | bytes 262176 | tf_op jit(solution)/shard_map/ppermute | solution.py:258
  70.4 0.1 fusion.5
  70.5 2.3 %collective-permute-start.9 = (bf16[2,64,256]{2,1,0:T(8,128)(2,1)S(1)}, bf16[2,64,256]{2,1,0:T(8,128)(2,1)S(1)}, u32[]{:S(2)}, u32[]{:S(2)}) collective-permute-start(bf16[2,64,256]{2,1,0:T(8,128)(2,1)S(1)} %get-tuple-element.25), channel_id=1, source_target_pairs={{0,1},{1,0},{2,3},{3,2},{4,5},{5,4},{6,7},{7,6},{8,9},{9,8},{10,11... | collective-permute-start | bytes 196616 | tf_op jit(solution)/shard_map/ppermute | solution.py:258
  72.9 0.6 collective-permute-start.11
  73.5 1.8 %collective-permute-start.10 = (bf16[2,64,256]{2,1,0:T(8,128)(2,1)S(1)}, bf16[2,64,256]{2,1,0:T(8,128)(2,1)S(1)}, u32[]{:S(2)}, u32[]{:S(2)}) collective-permute-start(bf16[2,64,256]{2,1,0:T(8,128)(2,1)S(1)} %get-tuple-element.27), channel_id=1, source_target_pairs={{0,2},{1,3},{2,0},{3,1},{4,6},{5,7},{6,4},{7,5},{8,10},{9,11},{10,... | collective-permute-start | bytes 196616 | tf_op jit(solution)/shard_map/ppermute | solution.py:258
  75.3 9.9 %all-to-all-start.1 = ((bf16[16,16,256]{2,1,0:T(8,128)(2,1)}), bf16[16,16,256]{2,1,0:T(8,128)(2,1)S(1)}, u32[]{:S(2)}, u32[]{:S(2)}) async-start(bf16[16,16,256]{2,1,0:T(8,128)(2,1)} %bitcast.6), calls=%async_computation.1 | async-start | bytes 262144 | tf_op jit(solution)/shard_map/all_to_all | solution.py:266
  85.2 0.0 collective-permute-done.9
  85.2 0.0 collective-permute-done.11
  85.3 0.0 collective-permute-done.10
  85.3 0.1 collective-permute-start.14
  85.4 1.2 %collective-permute-start.13 = (bf16[2,64,256]{2,1,0:T(8,128)(2,1)S(1)}, bf16[2,64,256]{2,1,0:T(8,128)(2,1)S(1)}, u32[]{:S(2)}, u32[]{:S(2)}) collective-permute-start(bf16[2,64,256]{2,1,0:T(8,128)(2,1)S(1)} %fusion.4.own_ref), channel_id=1, source_target_pairs={{0,128},{64,192},{128,0},{192,64},{1,129},{65,193},{129,1},{193,65... | collective-permute-start | bytes 196616 | tf_op jit(solution)/shard_map/ppermute | solution.py:258
  86.6 0.7 collective-permute-start.12
  87.3 9.7 %all-to-all-done.1 = bf16[16,16,256]{2,1,0:T(8,128)(2,1)S(1)} async-done(((bf16[16,16,256]{2,1,0:T(8,128)(2,1)}), bf16[16,16,256]{2,1,0:T(8,128)(2,1)S(1)}, u32[]{:S(2)}, u32[]{:S(2)}) %all-to-all-start.1) | async-done | bytes 131104 | tf_op jit(solution)/shard_map/all_to_all | solution.py:266
  97.0 0.8 shard_map.151
  97.8 0.0 collective-permute-done.14.c_ref
  97.8 0.0 collective-permute-done.13.b_ref
  97.8 0.0 collective-permute-done.12.a_ref
  97.8 0.8 shard_map.152
  (16 shorter events, 0.1 us)
Async XLA Ops:
  2.3 7.7 %copy-start.11 = (s32[16,8]{0,1:T(8,128)S(1)}, s32[16,8]{0,1:T(8,128)}, u32[]{:S(2)}) copy-start(s32[16,8]{0,1:T(8,128)} %param.15) | copy-start | bytes 1540
  2.4 7.7 %copy-start.12 = (s32[1,1,16,8,1]{2,4,3,1,0:T(1,128)S(1)}, s32[1,1,16,8,1]{2,4,3,1,0:T(1,128)}, u32[]{:S(2)}) copy-start(s32[1,1,16,8,1]{2,4,3,1,0:T(1,128)} %param.16) | copy-start | bytes 1540
  2.4 8.0 %copy-start.4 = (bf16[16,8,256]{2,1,0:T(8,128)(2,1)S(1)}, bf16[16,8,256]{2,1,0:T(8,128)(2,1)}, u32[]{:S(2)}) copy-start(bf16[16,8,256]{2,1,0:T(8,128)(2,1)} %cot_ref.1) | copy-start | bytes 196612
  2.4 8.0 %copy-start.5 = (f32[1,2048]{1,0:T(1,128)S(1)}, f32[1,2048]{1,0:T(1,128)}, u32[]{:S(2)}) copy-start(f32[1,2048]{1,0:T(1,128)} %constant.9.clone.outside_ref) | copy-start | bytes 24580
  2.4 8.0 %copy-start.6 = (f32[8,49]{1,0:T(8,128)S(1)}, f32[8,49]{1,0:T(8,128)}, u32[]{:S(2)}) copy-start(f32[8,49]{1,0:T(8,128)} %pos_ref.1) | copy-start | bytes 4708
  2.4 4.6 %collective-permute-start.1 = (bf16[3,8,256]{2,1,0:T(8,128)(2,1)S(1)}, bf16[3,8,256]{2,1,0:T(8,128)(2,1)S(1)}, u32[]{:S(2)}, u32[]{:S(2)}) collective-permute-start(bf16[3,8,256]{2,1,0:T(8,128)(2,1)S(1)} %get-tuple-element.30), channel_id=1, source_target_pairs={{64,0},{128,64},{192,128},{65,1},{129,65},{193,129},{66,2},{130,66... | collective-permute-start | bytes 36872 | tf_op jit(solution)/shard_map/ppermute | solution.py:254
  3.8 6.5 %copy-start.2 = (bf16[49,2048]{1,0:T(8,128)(2,1)S(1)}, bf16[49,2048]{1,0:T(8,128)(2,1)}, u32[]{:S(2)}) copy-start(bf16[49,2048]{1,0:T(8,128)(2,1)} %constant.8.clone.taps_ref) | copy-start | bytes 602116
  3.9 17.4 %copy-start = (bf16[256,768]{1,0:T(8,128)(2,1)S(1)}, bf16[256,768]{1,0:T(8,128)(2,1)}, u32[]{:S(2)}) copy-start(bf16[256,768]{1,0:T(8,128)(2,1)} %project_ref.1) | copy-start | bytes 1179652
  3.9 4.0 %collective-permute-start = (bf16[3,8,256]{2,1,0:T(8,128)(2,1)S(1)}, bf16[3,8,256]{2,1,0:T(8,128)(2,1)S(1)}, u32[]{:S(2)}, u32[]{:S(2)}) collective-permute-start(bf16[3,8,256]{2,1,0:T(8,128)(2,1)S(1)} %get-tuple-element.31), channel_id=1, source_target_pairs={{0,64},{64,128},{128,192},{1,65},{65,129},{129,193},{2,66},{66,130... | collective-permute-start | bytes 36872 | tf_op jit(solution)/shard_map/ppermute | solution.py:254
  7.9 4.3 %collective-permute-start.3 = (bf16[22,4,256]{2,1,0:T(4,128)(2,1)S(1)}, bf16[22,4,256]{2,1,0:T(4,128)(2,1)S(1)}, u32[]{:S(2)}, u32[]{:S(2)}) collective-permute-start(bf16[22,4,256]{2,1,0:T(4,128)(2,1)S(1)} %get-tuple-element.28), channel_id=1, source_target_pairs={{0,63},{1,0},{2,1},{3,2},{4,3},{5,4},{6,5},{7,6},{8,7},{9,8},{10,9... | collective-permute-start | bytes 135176 | tf_op jit(solution)/shard_map/ppermute | solution.py:254
  9.8 11.4 %collective-permute-start.2 = (bf16[22,4,256]{2,1,0:T(4,128)(2,1)S(1)}, bf16[22,4,256]{2,1,0:T(4,128)(2,1)S(1)}, u32[]{:S(2)}, u32[]{:S(2)}) collective-permute-start(bf16[22,4,256]{2,1,0:T(4,128)(2,1)S(1)} %get-tuple-element.29), channel_id=1, source_target_pairs={{0,1},{1,2},{2,3},{3,4},{4,5},{5,6},{6,7},{7,8},{8,9},{9,10},{10,1... | collective-permute-start | bytes 135176 | tf_op jit(solution)/shard_map/ppermute | solution.py:254
  10.4 10.9 %copy-start.1 = (bf16[16,8,256]{2,1,0:T(8,128)(2,1)S(1)}, bf16[16,8,256]{2,1,0:T(8,128)(2,1)}, u32[]{:S(2)}) copy-start(bf16[16,8,256]{2,1,0:T(8,128)(2,1)} %own_ref.1) | copy-start | bytes 196612
  10.4 10.9 %copy-start.3 = (bf16[256,256]{1,0:T(8,128)(2,1)S(1)}, bf16[256,256]{1,0:T(8,128)(2,1)}, u32[]{:S(2)}) copy-start(bf16[256,256]{1,0:T(8,128)(2,1)} %out_ref.1) | copy-start | bytes 393220
  10.4 10.9 %copy-start.8 = (f32[256]{0:T(256)S(1)}, f32[256]{0:T(256)}, u32[]{:S(2)}) copy-start(f32[256]{0:T(256)} %param.18) | copy-start | bytes 3076
  21.3 0.7 copy-start.7
  28.2 4.5 %copy-start.9 = (bf16[256,256]{1,0:T(8,128)(2,1)S(1)}, bf16[256,256]{1,0:T(8,128)(2,1)}, u32[]{:S(2)}) copy-start(bf16[256,256]{1,0:T(8,128)(2,1)} %param.23) | copy-start | bytes 393220
  28.2 4.5 %copy-start.10 = (bf16[256,256]{1,0:T(8,128)(2,1)S(1)}, bf16[256,256]{1,0:T(8,128)(2,1)}, u32[]{:S(2)}) copy-start(bf16[256,256]{1,0:T(8,128)(2,1)} %param.22) | copy-start | bytes 393220
  28.2 29.6 %all-to-all-start = ((bf16[16,16,512]{2,1,0:T(8,128)(2,1)}), bf16[16,16,512]{2,1,0:T(8,128)(2,1)S(1)}, u32[]{:S(2)}, u32[]{:S(2)}) async-start(bf16[16,16,512]{2,1,0:T(8,128)(2,1)} %bitcast.2), calls=%async_computation | async-start | bytes 524288 | tf_op jit(solution)/shard_map/all_to_all | solution.py:266
  32.8 9.3 %collective-permute-start.6 = (bf16[2,256,256]{2,1,0:T(8,128)(2,1)S(1)}, bf16[2,256,256]{2,1,0:T(8,128)(2,1)S(1)}, u32[]{:S(2)}, u32[]{:S(2)}) collective-permute-start(bf16[2,256,256]{2,1,0:T(8,128)(2,1)S(1)} %pad_maximum_fusion.own_ref), channel_id=1, source_target_pairs={{0,3},{1,2},{2,1},{3,0},{4,7},{5,6},{6,5},{7,4},{8,11},{9,10},{10,... | collective-permute-start | bytes 786440 | tf_op jit(solution)/shard_map/ppermute | solution.py:258
  33.9 22.9 %collective-permute-start.5 = (bf16[2,256,256]{2,1,0:T(8,128)(2,1)S(1)}, bf16[2,256,256]{2,1,0:T(8,128)(2,1)S(1)}, u32[]{:S(2)}, u32[]{:S(2)}) collective-permute-start(bf16[2,256,256]{2,1,0:T(8,128)(2,1)S(1)} %pad_maximum_fusion.own_ref), channel_id=1, source_target_pairs={{0,2},{1,3},{2,0},{3,1},{4,6},{5,7},{6,4},{7,5},{8,10},{9,11},{10,... | collective-permute-start | bytes 786440 | tf_op jit(solution)/shard_map/ppermute | solution.py:258
  42.0 15.8 %collective-permute-start.4 = (bf16[2,256,256]{2,1,0:T(8,128)(2,1)S(1)}, bf16[2,256,256]{2,1,0:T(8,128)(2,1)S(1)}, u32[]{:S(2)}, u32[]{:S(2)}) collective-permute-start(bf16[2,256,256]{2,1,0:T(8,128)(2,1)S(1)} %pad_maximum_fusion.own_ref), channel_id=1, source_target_pairs={{0,1},{1,0},{2,3},{3,2},{4,5},{5,4},{6,7},{7,6},{8,9},{9,8},{10,11... | collective-permute-start | bytes 786440 | tf_op jit(solution)/shard_map/ppermute | solution.py:258
  60.0 1.9 %collective-permute-start.7 = (bf16[2,4,2,64,256]{4,3,2,1,0:T(8,128)(2,1)S(1)}, bf16[2,4,2,64,256]{4,3,2,1,0:T(8,128)(2,1)S(1)}, u32[]{:S(2)}, u32[]{:S(2)}) collective-permute-start(bf16[2,4,2,64,256]{4,3,2,1,0:T(8,128)(2,1)S(1)} %get-tuple-element.20), channel_id=1, source_target_pairs={{0,64},{64,0},{128,192},{192,128},{1,65},{65,1},{129,193},{193,129... | collective-permute-start | bytes 1572872 | tf_op jit(solution)/shard_map/ppermute | solution.py:258
  62.0 8.4 %collective-permute-start.8 = (bf16[4,2,64,256]{3,2,1,0:T(8,128)(2,1)S(1)}, bf16[4,2,64,256]{3,2,1,0:T(8,128)(2,1)S(1)}, u32[]{:S(2)}, u32[]{:S(2)}) collective-permute-start(bf16[4,2,64,256]{3,2,1,0:T(8,128)(2,1)S(1)} %fusion), channel_id=1, source_target_pairs={{0,128},{64,192},{128,0},{192,64},{1,129},{65,193},{129,1},{193,65... | collective-permute-start | bytes 786440 | tf_op jit(solution)/shard_map/ppermute | solution.py:258
  70.5 14.7 %collective-permute-start.9 = (bf16[2,64,256]{2,1,0:T(8,128)(2,1)S(1)}, bf16[2,64,256]{2,1,0:T(8,128)(2,1)S(1)}, u32[]{:S(2)}, u32[]{:S(2)}) collective-permute-start(bf16[2,64,256]{2,1,0:T(8,128)(2,1)S(1)} %get-tuple-element.25), channel_id=1, source_target_pairs={{0,1},{1,0},{2,3},{3,2},{4,5},{5,4},{6,7},{7,6},{8,9},{9,8},{10,11... | collective-permute-start | bytes 196616 | tf_op jit(solution)/shard_map/ppermute | solution.py:258
  72.9 12.4 %collective-permute-start.11 = (bf16[2,64,256]{2,1,0:T(8,128)(2,1)S(1)}, bf16[2,64,256]{2,1,0:T(8,128)(2,1)S(1)}, u32[]{:S(2)}, u32[]{:S(2)}) collective-permute-start(bf16[2,64,256]{2,1,0:T(8,128)(2,1)S(1)} %get-tuple-element.26), channel_id=1, source_target_pairs={{0,3},{1,2},{2,1},{3,0},{4,7},{5,6},{6,5},{7,4},{8,11},{9,10},{10,... | collective-permute-start | bytes 196616 | tf_op jit(solution)/shard_map/ppermute | solution.py:258
  73.5 11.8 %collective-permute-start.10 = (bf16[2,64,256]{2,1,0:T(8,128)(2,1)S(1)}, bf16[2,64,256]{2,1,0:T(8,128)(2,1)S(1)}, u32[]{:S(2)}, u32[]{:S(2)}) collective-permute-start(bf16[2,64,256]{2,1,0:T(8,128)(2,1)S(1)} %get-tuple-element.27), channel_id=1, source_target_pairs={{0,2},{1,3},{2,0},{3,1},{4,6},{5,7},{6,4},{7,5},{8,10},{9,11},{10,... | collective-permute-start | bytes 196616 | tf_op jit(solution)/shard_map/ppermute | solution.py:258
  75.3 21.6 %all-to-all-start.1 = ((bf16[16,16,256]{2,1,0:T(8,128)(2,1)}), bf16[16,16,256]{2,1,0:T(8,128)(2,1)S(1)}, u32[]{:S(2)}, u32[]{:S(2)}) async-start(bf16[16,16,256]{2,1,0:T(8,128)(2,1)} %bitcast.6), calls=%async_computation.1 | async-start | bytes 262144 | tf_op jit(solution)/shard_map/all_to_all | solution.py:266
  85.3 12.5 %collective-permute-start.14 = (bf16[2,64,256]{2,1,0:T(8,128)(2,1)S(1)}, bf16[2,64,256]{2,1,0:T(8,128)(2,1)S(1)}, u32[]{:S(2)}, u32[]{:S(2)}) collective-permute-start(bf16[2,64,256]{2,1,0:T(8,128)(2,1)S(1)} %fusion.4.own_ref), channel_id=1, source_target_pairs={{0,192},{64,128},{128,64},{192,0},{1,193},{65,129},{129,65},{193,1... | collective-permute-start | bytes 196616 | tf_op jit(solution)/shard_map/ppermute | solution.py:258
  85.4 12.4 %collective-permute-start.13 = (bf16[2,64,256]{2,1,0:T(8,128)(2,1)S(1)}, bf16[2,64,256]{2,1,0:T(8,128)(2,1)S(1)}, u32[]{:S(2)}, u32[]{:S(2)}) collective-permute-start(bf16[2,64,256]{2,1,0:T(8,128)(2,1)S(1)} %fusion.4.own_ref), channel_id=1, source_target_pairs={{0,128},{64,192},{128,0},{192,64},{1,129},{65,193},{129,1},{193,65... | collective-permute-start | bytes 196616 | tf_op jit(solution)/shard_map/ppermute | solution.py:258
  86.6 11.3 %collective-permute-start.12 = (bf16[2,64,256]{2,1,0:T(8,128)(2,1)S(1)}, bf16[2,64,256]{2,1,0:T(8,128)(2,1)S(1)}, u32[]{:S(2)}, u32[]{:S(2)}) collective-permute-start(bf16[2,64,256]{2,1,0:T(8,128)(2,1)S(1)} %fusion.4.own_ref), channel_id=1, source_target_pairs={{0,64},{64,0},{128,192},{192,128},{1,65},{65,1},{129,193},{193,129... | collective-permute-start | bytes 196616 | tf_op jit(solution)/shard_map/ppermute | solution.py:258
where the time goes:
time: 99.1 us; the launch traced here: 98.7 us
  waiting for transfers between devices  46.8 us (47%)
  starting transfers between devices  37.4 us (38%)
  Pallas kernels  10.5 us (11%)
  other arithmetic  1.85 us (2%)
  local copies, waits for them, and re-layouts  1.18 us (1%)
    ppermute x11, waiting for transfers between devices, swap(): lax.ppermute(value, axis, [(i, i ^ mask) for i in range(lax.axis_size(axi...  25.8 us
    ppermute x11, starting transfers between devices, swap(): lax.ppermute(value, axis, [(i, i ^ mask) for i in range(lax.axis_size(axi...  16.3 us
    all_to_all x2, starting transfers between devices, exchange(): lax.all_to_all(value, 'lon', 0, 0, axis_index_groups=expert_groups(), til...  14.4 us
    ppermute x4, waiting for transfers between devices, shift(): return lax.ppermute(value, axis, pairs)  11.2 us
    pallas_call x5, Pallas kernels, call(): pl.pallas_call(kernel, out_shape=[jax.ShapeDtypeStruct(shape, dtype) for...  10.5 us
    all_to_all x2, waiting for transfers between devices, exchange(): lax.all_to_all(value, 'lon', 0, 0, axis_index_groups=expert_groups(), til...  9.73 us
    ppermute x4, starting transfers between devices, shift(): return lax.ppermute(value, axis, pairs)  6.69 us
  transfers between devices with their start and end apart: 17, of which 8 were waited for; matrix products, arithmetic and copies ran while one was open for 0% of the time, Pallas kernels for 1%

commit v1 on v0

--- a/solution.py
+++ b/solution.py
@@ -63,6 +63,16 @@
     return table.reshape(WINDOW * WINDOW, 2048), outside.reshape(1, 2048).astype(np.float32)
 
 
+def mark_kernel(state_ref, land_ref, marked_ref, even_ref, odd_ref):
+    land = jnp.broadcast_to(land_ref[...][:, :, None], (ROWS, COLS, D))
+    marked = jnp.where(land > 0, state_ref[...].astype(F32), LAND).astype(BF)
+    marked_ref[...] = marked
+    even = lax.axis_index("lat") & 1 == 0
+    top, bottom = marked[:REACH], marked[ROWS - REACH :]
+    even_ref[...] = jnp.where(even, bottom, top)
+    odd_ref[...] = jnp.where(even, top, bottom)
+
+
 def prepare_kernel(pos_ref, taps_ref, outside_ref, labels_ref, cot_ref, land_ref, bias_ref, place_ref, sendc_ref):
     pos = pos_ref[...]
     high = pos.astype(BF)
@@ -89,12 +99,18 @@
     sendc_ref[...] = dot(place, tangent.astype(BF)).astype(BF)
 
 
+def in_order(axis, even_ref, odd_ref):
+    even, odd = even_ref[...].astype(F32), odd_ref[...].astype(F32)
+    at_even = lax.axis_index(axis) & 1 == 0
+    return jnp.where(at_even, odd, even), jnp.where(at_even, even, odd)
+
+
 def attention_kernel(
     own_ref,
-    up_ref,
-    down_ref,
-    left_ref,
-    right_ref,
+    lat_even_ref,
+    lat_odd_ref,
+    lon_even_ref,
+    lon_odd_ref,
     land_ref,
     gain1_ref,
     gain2_ref,
@@ -103,19 +119,24 @@
     bias_ref,
     place_ref,
     sendc_ref,
+    near_ref,
+    middle_ref,
+    far_ref,
     residual_ref,
     send_ref,
+    fetched_ref,
     ext_ref,
     pen_ref,
 ):
+    fetched_ref[0] = near_ref[...]
+    fetched_ref[1] = middle_ref[...]
+    fetched_ref[2] = far_ref[...]
     lat = lax.axis_index("lat")
     top = jnp.where(lat == 0, FAR, 0.0).astype(F32)
     bottom = jnp.where(lat == lax.axis_size("lat") - 1, FAR, 0.0).astype(F32)
     own3 = own_ref[...].astype(F32)
-    up = up_ref[...].astype(F32)
-    down = down_ref[...].astype(F32)
-    left = left_ref[...].astype(F32)
-    right = right_ref[...].astype(F32)
+    up, down = in_order("lat", lat_even_ref, lat_odd_ref)
+    left, right = in_order("lon", lon_even_ref, lon_odd_ref)
 
     def marked(piece):
         return jnp.where(piece[:, :, 0:128] > 0.5 * LAND, FAR, 0.0)
@@ -189,15 +210,23 @@
     return hidden * half, slope
 
 
-def expert_kernel(got_ref, own_ref, *refs):
-    weight_refs = (own_ref,) + refs[0:3]
-    outputs_ref, keep_ref, give_ref, grad_ref = refs[3:]
+def expert_kernel(
+    got_ref, up_ref, down_ref, mine_ref, other_ref, outputs_ref, keep_ref, give_ref, grad_ref
+):
+    lat = lax.axis_index("lat")
+    first_core = lat & 1 == 0
     inputs = got_ref[:, 0:D]
     tangents = got_ref[:, D : 2 * D]
     outputs = jnp.zeros((SLOTS, D), F32)
     for member in range(4):
-        up = weight_refs[member][0]
-        down = weight_refs[member][1]
+        if member:
+            mine = mine_ref[member - 1]
+            other = other_ref[member - 1]
+            up = jnp.where(first_core, mine, other)
+            down = jnp.where(first_core, other, mine)
+        else:
+            up = up_ref[...]
+            down = down_ref[...]
         active, slope = gelu_parts(dot(inputs, up))
         active = active.astype(BF)
         outputs = outputs + dot(active, down)
@@ -205,7 +234,6 @@
         grad_ref[member, 0] = t_dot(inputs, pre_act)
         grad_ref[member, 1] = t_dot(active, tangents)
     outputs_ref[...] = outputs.astype(BF)
-    lat = lax.axis_index("lat")
     for far in range(2):
         for other in range(2):
             start = pl.multiple_of(jnp.bitwise_xor(lat, 2 * far + other) * 64, 64)
@@ -216,17 +244,16 @@
                 keep_ref[far] = chunk
 
 
-def combine_kernel(returned_ref, place_ref, residual_ref, land_ref, block_ref):
-    rows = lax.dot_general(
-        place_ref[...],
-        returned_ref[...],
-        (((0,), (0,)), ((), ())),
-        preferred_element_type=F32,
-    )
+def combine_kernel(
+    returned_ref, place_ref, residual_ref, land_ref, part_ref, a_ref, b_ref, c_ref, block_ref, total_ref
+):
+    rows = t_dot(place_ref[...], returned_ref[...])
     land = land_ref[...].astype(F32)
     block_ref[...] = (
         (land * (residual_ref[...].astype(F32) + rows)).astype(BF).reshape(ROWS, COLS, D)
     )
+    total = part_ref[...] + a_ref[...].astype(F32)
+    total_ref[...] = (total + b_ref[...].astype(F32) + c_ref[...].astype(F32)).astype(BF)
 
 
 def gather_kernel(own_ref, a_ref, b_ref, c_ref, up_ref, down_ref):
@@ -248,9 +275,11 @@
     )(*args)
 
 
-def shift(value, axis, step, closed):
+def pair_up(value, axis, first, closed):
     count = lax.axis_size(axis)
-    pairs = [(i, (i + step) % count) for i in range(count) if closed or 0 <= i + step < count]
+    pairs = []
+    for i in range(first, count if closed else count - 1, 2):
+        pairs += [(i, (i + 1) % count), ((i + 1) % count, i)]
     return lax.ppermute(value, axis, pairs)
 
 
@@ -259,12 +288,20 @@
 
 
 def expert_groups():
-    return [[8 * (e // 2) + (k if e % 2 == 0 else 7 - k) for e in range(EXPERTS)] for k in range(4)]
+    groups = []
+    for lat in range(4):
+        for k in range(4):
+            group = []
+            for e in range(EXPERTS):
+                place = lat ^ 2 if (e // 2) % 2 else lat
+                group.append(place * 64 + 8 * (e // 2) + (7 - k if e % 2 else k))
+            groups.append(group)
+    return groups
 
 
 def exchange(value):
     return lax.all_to_all(
-        value, "lon", 0, 0, axis_index_groups=expert_groups(), tiled=True
+        value, ("lat", "lon"), 0, 0, axis_index_groups=expert_groups(), tiled=True
     )
 
 
@@ -281,12 +318,20 @@
     up_weight,
     down_weight,
 ):
-    marked = jnp.where(land_sea[:, :, None] > 0, state, jnp.asarray(LAND, BF))
-    up = shift(marked[ROWS - REACH :], "lat", 1, False)
-    down = shift(marked[:REACH], "lat", -1, False)
+    marked, even, odd = call(
+        mark_kernel,
+        [((ROWS, COLS, D), BF), ((REACH, COLS, D), BF), ((REACH, COLS, D), BF)],
+        (state, land_sea),
+    )
+    lat_even = pair_up(even, "lat", 0, False)
+    lat_odd = pair_up(odd, "lat", 1, False)
+    at_even = lax.axis_index("lat") & 1 == 0
+    up = jnp.where(at_even, lat_odd, lat_even)
+    down = jnp.where(at_even, lat_even, lat_odd)
     tall = jnp.concatenate([up, marked, down], axis=0)
-    left = shift(tall[:, COLS - 4 :], "lon", 1, True)
-    right = shift(tall[:, :4], "lon", -1, True)
+    at_even = lax.axis_index("lon") & 1 == 0
+    lon_odd = pair_up(jnp.where(at_even, tall[:, :4], tall[:, 4:]), "lon", 1, True)
+    lon_even = pair_up(jnp.where(at_even, tall[:, 4:], tall[:, :4]), "lon", 0, True)
 
     land_column = land_sea.reshape(CELLS, 1)
     taps, outside = tap_tables()
@@ -302,19 +347,18 @@
             land_column,
         ),
     )
-    weights = [jnp.stack([up_weight, down_weight])]
-    for mask in (1, 2, 3):
-        weights.append(swap(weights[0], "lon", mask))
-
-    residual, send = call(
+    half = jnp.where(lax.axis_index("lat") & 1 == 0, up_weight, down_weight)
+    fetched = [swap(half, "lon", mask) for mask in (1, 2, 3)]
+
+    residual, send, fetched = call(
         attention_kernel,
-        [((CELLS, D), BF), ((SLOTS, 2 * D), BF)],
+        [((CELLS, D), BF), ((SLOTS, 2 * D), BF), ((3, D, UNITS), BF)],
         (
             state,
-            up,
-            down,
-            left,
-            right,
+            lat_even,
+            lat_odd,
+            lon_even,
+            lon_odd,
             land_column,
             first_gain.reshape(1, D),
             second_gain.reshape(1, D),
@@ -323,6 +367,7 @@
             bias,
             place,
             sendc,
+            *fetched,
         ),
         (pltpu.VMEM((EXT, 16, D), F32), pltpu.VMEM((EXT, 16, 128), F32)),
     )
@@ -330,27 +375,25 @@
     outputs, keep, give = call(
         expert_kernel,
         [((SLOTS, D), BF), ((2, 4, 2, 64, D), F32), ((2, 4, 2, 64, D), BF)],
-        (got, *weights),
+        (got, up_weight, down_weight, fetched, swap(fetched, "lat", 1)),
         (pltpu.VMEM((4, 2, 256, D), F32),),
     )
+    near = swap(give, "lat", 1)
+    sent = (keep[1] + near[1].astype(F32)).astype(BF)
+    outputs, sent = lax.optimization_barrier((outputs, sent))
     returned = exchange(outputs.reshape(EXPERTS, CAP, D)).reshape(SLOTS, D)
-
-    near = swap(give, "lat", 1)
-    far = swap((keep[1] + near[1].astype(F32)).astype(BF), "lat", 2)
+    far = swap(sent, "lat", 2)
     part = keep[0] + near[0].astype(F32) + far.astype(F32)
-    total = part[0]
-    for mask in (1, 2, 3):
-        total = total + swap(part[mask].astype(BF), "lon", mask).astype(F32)
-    total = total.astype(BF)
+    others = [swap(part[mask].astype(BF), "lon", mask) for mask in (1, 2, 3)]
+    block, total = call(
+        combine_kernel,
+        [((ROWS, COLS, D), BF), ((2, 64, D), BF)],
+        (returned, place, residual, land_column, part[0], *others),
+    )
     grad_up, grad_down = call(
         gather_kernel,
         [((D, UNITS), F32), ((UNITS, D), F32)],
         (total, *[swap(total, "lat", mask) for mask in (1, 2, 3)]),
-    )
-    (block,) = call(
-        combine_kernel,
-        [((ROWS, COLS, D), BF)],
-        (returned, place, residual, land_column),
     )
     return block, grad_up, grad_down
 

time: 99.1 us -> 79.5 us (0.80)
  the two profiles are of different devices: /device:TPU:32 before, /device:TPU:1 now
where the time goes in v1:
time: 79.5 us; the launch traced here: 79.1 us
  starting transfers between devices  44.2 us (56%)
  waiting for transfers between devices  20.4 us (26%)
  Pallas kernels  10.6 us (13%)
  local copies, waits for them, and re-layouts  1.93 us (2%)
  other arithmetic  1.17 us (1%)
  between operations  0.92 us (1%)
    ppermute x12, starting transfers between devices, swap(): lax.ppermute(value, axis, [(i, i ^ mask) for i in range(lax.axis_size(axi...  19.7 us
    ppermute x4, starting transfers between devices, pair_up(): return lax.ppermute(value, axis, pairs)  14.3 us
    ppermute x12, waiting for transfers between devices, swap(): lax.ppermute(value, axis, [(i, i ^ mask) for i in range(lax.axis_size(axi...  12.9 us
    pallas_call x6, Pallas kernels, call(): pl.pallas_call(kernel, out_shape=[jax.ShapeDtypeStruct(shape, dtype) for...  10.6 us
    all_to_all x2, starting transfers between devices, exchange(): lax.all_to_all(value, ('lat', 'lon'), 0, 0, axis_index_groups=expert_grou...  10.1 us
    all_to_all x2, waiting for transfers between devices, exchange(): lax.all_to_all(value, ('lat', 'lon'), 0, 0, axis_index_groups=expert_grou...  5.3 us
    ppermute x4, waiting for transfers between devices, pair_up(): return lax.ppermute(value, axis, pairs)  2.16 us
    unnamed x28, local copies, waits for them, and re-layouts  1.74 us
  transfers between devices with their start and end apart: 18, of which 11 were waited for; matrix products, arithmetic and copies ran while one was open for 2% of the time, Pallas kernels for 1%

profile of v1, /device:TPU:1, one launch (start us, length us, event | category | flops | bytes accessed | tf_op | source)
XLA Modules:
  0.0 79.1 jit_solution(1263135727501961767)
XLA Ops:
  0.6 0.8 copy.22.land_ref
  1.4 0.8 %copy-done.3 = bf16[16,8,256]{2,1,0:T(8,128)(2,1)S(1)} copy-done((bf16[16,8,256]{2,1,0:T(8,128)(2,1)S(1)}, bf16[16,8,256]{2,1,0:T(8,128)(2,1)}, u32[]{:S(2)}) %copy-start.3) | copy-done | bytes 65560
  2.2 0.1 shard_map.148
  2.3 3.3 %collective-permute-start = (bf16[3,8,256]{2,1,0:T(8,128)(2,1)S(1)}, bf16[3,8,256]{2,1,0:T(8,128)(2,1)S(1)}, u32[]{:S(2)}, u32[]{:S(2)}) collective-permute-start(bf16[3,8,256]{2,1,0:T(8,128)(2,1)S(1)} %get-tuple-element.21), channel_id=1, source_target_pairs={{0,64},{64,0},{128,192},{192,128},{1,65},{65,1},{129,193},{193,129... | collective-permute-start | bytes 36872 | tf_op jit(solution)/shard_map/ppermute | solution.py:283
  5.6 1.9 %collective-permute-start.1 = (bf16[3,8,256]{2,1,0:T(8,128)(2,1)S(1)}, bf16[3,8,256]{2,1,0:T(8,128)(2,1)S(1)}, u32[]{:S(2)}, u32[]{:S(2)}) collective-permute-start(bf16[3,8,256]{2,1,0:T(8,128)(2,1)S(1)} %get-tuple-element.22), channel_id=1, source_target_pairs={{64,128},{128,64},{65,129},{129,65},{66,130},{130,66},{67,131},{13... | collective-permute-start | bytes 36872 | tf_op jit(solution)/shard_map/ppermute | solution.py:283
  7.6 0.0 copy-start.12
  7.6 0.0 copy-start.10
  7.6 0.0 copy-start.11
  7.6 0.9 %broadcast_select_fusion = bf16[256,256]{1,0:T(8,128)(2,1)S(1)} fusion(bf16[256,256]{1,0:T(8,128)(2,1)} %up_ref.1, bf16[256,256]{1,0:T(8,128)(2,1)} %down_ref.1, pred[]{:T(512)S(6)} %eq.8), kind=kLoop, calls=%fused_computation.4 | loop fusion | flops 65536 | bytes 393217 | tf_op jit(solution)/shard_map/jit(_where)/select_n | solution.py:350
  8.5 3.8 %collective-permute-start.6 = (bf16[256,256]{1,0:T(8,128)(2,1)S(1)}, bf16[256,256]{1,0:T(8,128)(2,1)S(1)}, u32[]{:S(2)}, u32[]{:S(2)}) collective-permute-start(bf16[256,256]{1,0:T(8,128)(2,1)S(1)} %broadcast_select_fusion), channel_id=1, source_target_pairs={{0,3},{1,2},{2,1},{3,0},{4,7},{5,6},{6,5},{7,4},{8,11},{9,10},{10,... | collective-permute-start | bytes 393224 | tf_op jit(solution)/shard_map/ppermute | solution.py:287
  12.3 0.0 collective-permute-start.5
  12.4 0.4 collective-permute-start.4
  12.7 0.0 collective-permute-done.lat_even_ref
  12.7 0.0 collective-permute-done.1.lat_odd_ref
  12.7 0.0 copy-start.8
  12.8 0.0 copy-start.9
  12.8 0.0 copy-start.5
  12.8 0.0 copy-start.2
  12.8 0.1 broadcast_select_fusion.1
  12.9 9.1 %collective-permute-start.3 = (bf16[22,4,256]{2,1,0:T(4,128)(2,1)S(1)}, bf16[22,4,256]{2,1,0:T(4,128)(2,1)S(1)}, u32[]{:S(2)}, u32[]{:S(2)}) collective-permute-start(bf16[22,4,256]{2,1,0:T(4,128)(2,1)S(1)} %get-tuple-element.44), channel_id=1, source_target_pairs={{1,2},{2,1},{3,4},{4,3},{5,6},{6,5},{7,8},{8,7},{9,10},{10,9},{11,... | collective-permute-start | bytes 135176 | tf_op jit(solution)/shard_map/ppermute | solution.py:283
  22.0 0.0 collective-permute-start.2
  22.0 0.1 reshape.46.land_ref
  22.1 0.0 copy-done.12
  22.1 0.1 copy.24
  22.2 0.1 reshape.41.labels_ref
  22.3 0.0 copy-done.7
  22.3 0.0 copy-done.8
  22.3 0.0 copy-start.4
  22.3 0.0 copy-start.6
  22.3 0.4 shard_map.149
  22.7 0.7 collective-permute-done.3.lon_odd_ref
  23.4 1.5 %collective-permute-done.2.lon_even_ref = bf16[22,4,256]{2,1,0:T(4,128)(2,1)S(1)} collective-permute-done((bf16[22,4,256]{2,1,0:T(4,128)(2,1)S(1)}, bf16[22,4,256]{2,1,0:T(4,128)(2,1)S(1)}, u32[]{:S(2)}, u32[]{:S(2)}) %collective-permute-start.2) | collective-permute-done | bytes 45088 | tf_op jit(solution)/shard_map/ppermute | solution.py:283
  24.9 0.0 collective-permute-done.6.far_ref
  24.9 0.0 collective-permute-done.5.middle_ref
  24.9 0.0 collective-permute-done.4.near_ref
  25.0 6.3 %shard_map.150 = (bf16[128,256]{1,0:T(8,128)(2,1)S(1)}, bf16[256,512]{1,0:T(8,128)(2,1)}, bf16[3,256,256]{2,1,0:T(8,128)(2,1)S(1)}) custom-call(bf16[16,8,256]{2,1,0:T(8,128)(2,1)S(1)} %copy-done.4, bf16[3,8,256]{2,1,0:T(8,128)(2,1)S(1)} %collective-permute-done.lat_even_ref, bf16[3,8,256]{2,1,0:T(8,128)(2,1)S(1)} %collective-permute-done.1.lat_odd_ref, ...), custom_call_target="tpu_custom_call" | custom-call | tf_op jit(solution)/shard_map/pallas_call | solution.py:268
  31.2 5.6 %all-to-all-start = ((bf16[16,16,512]{2,1,0:T(8,128)(2,1)}), bf16[16,16,512]{2,1,0:T(8,128)(2,1)S(1)}, u32[]{:S(2)}, u32[]{:S(2)}) async-start(bf16[16,16,512]{2,1,0:T(8,128)(2,1)} %bitcast.2), calls=%async_computation | async-start | bytes 524288 | tf_op jit(solution)/shard_map/all_to_all | solution.py:303
  36.8 3.9 %collective-permute-start.7 = (bf16[3,256,256]{2,1,0:T(8,128)(2,1)S(1)}, bf16[3,256,256]{2,1,0:T(8,128)(2,1)S(1)}, u32[]{:S(2)}, u32[]{:S(2)}) collective-permute-start(bf16[3,256,256]{2,1,0:T(8,128)(2,1)S(1)} %get-tuple-element.28.mine_ref), channel_id=1, source_target_pairs={{0,64},{64,0},{128,192},{192,128},{1,65},{65,1},{129,193},{193,129... | collective-permute-start | bytes 1179656 | tf_op jit(solution)/shard_map/ppermute | solution.py:287
  40.7 1.3 %collective-permute-done.7.other_ref = bf16[3,256,256]{2,1,0:T(8,128)(2,1)S(1)} collective-permute-done((bf16[3,256,256]{2,1,0:T(8,128)(2,1)S(1)}, bf16[3,256,256]{2,1,0:T(8,128)(2,1)S(1)}, u32[]{:S(2)}, u32[]{:S(2)}) %collective-permute-start.7) | collective-permute-done | bytes 393248 | tf_op jit(solution)/shard_map/ppermute | solution.py:287
  42.0 3.5 %all-to-all-done = bf16[16,16,512]{2,1,0:T(8,128)(2,1)S(1)} async-done(((bf16[16,16,512]{2,1,0:T(8,128)(2,1)}), bf16[16,16,512]{2,1,0:T(8,128)(2,1)S(1)}, u32[]{:S(2)}, u32[]{:S(2)}) %all-to-all-start) | async-done | bytes 262176 | tf_op jit(solution)/shard_map/all_to_all | solution.py:303
  45.6 0.0 copy-done.1
  45.6 2.1 %shard_map.151 = (bf16[256,256]{1,0:T(8,128)(2,1)}, f32[2,4,2,64,256]{4,3,2,1,0:T(8,128)S(1)}, bf16[2,4,2,64,256]{4,3,2,1,0:T(8,128)(2,1)S(1)}) custom-call(bf16[256,512]{1,0:T(8,128)(2,1)S(1)} %bitcast.23, bf16[256,256]{1,0:T(8,128)(2,1)S(1)} %copy-done, bf16[256,256]{1,0:T(8,128)(2,1)S(1)} %copy-done.1, ...), custom_call_target="tpu_custom_call" | custom-call | tf_op jit(solution)/shard_map/pallas_call | solution.py:268
  47.7 4.9 %collective-permute-start.8 = (bf16[2,4,2,64,256]{4,3,2,1,0:T(8,128)(2,1)S(1)}, bf16[2,4,2,64,256]{4,3,2,1,0:T(8,128)(2,1)S(1)}, u32[]{:S(2)}, u32[]{:S(2)}) collective-permute-start(bf16[2,4,2,64,256]{4,3,2,1,0:T(8,128)(2,1)S(1)} %get-tuple-element.31), channel_id=1, source_target_pairs={{0,64},{64,0},{128,192},{192,128},{1,65},{65,1},{129,193},{193,129... | collective-permute-start | bytes 1572872 | tf_op jit(solution)/shard_map/ppermute | solution.py:287
  52.7 1.5 %collective-permute-done.8 = bf16[2,4,2,64,256]{4,3,2,1,0:T(8,128)(2,1)S(1)} collective-permute-done((bf16[2,4,2,64,256]{4,3,2,1,0:T(8,128)(2,1)S(1)}, bf16[2,4,2,64,256]{4,3,2,1,0:T(8,128)(2,1)S(1)}, u32[]{:S(2)}, u32[]{:S(2)}) %collective-permute-start.8) | collective-permute-done | bytes 524320 | tf_op jit(solution)/shard_map/ppermute | solution.py:287
  54.2 0.1 fusion
  54.3 0.1 collective-permute-start.9
  54.4 4.6 %all-to-all-start.1 = ((bf16[16,16,256]{2,1,0:T(8,128)(2,1)}), bf16[16,16,256]{2,1,0:T(8,128)(2,1)S(1)}, u32[]{:S(2)}, u32[]{:S(2)}) async-start(bf16[16,16,256]{2,1,0:T(8,128)(2,1)} %bitcast.5), calls=%async_computation.1 | async-start | bytes 262144 | tf_op jit(solution)/shard_map/all_to_all | solution.py:303
  59.0 2.9 %collective-permute-done.9 = bf16[4,2,64,256]{3,2,1,0:T(8,128)(2,1)S(1)} collective-permute-done((bf16[4,2,64,256]{3,2,1,0:T(8,128)(2,1)S(1)}, bf16[4,2,64,256]{3,2,1,0:T(8,128)(2,1)S(1)}, u32[]{:S(2)}, u32[]{:S(2)}) %collective-permute-start.9) | collective-permute-done | bytes 262176 | tf_op jit(solution)/shard_map/ppermute | solution.py:287
  61.9 0.1 fusion.1
  62.0 1.4 %collective-permute-start.12 = (bf16[2,64,256]{2,1,0:T(8,128)(2,1)S(1)}, bf16[2,64,256]{2,1,0:T(8,128)(2,1)S(1)}, u32[]{:S(2)}, u32[]{:S(2)}) collective-permute-start(bf16[2,64,256]{2,1,0:T(8,128)(2,1)S(1)} %get-tuple-element.41), channel_id=1, source_target_pairs={{0,3},{1,2},{2,1},{3,0},{4,7},{5,6},{6,5},{7,4},{8,11},{9,10},{10,... | collective-permute-start | bytes 196616 | tf_op jit(solution)/shard_map/ppermute | solution.py:287
  63.4 2.3 %collective-permute-start.11 = (bf16[2,64,256]{2,1,0:T(8,128)(2,1)S(1)}, bf16[2,64,256]{2,1,0:T(8,128)(2,1)S(1)}, u32[]{:S(2)}, u32[]{:S(2)}) collective-permute-start(bf16[2,64,256]{2,1,0:T(8,128)(2,1)S(1)} %get-tuple-element.42), channel_id=1, source_target_pairs={{0,2},{1,3},{2,0},{3,1},{4,6},{5,7},{6,4},{7,5},{8,10},{9,11},{10,... | collective-permute-start | bytes 196616 | tf_op jit(solution)/shard_map/ppermute | solution.py:287
  65.7 0.0 collective-permute-start.10
  65.7 1.8 %all-to-all-done.1 = bf16[16,16,256]{2,1,0:T(8,128)(2,1)S(1)} async-done(((bf16[16,16,256]{2,1,0:T(8,128)(2,1)}), bf16[16,16,256]{2,1,0:T(8,128)(2,1)S(1)}, u32[]{:S(2)}, u32[]{:S(2)}) %all-to-all-start.1) | async-done | bytes 131104 | tf_op jit(solution)/shard_map/all_to_all | solution.py:303
  67.5 0.8 %collective-permute-done.12.c_ref = bf16[2,64,256]{2,1,0:T(8,128)(2,1)S(1)} collective-permute-done((bf16[2,64,256]{2,1,0:T(8,128)(2,1)S(1)}, bf16[2,64,256]{2,1,0:T(8,128)(2,1)S(1)}, u32[]{:S(2)}, u32[]{:S(2)}) %collective-permute-start.12) | collective-permute-done | bytes 65568 | tf_op jit(solution)/shard_map/ppermute | solution.py:287
  68.3 3.1 %collective-permute-done.11.b_ref = bf16[2,64,256]{2,1,0:T(8,128)(2,1)S(1)} collective-permute-done((bf16[2,64,256]{2,1,0:T(8,128)(2,1)S(1)}, bf16[2,64,256]{2,1,0:T(8,128)(2,1)S(1)}, u32[]{:S(2)}, u32[]{:S(2)}) %collective-permute-start.11) | collective-permute-done | bytes 65568 | tf_op jit(solution)/shard_map/ppermute | solution.py:287
  71.3 0.0 collective-permute-done.10.a_ref
  71.3 0.8 %shard_map.152 = (bf16[16,8,256]{2,1,0:T(8,128)(2,1)}, bf16[2,64,256]{2,1,0:T(8,128)(2,1)S(1)}) custom-call(bf16[256,256]{1,0:T(8,128)(2,1)S(1)} %bitcast.24, bf16[256,128]{1,0:T(8,128)(2,1)S(1)} %get-tuple-element.25.place_ref, bf16[128,256]{1,0:T(8,128)(2,1)S(1)} %get-tuple-element.33.residual_ref, s32[128,1]{1,0:T(8,128)S(1)} %reshape.46.land_ref, ...), custom_call_target="tpu_custom_call" | custom-call | tf_op jit(solution)/shard_map/pallas_call | solution.py:268
  72.2 1.5 %collective-permute-start.15 = (bf16[2,64,256]{2,1,0:T(8,128)(2,1)S(1)}, bf16[2,64,256]{2,1,0:T(8,128)(2,1)S(1)}, u32[]{:S(2)}, u32[]{:S(2)}) collective-permute-start(bf16[2,64,256]{2,1,0:T(8,128)(2,1)S(1)} %get-tuple-element.36.own_ref), channel_id=1, source_target_pairs={{0,192},{64,128},{128,64},{192,0},{1,193},{65,129},{129,65},{193,1... | collective-permute-start | bytes 196616 | tf_op jit(solution)/shard_map/ppermute | solution.py:287
  73.7 1.4 %collective-permute-start.14 = (bf16[2,64,256]{2,1,0:T(8,128)(2,1)S(1)}, bf16[2,64,256]{2,1,0:T(8,128)(2,1)S(1)}, u32[]{:S(2)}, u32[]{:S(2)}) collective-permute-start(bf16[2,64,256]{2,1,0:T(8,128)(2,1)S(1)} %get-tuple-element.36.own_ref), channel_id=1, source_target_pairs={{0,128},{64,192},{128,0},{192,64},{1,129},{65,193},{129,1},{193,65... | collective-permute-start | bytes 196616 | tf_op jit(solution)/shard_map/ppermute | solution.py:287
  75.1 0.0 collective-permute-start.13
  75.1 0.8 collective-permute-done.15.c_ref
  75.9 2.4 %collective-permute-done.14.b_ref = bf16[2,64,256]{2,1,0:T(8,128)(2,1)S(1)} collective-permute-done((bf16[2,64,256]{2,1,0:T(8,128)(2,1)S(1)}, bf16[2,64,256]{2,1,0:T(8,128)(2,1)S(1)}, u32[]{:S(2)}, u32[]{:S(2)}) %collective-permute-start.14) | collective-permute-done | bytes 65568 | tf_op jit(solution)/shard_map/ppermute | solution.py:287
  78.3 0.0 collective-permute-done.13.a_ref
  78.3 0.8 %shard_map.153 = (f32[256,256]{1,0:T(8,128)}, f32[256,256]{1,0:T(8,128)}) custom-call(bf16[2,64,256]{2,1,0:T(8,128)(2,1)S(1)} %get-tuple-element.36.own_ref, bf16[2,64,256]{2,1,0:T(8,128)(2,1)S(1)} %collective-permute-done.13.a_ref, bf16[2,64,256]{2,1,0:T(8,128)(2,1)S(1)} %collective-permute-done.14.b_ref, bf16[2,64,256]{2,1,0:T(8,128)(2,1)S(1)} %collective-permute-done.15.c_ref), custom_call_target="tpu_custom_call" | custom-call | tf_op jit(solution)/shard_map/pallas_call | solution.py:268
  (16 shorter events, 0.1 us)
Async XLA Ops:
  1.4 0.8 %copy-start.3 = (bf16[16,8,256]{2,1,0:T(8,128)(2,1)S(1)}, bf16[16,8,256]{2,1,0:T(8,128)(2,1)}, u32[]{:S(2)}) copy-start(bf16[16,8,256]{2,1,0:T(8,128)(2,1)} %own_ref.1) | copy-start | bytes 196612
  2.3 10.4 %collective-permute-start = (bf16[3,8,256]{2,1,0:T(8,128)(2,1)S(1)}, bf16[3,8,256]{2,1,0:T(8,128)(2,1)S(1)}, u32[]{:S(2)}, u32[]{:S(2)}) collective-permute-start(bf16[3,8,256]{2,1,0:T(8,128)(2,1)S(1)} %get-tuple-element.21), channel_id=1, source_target_pairs={{0,64},{64,0},{128,192},{192,128},{1,65},{65,1},{129,193},{193,129... | collective-permute-start | bytes 36872 | tf_op jit(solution)/shard_map/ppermute | solution.py:283
  5.6 7.1 %collective-permute-start.1 = (bf16[3,8,256]{2,1,0:T(8,128)(2,1)S(1)}, bf16[3,8,256]{2,1,0:T(8,128)(2,1)S(1)}, u32[]{:S(2)}, u32[]{:S(2)}) collective-permute-start(bf16[3,8,256]{2,1,0:T(8,128)(2,1)S(1)} %get-tuple-element.22), channel_id=1, source_target_pairs={{64,128},{128,64},{65,129},{129,65},{66,130},{130,66},{67,131},{13... | collective-permute-start | bytes 36872 | tf_op jit(solution)/shard_map/ppermute | solution.py:283
  7.6 14.5 %copy-start.12 = (s32[1,1,16,8,1]{2,4,3,1,0:T(1,128)S(1)}, s32[1,1,16,8,1]{2,4,3,1,0:T(1,128)}, u32[]{:S(2)}) copy-start(s32[1,1,16,8,1]{2,4,3,1,0:T(1,128)} %param.16) | copy-start | bytes 1540
  7.6 17.3 %copy-start.10 = (f32[256]{0:T(256)S(1)}, f32[256]{0:T(256)}, u32[]{:S(2)}) copy-start(f32[256]{0:T(256)} %param.17) | copy-start | bytes 3076
  7.6 17.3 %copy-start.11 = (f32[256]{0:T(256)S(1)}, f32[256]{0:T(256)}, u32[]{:S(2)}) copy-start(f32[256]{0:T(256)} %param.18) | copy-start | bytes 3076
  8.5 16.4 %collective-permute-start.6 = (bf16[256,256]{1,0:T(8,128)(2,1)S(1)}, bf16[256,256]{1,0:T(8,128)(2,1)S(1)}, u32[]{:S(2)}, u32[]{:S(2)}) collective-permute-start(bf16[256,256]{1,0:T(8,128)(2,1)S(1)} %broadcast_select_fusion), channel_id=1, source_target_pairs={{0,3},{1,2},{2,1},{3,0},{4,7},{5,6},{6,5},{7,4},{8,11},{9,10},{10,... | collective-permute-start | bytes 393224 | tf_op jit(solution)/shard_map/ppermute | solution.py:287
  12.3 12.6 %collective-permute-start.5 = (bf16[256,256]{1,0:T(8,128)(2,1)S(1)}, bf16[256,256]{1,0:T(8,128)(2,1)S(1)}, u32[]{:S(2)}, u32[]{:S(2)}) collective-permute-start(bf16[256,256]{1,0:T(8,128)(2,1)S(1)} %broadcast_select_fusion), channel_id=1, source_target_pairs={{0,2},{1,3},{2,0},{3,1},{4,6},{5,7},{6,4},{7,5},{8,10},{9,11},{10,... | collective-permute-start | bytes 393224 | tf_op jit(solution)/shard_map/ppermute | solution.py:287
  12.4 12.6 %collective-permute-start.4 = (bf16[256,256]{1,0:T(8,128)(2,1)S(1)}, bf16[256,256]{1,0:T(8,128)(2,1)S(1)}, u32[]{:S(2)}, u32[]{:S(2)}) collective-permute-start(bf16[256,256]{1,0:T(8,128)(2,1)S(1)} %broadcast_select_fusion), channel_id=1, source_target_pairs={{0,1},{1,0},{2,3},{3,2},{4,5},{5,4},{6,7},{7,6},{8,9},{9,8},{10,11... | collective-permute-start | bytes 393224 | tf_op jit(solution)/shard_map/ppermute | solution.py:287
  12.7 9.5 %copy-start.7 = (bf16[16,8,256]{2,1,0:T(8,128)(2,1)S(1)}, bf16[16,8,256]{2,1,0:T(8,128)(2,1)}, u32[]{:S(2)}) copy-start(bf16[16,8,256]{2,1,0:T(8,128)(2,1)} %cot_ref.1) | copy-start | bytes 196612
  12.7 9.5 %copy-start.8 = (f32[1,2048]{1,0:T(1,128)S(1)}, f32[1,2048]{1,0:T(1,128)}, u32[]{:S(2)}) copy-start(f32[1,2048]{1,0:T(1,128)} %constant.18.clone.outside_ref) | copy-start | bytes 24580
  12.8 9.5 %copy-start.9 = (f32[8,49]{1,0:T(8,128)S(1)}, f32[8,49]{1,0:T(8,128)}, u32[]{:S(2)}) copy-start(f32[8,49]{1,0:T(8,128)} %pos_ref.1) | copy-start | bytes 4708
  12.8 9.5 %copy-start.5 = (bf16[49,2048]{1,0:T(8,128)(2,1)S(1)}, bf16[49,2048]{1,0:T(8,128)(2,1)}, u32[]{:S(2)}) copy-start(bf16[49,2048]{1,0:T(8,128)(2,1)} %constant.17.clone.taps_ref) | copy-start | bytes 602116
  12.8 12.1 %copy-start.2 = (bf16[256,768]{1,0:T(8,128)(2,1)S(1)}, bf16[256,768]{1,0:T(8,128)(2,1)}, u32[]{:S(2)}) copy-start(bf16[256,768]{1,0:T(8,128)(2,1)} %project_ref.1) | copy-start | bytes 1179652
  12.9 10.5 %collective-permute-start.3 = (bf16[22,4,256]{2,1,0:T(4,128)(2,1)S(1)}, bf16[22,4,256]{2,1,0:T(4,128)(2,1)S(1)}, u32[]{:S(2)}, u32[]{:S(2)}) collective-permute-start(bf16[22,4,256]{2,1,0:T(4,128)(2,1)S(1)} %get-tuple-element.44), channel_id=1, source_target_pairs={{1,2},{2,1},{3,4},{4,3},{5,6},{6,5},{7,8},{8,7},{9,10},{10,9},{11,... | collective-permute-start | bytes 135176 | tf_op jit(solution)/shard_map/ppermute | solution.py:283
  22.0 2.9 %collective-permute-start.2 = (bf16[22,4,256]{2,1,0:T(4,128)(2,1)S(1)}, bf16[22,4,256]{2,1,0:T(4,128)(2,1)S(1)}, u32[]{:S(2)}, u32[]{:S(2)}) collective-permute-start(bf16[22,4,256]{2,1,0:T(4,128)(2,1)S(1)} %get-tuple-element.45), channel_id=1, source_target_pairs={{0,1},{1,0},{2,3},{3,2},{4,5},{5,4},{6,7},{7,6},{8,9},{9,8},{10,11... | collective-permute-start | bytes 135176 | tf_op jit(solution)/shard_map/ppermute | solution.py:283
  22.3 2.7 %copy-start.4 = (bf16[16,8,256]{2,1,0:T(8,128)(2,1)S(1)}, bf16[16,8,256]{2,1,0:T(8,128)(2,1)}, u32[]{:S(2)}) copy-start(bf16[16,8,256]{2,1,0:T(8,128)(2,1)} %own_ref.1) | copy-start | bytes 196612
  22.3 2.7 %copy-start.6 = (bf16[256,256]{1,0:T(8,128)(2,1)S(1)}, bf16[256,256]{1,0:T(8,128)(2,1)}, u32[]{:S(2)}) copy-start(bf16[256,256]{1,0:T(8,128)(2,1)} %out_ref.1) | copy-start | bytes 393220
  31.2 14.4 %copy-start = (bf16[256,256]{1,0:T(8,128)(2,1)S(1)}, bf16[256,256]{1,0:T(8,128)(2,1)}, u32[]{:S(2)}) copy-start(bf16[256,256]{1,0:T(8,128)(2,1)} %up_ref.1) | copy-start | bytes 393220
  31.2 14.4 %copy-start.1 = (bf16[256,256]{1,0:T(8,128)(2,1)S(1)}, bf16[256,256]{1,0:T(8,128)(2,1)}, u32[]{:S(2)}) copy-start(bf16[256,256]{1,0:T(8,128)(2,1)} %down_ref.1) | copy-start | bytes 393220
  31.2 14.3 %all-to-all-start = ((bf16[16,16,512]{2,1,0:T(8,128)(2,1)}), bf16[16,16,512]{2,1,0:T(8,128)(2,1)S(1)}, u32[]{:S(2)}, u32[]{:S(2)}) async-start(bf16[16,16,512]{2,1,0:T(8,128)(2,1)} %bitcast.2), calls=%async_computation | async-start | bytes 524288 | tf_op jit(solution)/shard_map/all_to_all | solution.py:303
  36.8 5.2 %collective-permute-start.7 = (bf16[3,256,256]{2,1,0:T(8,128)(2,1)S(1)}, bf16[3,256,256]{2,1,0:T(8,128)(2,1)S(1)}, u32[]{:S(2)}, u32[]{:S(2)}) collective-permute-start(bf16[3,256,256]{2,1,0:T(8,128)(2,1)S(1)} %get-tuple-element.28.mine_ref), channel_id=1, source_target_pairs={{0,64},{64,0},{128,192},{192,128},{1,65},{65,1},{129,193},{193,129... | collective-permute-start | bytes 1179656 | tf_op jit(solution)/shard_map/ppermute | solution.py:287
  47.7 6.5 %collective-permute-start.8 = (bf16[2,4,2,64,256]{4,3,2,1,0:T(8,128)(2,1)S(1)}, bf16[2,4,2,64,256]{4,3,2,1,0:T(8,128)(2,1)S(1)}, u32[]{:S(2)}, u32[]{:S(2)}) collective-permute-start(bf16[2,4,2,64,256]{4,3,2,1,0:T(8,128)(2,1)S(1)} %get-tuple-element.31), channel_id=1, source_target_pairs={{0,64},{64,0},{128,192},{192,128},{1,65},{65,1},{129,193},{193,129... | collective-permute-start | bytes 1572872 | tf_op jit(solution)/shard_map/ppermute | solution.py:287
  54.3 7.6 %collective-permute-start.9 = (bf16[4,2,64,256]{3,2,1,0:T(8,128)(2,1)S(1)}, bf16[4,2,64,256]{3,2,1,0:T(8,128)(2,1)S(1)}, u32[]{:S(2)}, u32[]{:S(2)}) collective-permute-start(bf16[4,2,64,256]{3,2,1,0:T(8,128)(2,1)S(1)} %fusion), channel_id=1, source_target_pairs={{0,128},{64,192},{128,0},{192,64},{1,129},{65,193},{129,1},{193,65... | collective-permute-start | bytes 786440 | tf_op jit(solution)/shard_map/ppermute | solution.py:287
  54.4 13.1 %all-to-all-start.1 = ((bf16[16,16,256]{2,1,0:T(8,128)(2,1)}), bf16[16,16,256]{2,1,0:T(8,128)(2,1)S(1)}, u32[]{:S(2)}, u32[]{:S(2)}) async-start(bf16[16,16,256]{2,1,0:T(8,128)(2,1)} %bitcast.5), calls=%async_computation.1 | async-start | bytes 262144 | tf_op jit(solution)/shard_map/all_to_all | solution.py:303
  62.0 6.3 %collective-permute-start.12 = (bf16[2,64,256]{2,1,0:T(8,128)(2,1)S(1)}, bf16[2,64,256]{2,1,0:T(8,128)(2,1)S(1)}, u32[]{:S(2)}, u32[]{:S(2)}) collective-permute-start(bf16[2,64,256]{2,1,0:T(8,128)(2,1)S(1)} %get-tuple-element.41), channel_id=1, source_target_pairs={{0,3},{1,2},{2,1},{3,0},{4,7},{5,6},{6,5},{7,4},{8,11},{9,10},{10,... | collective-permute-start | bytes 196616 | tf_op jit(solution)/shard_map/ppermute | solution.py:287
  63.4 8.0 %collective-permute-start.11 = (bf16[2,64,256]{2,1,0:T(8,128)(2,1)S(1)}, bf16[2,64,256]{2,1,0:T(8,128)(2,1)S(1)}, u32[]{:S(2)}, u32[]{:S(2)}) collective-permute-start(bf16[2,64,256]{2,1,0:T(8,128)(2,1)S(1)} %get-tuple-element.42), channel_id=1, source_target_pairs={{0,2},{1,3},{2,0},{3,1},{4,6},{5,7},{6,4},{7,5},{8,10},{9,11},{10,... | collective-permute-start | bytes 196616 | tf_op jit(solution)/shard_map/ppermute | solution.py:287
  65.7 5.7 %collective-permute-start.10 = (bf16[2,64,256]{2,1,0:T(8,128)(2,1)S(1)}, bf16[2,64,256]{2,1,0:T(8,128)(2,1)S(1)}, u32[]{:S(2)}, u32[]{:S(2)}) collective-permute-start(bf16[2,64,256]{2,1,0:T(8,128)(2,1)S(1)} %get-tuple-element.43), channel_id=1, source_target_pairs={{0,1},{1,0},{2,3},{3,2},{4,5},{5,4},{6,7},{7,6},{8,9},{9,8},{10,11... | collective-permute-start | bytes 196616 | tf_op jit(solution)/shard_map/ppermute | solution.py:287
  72.2 3.7 %collective-permute-start.15 = (bf16[2,64,256]{2,1,0:T(8,128)(2,1)S(1)}, bf16[2,64,256]{2,1,0:T(8,128)(2,1)S(1)}, u32[]{:S(2)}, u32[]{:S(2)}) collective-permute-start(bf16[2,64,256]{2,1,0:T(8,128)(2,1)S(1)} %get-tuple-element.36.own_ref), channel_id=1, source_target_pairs={{0,192},{64,128},{128,64},{192,0},{1,193},{65,129},{129,65},{193,1... | collective-permute-start | bytes 196616 | tf_op jit(solution)/shard_map/ppermute | solution.py:287
  73.7 4.6 %collective-permute-start.14 = (bf16[2,64,256]{2,1,0:T(8,128)(2,1)S(1)}, bf16[2,64,256]{2,1,0:T(8,128)(2,1)S(1)}, u32[]{:S(2)}, u32[]{:S(2)}) collective-permute-start(bf16[2,64,256]{2,1,0:T(8,128)(2,1)S(1)} %get-tuple-element.36.own_ref), channel_id=1, source_target_pairs={{0,128},{64,192},{128,0},{192,64},{1,129},{65,193},{129,1},{193,65... | collective-permute-start | bytes 196616 | tf_op jit(solution)/shard_map/ppermute | solution.py:287
  75.1 3.2 %collective-permute-start.13 = (bf16[2,64,256]{2,1,0:T(8,128)(2,1)S(1)}, bf16[2,64,256]{2,1,0:T(8,128)(2,1)S(1)}, u32[]{:S(2)}, u32[]{:S(2)}) collective-permute-start(bf16[2,64,256]{2,1,0:T(8,128)(2,1)S(1)} %get-tuple-element.36.own_ref), channel_id=1, source_target_pairs={{0,64},{64,0},{128,192},{192,128},{1,65},{65,1},{129,193},{193,129... | collective-permute-start | bytes 196616 | tf_op jit(solution)/shard_map/ppermute | solution.py:287

commit v2 on v1

--- a/solution.py
+++ b/solution.py
@@ -63,17 +63,43 @@
     return table.reshape(WINDOW * WINDOW, 2048), outside.reshape(1, 2048).astype(np.float32)
 
 
-def mark_kernel(state_ref, land_ref, marked_ref, even_ref, odd_ref):
-    land = jnp.broadcast_to(land_ref[...][:, :, None], (ROWS, COLS, D))
+def column(table):
+    return jnp.concatenate([table[:, i : i + 1] for i in range(ROWS)], axis=0)
+
+
+def mark_kernel(state_ref, land_ref, up_ref, down_ref, marked_ref, even_ref, odd_ref, half_ref):
+    even = lax.axis_index("lat") & 1 == 0
+    land = column(land_ref[...]).reshape(ROWS, COLS, 1)
     marked = jnp.where(land > 0, state_ref[...].astype(F32), LAND).astype(BF)
     marked_ref[...] = marked
-    even = lax.axis_index("lat") & 1 == 0
     top, bottom = marked[:REACH], marked[ROWS - REACH :]
     even_ref[...] = jnp.where(even, bottom, top)
     odd_ref[...] = jnp.where(even, top, bottom)
-
-
-def prepare_kernel(pos_ref, taps_ref, outside_ref, labels_ref, cot_ref, land_ref, bias_ref, place_ref, sendc_ref):
+    half_ref[...] = jnp.where(even, up_ref[...], down_ref[...])
+
+
+def prepare_kernel(
+    pos_ref,
+    taps_ref,
+    outside_ref,
+    labels_ref,
+    cot_ref,
+    land_ref,
+    state_ref,
+    gain1_ref,
+    gain2_ref,
+    project_ref,
+    bias_ref,
+    place_ref,
+    sendc_ref,
+    triple_ref,
+    gains_ref,
+):
+    land = column(land_ref[...])
+    gains_ref[0:1] = gain1_ref[...]
+    gains_ref[1:2] = gain2_ref[...]
+    own = state_ref[...].astype(F32).reshape(CELLS, D)
+    triple_ref[...] = dot(layer_norm(own, gain1_ref[...]), project_ref[...]).astype(BF)
     pos = pos_ref[...]
     high = pos.astype(BF)
     rest = pos - high.astype(F32)
@@ -83,20 +109,20 @@
     bias = dot(high, taps) + dot(middle, taps) + dot(low, taps) + outside_ref[...]
     for q in range(16):
         bias_ref[q * 8 : q * 8 + 8, :] = bias[:, q * 128 : q * 128 + 128]
-    labels = labels_ref[...]
-    named = lax.broadcasted_iota(jnp.int32, (EXPERTS, CELLS), 0) == labels
+    labels = column(labels_ref[...])
+    named = lax.broadcasted_iota(jnp.int32, (CELLS, EXPERTS), 1) == labels
     named = jnp.where(named, 1.0, 0.0)
-    earlier = lax.broadcasted_iota(jnp.int32, (CELLS, CELLS), 0) < lax.broadcasted_iota(
-        jnp.int32, (CELLS, CELLS), 1
-    )
-    before = dot(named.astype(BF), jnp.where(earlier, 1.0, 0.0).astype(BF))
-    rank = jnp.sum(before * named, axis=0, keepdims=True)
+    earlier = lax.broadcasted_iota(jnp.int32, (CELLS, CELLS), 1) < lax.broadcasted_iota(
+        jnp.int32, (CELLS, CELLS), 0
+    )
+    before = dot(jnp.where(earlier, 1.0, 0.0).astype(BF), named.astype(BF))
+    rank = jnp.sum(before * named, axis=1, keepdims=True)
     slot = labels * CAP + rank.astype(jnp.int32)
-    place = lax.broadcasted_iota(jnp.int32, (SLOTS, CELLS), 0) == slot
+    place = lax.broadcasted_iota(jnp.int32, (CELLS, SLOTS), 1) == slot
     place = jnp.where(place, 1.0, 0.0).astype(BF)
     place_ref[...] = place
-    tangent = cot_ref[...].astype(F32).reshape(CELLS, D) * land_ref[...].astype(F32)
-    sendc_ref[...] = dot(place, tangent.astype(BF)).astype(BF)
+    tangent = cot_ref[...].astype(F32).reshape(CELLS, D) * land.astype(F32)
+    sendc_ref[...] = t_dot(place, tangent.astype(BF)).astype(BF)
 
 
 def in_order(axis, even_ref, odd_ref):
@@ -112,56 +138,53 @@
     lon_even_ref,
     lon_odd_ref,
     land_ref,
-    gain1_ref,
-    gain2_ref,
+    gains_ref,
+    triple_ref,
     project_ref,
     out_ref,
     bias_ref,
     place_ref,
     sendc_ref,
+    half_ref,
     near_ref,
-    middle_ref,
-    far_ref,
     residual_ref,
     send_ref,
     fetched_ref,
-    ext_ref,
+    side_ref,
     pen_ref,
 ):
-    fetched_ref[0] = near_ref[...]
-    fetched_ref[1] = middle_ref[...]
-    fetched_ref[2] = far_ref[...]
+    fetched_ref[0] = half_ref[...]
+    fetched_ref[1] = near_ref[...]
     lat = lax.axis_index("lat")
     top = jnp.where(lat == 0, FAR, 0.0).astype(F32)
     bottom = jnp.where(lat == lax.axis_size("lat") - 1, FAR, 0.0).astype(F32)
-    own3 = own_ref[...].astype(F32)
     up, down = in_order("lat", lat_even_ref, lat_odd_ref)
     left, right = in_order("lon", lon_even_ref, lon_odd_ref)
+    side_ref[:, 0:4] = left
+    side_ref[:, 4:8] = right
+    side = side_ref[...]
 
     def marked(piece):
         return jnp.where(piece[:, :, 0:128] > 0.5 * LAND, FAR, 0.0)
 
-    ext_ref[0:REACH, 0:8, :] = up
-    ext_ref[REACH : REACH + ROWS, 0:8, :] = own3
-    ext_ref[REACH + ROWS : EXT, 0:8, :] = down
-    ext_ref[:, 8:12, :] = left
-    ext_ref[:, 12:16, :] = right
-    land = land_ref[...].reshape(ROWS, COLS, 1)
-    pen_ref[0:REACH, 0:8, :] = marked(up)
-    pen_ref[REACH : REACH + ROWS, 0:8, :] = jnp.broadcast_to(
-        jnp.where(land > 0, 0.0, FAR), (ROWS, COLS, 128)
-    )
-    pen_ref[REACH + ROWS : EXT, 0:8, :] = marked(down)
-    pen_ref[:, 8:12, :] = marked(left)
-    pen_ref[:, 12:16, :] = marked(right)
+    own_rows = pl.ds(REACH, ROWS)
+    land = column(land_ref[...]).reshape(ROWS, COLS, 1)
+    pen_ref[:, 8:16] = marked(side)
+    pen_ref[0:REACH, 0:8] = marked(up)
+    pen_ref[own_rows, 0:8] = jnp.broadcast_to(jnp.where(land > 0, 0.0, FAR), (ROWS, COLS, 128))
+    pen_ref[REACH + ROWS : EXT, 0:8] = marked(down)
     pen_ref[0:REACH] = pen_ref[0:REACH] + top
     pen_ref[REACH + ROWS : EXT] = pen_ref[REACH + ROWS : EXT] + bottom
-    own = own3.reshape(CELLS, D)
-    gain1 = gain1_ref[...]
-    normed = layer_norm(ext_ref[...].reshape(EXT * 16, D), gain1)
-    keyvals = dot(normed, project_ref[:, D : 3 * D]).astype(BF)
-    queries = dot(layer_norm(own, gain1), project_ref[:, 0:D]).astype(BF)
     pen = pen_ref[...].reshape(EXT * 16, 128).astype(BF)
+
+    halo = jnp.concatenate([side, up, down], axis=0).reshape((EXT + 2 * REACH) * 8, D)
+    halo = dot(layer_norm(halo, gains_ref[0:1]), project_ref[:, D : 3 * D])
+    halo = halo.reshape(EXT + 2 * REACH, 8, 2 * D)
+    middle = triple_ref[:, D : 3 * D].astype(F32).reshape(ROWS, COLS, 2 * D)
+    middle = jnp.concatenate([halo[EXT : EXT + REACH], middle, halo[EXT + REACH :]], axis=0)
+    keyvals = jnp.concatenate([middle, halo[:EXT]], axis=1).reshape(EXT * 16, 2 * D).astype(BF)
+    queries = triple_ref[:, 0:D]
+    own = own_ref[...].astype(F32).reshape(CELLS, D)
 
     row = lax.broadcasted_iota(jnp.int32, (128, D), 0)
     lane = lax.broadcasted_iota(jnp.int32, (128, D), 1)
@@ -180,27 +203,32 @@
     ).astype(BF)
     row = lax.broadcasted_iota(jnp.int32, (128, 128), 0)
     lane = lax.broadcasted_iota(jnp.int32, (128, 128), 1)
-    first_lane = jnp.where(lane == 0, 1.0, 0.0).astype(BF)
+    first_lane = jnp.where(lane[0:8] == 0, 1.0, 0.0).astype(BF)
     query = row // HEADS
     centre = lane == (query // COLS + REACH) * 16 + query % COLS
     bias = bias_ref[...]
     scale = 1.0 / math.sqrt(HD)
+    closed = dot_t(first_lane, pen)
+    pairs = range(ROWS // 2)
+    scores = []
+    for pair in pairs:
+        wide = (dot(spread, queries[16 * pair : 16 * pair + 16]) * head_mask).astype(BF)
+        scores.append(dot_t(wide, keyvals[32 * pair : 32 * pair + 128, 0:D]))
+    weights = []
+    for pair in pairs:
+        shut = jnp.concatenate([closed[:, 32 * pair : 32 * pair + 128]] * 16, axis=0)
+        score = scores[pair] * scale + bias + jnp.where(centre, 0.0, shut)
+        raw = jnp.exp(score - jnp.max(score, axis=1, keepdims=True))
+        weights.append((raw / jnp.sum(raw, axis=1, keepdims=True)).astype(BF))
     pieces = []
-    for pair in range(ROWS // 2):
-        keys = keyvals[32 * pair : 32 * pair + 128, 0:D]
-        values = keyvals[32 * pair : 32 * pair + 128, D : 2 * D]
-        wide = (dot(spread, queries[16 * pair : 16 * pair + 16]) * head_mask).astype(BF)
-        closed = dot_t(first_lane, pen[32 * pair : 32 * pair + 128])
-        scores = dot_t(wide, keys) * scale + bias + jnp.where(centre, 0.0, closed)
-        raw = jnp.exp(scores - jnp.max(scores, axis=1, keepdims=True))
-        weights = (raw / jnp.sum(raw, axis=1, keepdims=True)).astype(BF)
-        taken = (dot(weights, values) * head_mask).astype(BF)
-        pieces.append(dot(gather, taken))
+    for pair in pairs:
+        taken = dot(weights[pair], keyvals[32 * pair : 32 * pair + 128, D : 2 * D])
+        pieces.append(dot(gather, (taken * head_mask).astype(BF)))
     attended = jnp.concatenate(pieces, axis=0).astype(BF)
     residual = (own + dot(attended, out_ref[...])).astype(BF)
     residual_ref[...] = residual
-    second = layer_norm(residual.astype(F32), gain2_ref[...])
-    send_ref[:, 0:D] = dot(place_ref[...], second).astype(BF)
+    second = layer_norm(residual.astype(F32), gains_ref[1:2])
+    send_ref[:, 0:D] = t_dot(place_ref[...], second).astype(BF)
     send_ref[:, D : 2 * D] = sendc_ref[...]
 
 
@@ -211,7 +239,17 @@
 
 
 def expert_kernel(
-    got_ref, up_ref, down_ref, mine_ref, other_ref, outputs_ref, keep_ref, give_ref, grad_ref
+    got_ref,
+    up_ref,
+    down_ref,
+    mine1_ref,
+    mine2_ref,
+    other1_ref,
+    other2_ref,
+    outputs_ref,
+    keep_ref,
+    give_ref,
+    grad_ref,
 ):
     lat = lax.axis_index("lat")
     first_core = lat & 1 == 0
@@ -220,8 +258,8 @@
     outputs = jnp.zeros((SLOTS, D), F32)
     for member in range(4):
         if member:
-            mine = mine_ref[member - 1]
-            other = other_ref[member - 1]
+            mine = mine1_ref[...] if member == 1 else mine2_ref[member - 2]
+            other = other1_ref[...] if member == 1 else other2_ref[member - 2]
             up = jnp.where(first_core, mine, other)
             down = jnp.where(first_core, other, mine)
         else:
@@ -247,8 +285,8 @@
 def combine_kernel(
     returned_ref, place_ref, residual_ref, land_ref, part_ref, a_ref, b_ref, c_ref, block_ref, total_ref
 ):
-    rows = t_dot(place_ref[...], returned_ref[...])
-    land = land_ref[...].astype(F32)
+    rows = dot(place_ref[...], returned_ref[...])
+    land = column(land_ref[...]).astype(F32)
     block_ref[...] = (
         (land * (residual_ref[...].astype(F32) + rows)).astype(BF).reshape(ROWS, COLS, D)
     )
@@ -264,14 +302,29 @@
         down_ref[pl.ds(start, 64), :] = ref[1].astype(F32)
 
 
-def call(kernel, outs, args, scratch=()):
+def call(kernel, outs, args, scratch=(), fetch=0):
+    def fetching(*refs):
+        kept = len(args) + len(outs) + len(scratch)
+        copies = [
+            pltpu.make_async_copy(refs[i], refs[kept + i], refs[-1].at[i]) for i in range(fetch)
+        ]
+        for copy in copies:
+            copy.start()
+        for copy in copies:
+            copy.wait()
+        kernel(*refs[kept : kept + fetch], *refs[fetch:kept])
+
+    spaces = [pltpu.HBM] * fetch + [pltpu.VMEM] * (len(args) - fetch)
+    landing = [pltpu.VMEM(arg.shape, arg.dtype) for arg in args[:fetch]]
+    if fetch:
+        landing.append(pltpu.SemaphoreType.DMA((fetch,)))
     return pl.pallas_call(
-        kernel,
+        fetching if fetch else kernel,
         out_shape=[jax.ShapeDtypeStruct(shape, dtype) for shape, dtype in outs],
-        in_specs=vmem(len(args)),
+        in_specs=[pl.BlockSpec(memory_space=space) for space in spaces],
         out_specs=vmem(len(outs)),
-        scratch_shapes=list(scratch),
-        compiler_params=pltpu.CompilerParams(vmem_limit_bytes=VMEM_LIMIT),
+        scratch_shapes=list(scratch) + landing,
+        compiler_params=pltpu.CompilerParams(vmem_limit_bytes=None if fetch else VMEM_LIMIT),
     )(*args)
 
 
@@ -318,10 +371,12 @@
     up_weight,
     down_weight,
 ):
-    marked, even, odd = call(
+    land = land_sea.T
+    marked, even, odd, half = call(
         mark_kernel,
-        [((ROWS, COLS, D), BF), ((REACH, COLS, D), BF), ((REACH, COLS, D), BF)],
-        (state, land_sea),
+        [((ROWS, COLS, D), BF), ((REACH, COLS, D), BF), ((REACH, COLS, D), BF), ((D, UNITS), BF)],
+        (state, land, up_weight, down_weight),
+        fetch=4,
     )
     lat_even = pair_up(even, "lat", 0, False)
     lat_odd = pair_up(odd, "lat", 1, False)
@@ -333,49 +388,67 @@
     lon_odd = pair_up(jnp.where(at_even, tall[:, :4], tall[:, 4:]), "lon", 1, True)
     lon_even = pair_up(jnp.where(at_even, tall[:, 4:], tall[:, :4]), "lon", 0, True)
 
-    land_column = land_sea.reshape(CELLS, 1)
     taps, outside = tap_tables()
-    bias, place, sendc = call(
+    bias, place, sendc, triple, gains = call(
         prepare_kernel,
-        [((128, 128), F32), ((SLOTS, CELLS), BF), ((SLOTS, D), BF)],
+        [
+            ((128, 128), F32),
+            ((CELLS, SLOTS), BF),
+            ((SLOTS, D), BF),
+            ((CELLS, 3 * D), BF),
+            ((2, D), F32),
+        ],
         (
             pos_bias,
             jnp.asarray(taps, BF),
             jnp.asarray(outside),
-            regime.reshape(1, CELLS),
+            regime.reshape(ROWS, COLS).T,
             cotangent,
-            land_column,
+            land,
+            state,
+            first_gain.reshape(1, D),
+            second_gain.reshape(1, D),
+            project_weight,
         ),
     )
-    half = jnp.where(lax.axis_index("lat") & 1 == 0, up_weight, down_weight)
-    fetched = [swap(half, "lon", mask) for mask in (1, 2, 3)]
-
-    residual, send, fetched = call(
+    fetched = swap(half, "lon", 1)
+
+    residual, send, known = call(
         attention_kernel,
-        [((CELLS, D), BF), ((SLOTS, 2 * D), BF), ((3, D, UNITS), BF)],
+        [((CELLS, D), BF), ((SLOTS, 2 * D), BF), ((2, D, UNITS), BF)],
         (
             state,
             lat_even,
             lat_odd,
             lon_even,
             lon_odd,
-            land_column,
-            first_gain.reshape(1, D),
-            second_gain.reshape(1, D),
+            land,
+            gains,
+            triple,
             project_weight,
             out_weight,
             bias,
             place,
             sendc,
-            *fetched,
+            half,
+            fetched,
         ),
-        (pltpu.VMEM((EXT, 16, D), F32), pltpu.VMEM((EXT, 16, 128), F32)),
+        (pltpu.VMEM((EXT, 8, D), F32), pltpu.VMEM((EXT, 16, 128), F32)),
     )
     got = exchange(send.reshape(EXPERTS, CAP, 2 * D)).reshape(SLOTS, 2 * D)
+    beyond = swap(known, "lon", 2)
     outputs, keep, give = call(
         expert_kernel,
         [((SLOTS, D), BF), ((2, 4, 2, 64, D), F32), ((2, 4, 2, 64, D), BF)],
-        (got, up_weight, down_weight, fetched, swap(fetched, "lat", 1)),
+        (
+            got,
+            up_weight,
+            down_weight,
+            fetched,
+            beyond,
+            swap(fetched, "lat", 1),
+            swap(beyond, "lat", 1),
+        ),
         (pltpu.VMEM((4, 2, 256, D), F32),),
     )
     near = swap(give, "lat", 1)
@@ -388,7 +461,7 @@
     block, total = call(
         combine_kernel,
         [((ROWS, COLS, D), BF), ((2, 64, D), BF)],
-        (returned, place, residual, land_column, part[0], *others),
+        (returned, place, residual, land, part[0], *others),
     )
     grad_up, grad_down = call(
         gather_kernel,

time: 79.5 us -> 75.6 us (0.951)
  starting transfers between devices: 44.2 us -> 37.6 us
  waiting for transfers between devices: 20.4 us -> 25.1 us
  local copies, waits for them, and re-layouts: 1.93 us -> 0.7 us
    ppermute x12, waiting for transfers between devices: 12.9 us -> 20.3 us  [swap(): lax.ppermute(value, axis, [(i, i ^ mask) for i in range(lax.axis_size(axi...]
    ppermute x12, starting transfers between devices: 19.7 us -> 14.7 us  [swap(): lax.ppermute(value, axis, [(i, i ^ mask) for i in range(lax.axis_size(axi...]
    all_to_all x2, waiting for transfers between devices: 5.3 us -> 1.02 us  [exchange(): lax.all_to_all(value, ('lat', 'lon'), 0, 0, axis_index_groups=expert_grou...]
    ppermute x4, waiting for transfers between devices: 2.16 us -> 3.78 us  [pair_up(): return lax.ppermute(value, axis, pairs)]
    all_to_all x2, starting transfers between devices: 10.1 us -> 8.76 us  [exchange(): lax.all_to_all(value, ('lat', 'lon'), 0, 0, axis_index_groups=expert_grou...]
    unnamed x28, local copies, waits for them, and re-layouts: 1.74 us -> 0.67 us
    select_n x1 -> x0, other arithmetic: 0.93 us -> none  [on_device(): half = jnp.where(lax.axis_index('lat') & 1 == 0, up_weight, down_weight)]
    concatenate x1, other arithmetic: 0.01 us -> 0.85 us  [on_device(): tall = jnp.concatenate([up, marked, down], axis=0)]
  transfers between devices with their start and end apart: 18 -> 18, of which waited for: 11 -> 10; matrix products, arithmetic and copies ran while one was open for 2% -> 1% of each run, Pallas kernels for 1% -> 1%
where the time goes in v2:
time: 75.6 us; the launch traced here: 75.3 us
  starting transfers between devices  37.6 us (50%)
  waiting for transfers between devices  25.1 us (33%)
  Pallas kernels  9.94 us (13%)
  other arithmetic  1.1 us (1%)
  between operations  0.89 us (1%)
    ppermute x12, waiting for transfers between devices, swap(): lax.ppermute(value, axis, [(i, i ^ mask) for i in range(lax.axis_size(axi...  20.3 us
    ppermute x12, starting transfers between devices, swap(): lax.ppermute(value, axis, [(i, i ^ mask) for i in range(lax.axis_size(axi...  14.7 us
    ppermute x4, starting transfers between devices, pair_up(): return lax.ppermute(value, axis, pairs)  14.1 us
    pallas_call x6, Pallas kernels, call(): pl.pallas_call(fetching if fetch else kernel, out_shape=[jax.ShapeDtypeSt...  9.94 us
    all_to_all x2, starting transfers between devices, exchange(): lax.all_to_all(value, ('lat', 'lon'), 0, 0, axis_index_groups=expert_grou...  8.76 us
    ppermute x4, waiting for transfers between devices, pair_up(): return lax.ppermute(value, axis, pairs)  3.78 us
  transfers between devices with their start and end apart: 18, of which 10 were waited for; matrix products, arithmetic and copies ran while one was open for 1% of the time, Pallas kernels for 1%

profile of v2, /device:TPU:1, one launch (start us, length us, event | category | flops | bytes accessed | tf_op | source)
XLA Modules:
  0.0 75.3 jit_solution(14552835700226512876)
XLA Ops:
  0.6 0.0 copy-start
  0.6 1.9 %shard_map.148 = (bf16[16,8,256]{2,1,0:T(8,128)(2,1)}, bf16[3,8,256]{2,1,0:T(8,128)(2,1)}, bf16[3,8,256]{2,1,0:T(8,128)(2,1)}, bf16[256,256]{1,0:T(8,128)(2,1)}) custom-call(bf16[16,8,256]{2,1,0:T(8,128)(2,1)} %own_ref.1, s32[8,16]{1,0:T(8,128)} %bitcast.25, bf16[256,256]{1,0:T(8,128)(2,1)} %up_ref.1, bf16[256,256]{1,0:T(8,128)(2,1)} %down_ref.1), custom_call_target="tpu_custom_call" | custom-call | tf_op jit(solution)/shard_map/pallas_call | solution.py:321
  2.5 0.0 copy-start.4
  2.6 3.3 %collective-permute-start = (bf16[3,8,256]{2,1,0:T(8,128)(2,1)}, bf16[3,8,256]{2,1,0:T(8,128)(2,1)S(1)}, u32[]{:S(2)}, u32[]{:S(2)}) collective-permute-start(bf16[3,8,256]{2,1,0:T(8,128)(2,1)} %get-tuple-element.24), channel_id=1, source_target_pairs={{0,64},{64,0},{128,192},{192,128},{1,65},{65,1},{129,193},{193,129... | collective-permute-start | bytes 36872 | tf_op jit(solution)/shard_map/ppermute | solution.py:336
  5.9 1.9 %collective-permute-start.1 = (bf16[3,8,256]{2,1,0:T(8,128)(2,1)}, bf16[3,8,256]{2,1,0:T(8,128)(2,1)S(1)}, u32[]{:S(2)}, u32[]{:S(2)}) collective-permute-start(bf16[3,8,256]{2,1,0:T(8,128)(2,1)} %get-tuple-element.25), channel_id=1, source_target_pairs={{64,128},{128,64},{65,129},{129,65},{66,130},{130,66},{67,131},{13... | collective-permute-start | bytes 36872 | tf_op jit(solution)/shard_map/ppermute | solution.py:336
  7.8 1.1 %collective-permute-start.4 = (bf16[256,256]{1,0:T(8,128)(2,1)}, bf16[256,256]{1,0:T(8,128)(2,1)S(1)}, u32[]{:S(2)}, u32[]{:S(2)}) collective-permute-start(bf16[256,256]{1,0:T(8,128)(2,1)} %get-tuple-element.32.half_ref), channel_id=1, source_target_pairs={{0,1},{1,0},{2,3},{3,2},{4,5},{5,4},{6,7},{7,6},{8,9},{9,8},{10,11... | collective-permute-start | bytes 393224 | tf_op jit(solution)/shard_map/ppermute | solution.py:340
  8.9 0.0 collective-permute-done.lat_even_ref
  8.9 2.5 %collective-permute-done.1.lat_odd_ref = bf16[3,8,256]{2,1,0:T(8,128)(2,1)S(1)} collective-permute-done((bf16[3,8,256]{2,1,0:T(8,128)(2,1)}, bf16[3,8,256]{2,1,0:T(8,128)(2,1)S(1)}, u32[]{:S(2)}, u32[]{:S(2)}) %collective-permute-start.1) | collective-permute-done | bytes 12320 | tf_op jit(solution)/shard_map/ppermute | solution.py:336
  11.4 0.9 %pad_maximum_fusion = bf16[22,8,256]{2,1,0:T(8,128)(2,1)S(1)} fusion(bf16[3,8,256]{2,1,0:T(8,128)(2,1)S(1)} %get-tuple-element.53, bf16[16,8,256]{2,1,0:T(8,128)(2,1)} %get-tuple-element.26, bf16[3,8,256]{2,1,0:T(8,128)(2,1)S(1)} %get-tuple-element.52), kind=kLoop, calls=%fused_computation.4 | loop fusion | flops 90112 | bytes 180224 | tf_op jit(solution)/shard_map/concatenate | solution.py:386
  12.2 0.0 copy-start.1
  12.3 0.0 copy-start.8
  12.3 0.0 copy-start.9
  12.3 0.0 copy-start.11
  12.3 0.0 copy-start.13
  12.3 0.1 broadcast_select_fusion
  12.4 0.0 copy-start.10
  12.4 0.0 copy-start.7
  12.4 8.8 %collective-permute-start.3 = (bf16[22,4,256]{2,1,0:T(4,128)(2,1)S(1)}, bf16[22,4,256]{2,1,0:T(4,128)(2,1)S(1)}, u32[]{:S(2)}, u32[]{:S(2)}) collective-permute-start(bf16[22,4,256]{2,1,0:T(4,128)(2,1)S(1)} %get-tuple-element.50), channel_id=1, source_target_pairs={{1,2},{2,1},{3,4},{4,3},{5,6},{6,5},{7,8},{8,7},{9,10},{10,9},{11,... | collective-permute-start | bytes 135176 | tf_op jit(solution)/shard_map/ppermute | solution.py:336
  21.2 0.0 collective-permute-start.2
  21.2 0.0 copy-done.4
  21.3 0.0 copy-done.1
  21.3 0.0 copy-done.8
  21.3 0.0 copy-done.9
  21.3 0.0 copy-done.11
  21.3 0.0 copy-done.13
  21.3 0.0 copy-done.10
  21.3 0.0 copy-done.7
  21.3 0.6 copy-done.12
  21.9 0.9 %shard_map.149 = (f32[128,128]{1,0:T(8,128)S(1)}, bf16[128,256]{1,0:T(8,128)(2,1)S(1)}, bf16[256,256]{1,0:T(8,128)(2,1)S(1)}, bf16[128,768]{1,0:T(8,128)(2,1)S(1)}, f32[2,256]{1,0:T(2,128)S(1)}) custom-call(f32[8,49]{1,0:T(8,128)S(1)} %copy-done.10, bf16[49,2048]{1,0:T(8,128)(2,1)S(1)} %copy-done.4, f32[1,2048]{1,0:T(1,128)S(1)} %copy-done.9, ...), custom_call_target="tpu_custom_call" | custom-call | tf_op jit(solution)/shard_map/pallas_call | solution.py:321
  22.8 0.0 collective-permute-done.3.lon_odd_ref
  22.8 1.3 %collective-permute-done.2.lon_even_ref = bf16[22,4,256]{2,1,0:T(4,128)(2,1)S(1)} collective-permute-done((bf16[22,4,256]{2,1,0:T(4,128)(2,1)S(1)}, bf16[22,4,256]{2,1,0:T(4,128)(2,1)S(1)}, u32[]{:S(2)}, u32[]{:S(2)}) %collective-permute-start.2) | collective-permute-done | bytes 45088 | tf_op jit(solution)/shard_map/ppermute | solution.py:336
  24.1 0.0 collective-permute-done.4.near_ref.mine1_ref
  24.1 3.4 %shard_map.150 = (bf16[128,256]{1,0:T(8,128)(2,1)S(1)}, bf16[256,512]{1,0:T(8,128)(2,1)}, bf16[2,256,256]{2,1,0:T(8,128)(2,1)S(1)}) custom-call(bf16[16,8,256]{2,1,0:T(8,128)(2,1)S(1)} %copy-done.1, bf16[3,8,256]{2,1,0:T(8,128)(2,1)S(1)} %collective-permute-done.lat_even_ref, bf16[3,8,256]{2,1,0:T(8,128)(2,1)S(1)} %collective-permute-done.1.lat_odd_ref, ...), custom_call_target="tpu_custom_call" | custom-call | tf_op jit(solution)/shard_map/pallas_call | solution.py:321
  27.5 0.0 collective-permute-start.5
  27.5 3.7 %all-to-all-start = ((bf16[16,16,512]{2,1,0:T(8,128)(2,1)}), bf16[16,16,512]{2,1,0:T(8,128)(2,1)S(1)}, u32[]{:S(2)}, u32[]{:S(2)}) async-start(bf16[16,16,512]{2,1,0:T(8,128)(2,1)} %bitcast.5), calls=%async_computation | async-start | bytes 524288 | tf_op jit(solution)/shard_map/all_to_all | solution.py:356
  31.2 8.7 %collective-permute-done.5.mine2_ref = bf16[2,256,256]{2,1,0:T(8,128)(2,1)S(1)} collective-permute-done((bf16[2,256,256]{2,1,0:T(8,128)(2,1)S(1)}, bf16[2,256,256]{2,1,0:T(8,128)(2,1)S(1)}, u32[]{:S(2)}, u32[]{:S(2)}) %collective-permute-start.5) | collective-permute-done | bytes 262176 | tf_op jit(solution)/shard_map/ppermute | solution.py:340
  39.9 0.5 collective-permute-start.7
  40.4 0.1 collective-permute-start.6
  40.4 1.3 %collective-permute-done.6.other1_ref = bf16[256,256]{1,0:T(8,128)(2,1)S(1)} collective-permute-done((bf16[256,256]{1,0:T(8,128)(2,1)S(1)}, bf16[256,256]{1,0:T(8,128)(2,1)S(1)}, u32[]{:S(2)}, u32[]{:S(2)}) %collective-permute-start.6) | collective-permute-done | bytes 131104 | tf_op jit(solution)/shard_map/ppermute | solution.py:340
  41.7 0.0 all-to-all-done
  41.7 0.0 collective-permute-done.7.other2_ref
  41.7 2.1 %shard_map.151 = (bf16[256,256]{1,0:T(8,128)(2,1)}, f32[2,4,2,64,256]{4,3,2,1,0:T(8,128)S(1)}, bf16[2,4,2,64,256]{4,3,2,1,0:T(8,128)(2,1)S(1)}) custom-call(bf16[256,512]{1,0:T(8,128)(2,1)S(1)} %bitcast.23, bf16[256,256]{1,0:T(8,128)(2,1)S(1)} %copy-done.2, bf16[256,256]{1,0:T(8,128)(2,1)S(1)} %copy-done.3, ...), custom_call_target="tpu_custom_call" | custom-call | tf_op jit(solution)/shard_map/pallas_call | solution.py:321
  43.9 4.6 %collective-permute-start.8 = (bf16[2,4,2,64,256]{4,3,2,1,0:T(8,128)(2,1)S(1)}, bf16[2,4,2,64,256]{4,3,2,1,0:T(8,128)(2,1)S(1)}, u32[]{:S(2)}, u32[]{:S(2)}) collective-permute-start(bf16[2,4,2,64,256]{4,3,2,1,0:T(8,128)(2,1)S(1)} %get-tuple-element.37), channel_id=1, source_target_pairs={{0,64},{64,0},{128,192},{192,128},{1,65},{65,1},{129,193},{193,129... | collective-permute-start | bytes 1572872 | tf_op jit(solution)/shard_map/ppermute | solution.py:340
  48.5 1.5 %collective-permute-done.8 = bf16[2,4,2,64,256]{4,3,2,1,0:T(8,128)(2,1)S(1)} collective-permute-done((bf16[2,4,2,64,256]{4,3,2,1,0:T(8,128)(2,1)S(1)}, bf16[2,4,2,64,256]{4,3,2,1,0:T(8,128)(2,1)S(1)}, u32[]{:S(2)}, u32[]{:S(2)}) %collective-permute-start.8) | collective-permute-done | bytes 524320 | tf_op jit(solution)/shard_map/ppermute | solution.py:340
  50.1 0.1 fusion
  50.1 0.1 collective-permute-start.9
  50.2 5.1 %all-to-all-start.1 = ((bf16[16,16,256]{2,1,0:T(8,128)(2,1)}), bf16[16,16,256]{2,1,0:T(8,128)(2,1)S(1)}, u32[]{:S(2)}, u32[]{:S(2)}) async-start(bf16[16,16,256]{2,1,0:T(8,128)(2,1)} %bitcast.8), calls=%async_computation.1 | async-start | bytes 262144 | tf_op jit(solution)/shard_map/all_to_all | solution.py:356
  55.3 2.4 %collective-permute-done.9 = bf16[4,2,64,256]{3,2,1,0:T(8,128)(2,1)S(1)} collective-permute-done((bf16[4,2,64,256]{3,2,1,0:T(8,128)(2,1)S(1)}, bf16[4,2,64,256]{3,2,1,0:T(8,128)(2,1)S(1)}, u32[]{:S(2)}, u32[]{:S(2)}) %collective-permute-start.9) | collective-permute-done | bytes 262176 | tf_op jit(solution)/shard_map/ppermute | solution.py:340
  57.7 0.1 fusion.1
  57.9 0.1 collective-permute-start.12
  58.0 4.7 %collective-permute-start.11 = (bf16[2,64,256]{2,1,0:T(8,128)(2,1)S(1)}, bf16[2,64,256]{2,1,0:T(8,128)(2,1)S(1)}, u32[]{:S(2)}, u32[]{:S(2)}) collective-permute-start(bf16[2,64,256]{2,1,0:T(8,128)(2,1)S(1)} %get-tuple-element.48), channel_id=1, source_target_pairs={{0,2},{1,3},{2,0},{3,1},{4,6},{5,7},{6,4},{7,5},{8,10},{9,11},{10,... | collective-permute-start | bytes 196616 | tf_op jit(solution)/shard_map/ppermute | solution.py:340
  62.6 0.2 collective-permute-start.10
  62.8 1.0 %all-to-all-done.1 = bf16[16,16,256]{2,1,0:T(8,128)(2,1)S(1)} async-done(((bf16[16,16,256]{2,1,0:T(8,128)(2,1)}), bf16[16,16,256]{2,1,0:T(8,128)(2,1)S(1)}, u32[]{:S(2)}, u32[]{:S(2)}) %all-to-all-start.1) | async-done | bytes 131104 | tf_op jit(solution)/shard_map/all_to_all | solution.py:356
  63.9 0.0 collective-permute-done.12.c_ref
  63.9 3.1 %collective-permute-done.11.b_ref = bf16[2,64,256]{2,1,0:T(8,128)(2,1)S(1)} collective-permute-done((bf16[2,64,256]{2,1,0:T(8,128)(2,1)S(1)}, bf16[2,64,256]{2,1,0:T(8,128)(2,1)S(1)}, u32[]{:S(2)}, u32[]{:S(2)}) %collective-permute-start.11) | collective-permute-done | bytes 65568 | tf_op jit(solution)/shard_map/ppermute | solution.py:340
  67.0 0.0 collective-permute-done.10.a_ref
  67.0 0.8 %shard_map.152 = (bf16[16,8,256]{2,1,0:T(8,128)(2,1)}, bf16[2,64,256]{2,1,0:T(8,128)(2,1)S(1)}) custom-call(bf16[256,256]{1,0:T(8,128)(2,1)S(1)} %bitcast.24, bf16[128,256]{1,0:T(8,128)(2,1)S(1)} %get-tuple-element.30.place_ref, bf16[128,256]{1,0:T(8,128)(2,1)S(1)} %get-tuple-element.39.residual_ref, s32[8,16]{1,0:T(8,128)S(1)} %bitcast.28, ...), custom_call_target="tpu_custom_call" | custom-call | tf_op jit(solution)/shard_map/pallas_call | solution.py:321
  67.8 1.8 %collective-permute-start.15 = (bf16[2,64,256]{2,1,0:T(8,128)(2,1)S(1)}, bf16[2,64,256]{2,1,0:T(8,128)(2,1)S(1)}, u32[]{:S(2)}, u32[]{:S(2)}) collective-permute-start(bf16[2,64,256]{2,1,0:T(8,128)(2,1)S(1)} %get-tuple-element.42.own_ref), channel_id=1, source_target_pairs={{0,192},{64,128},{128,64},{192,0},{1,193},{65,129},{129,65},{193,1... | collective-permute-start | bytes 196616 | tf_op jit(solution)/shard_map/ppermute | solution.py:340
  69.6 1.7 %collective-permute-start.14 = (bf16[2,64,256]{2,1,0:T(8,128)(2,1)S(1)}, bf16[2,64,256]{2,1,0:T(8,128)(2,1)S(1)}, u32[]{:S(2)}, u32[]{:S(2)}) collective-permute-start(bf16[2,64,256]{2,1,0:T(8,128)(2,1)S(1)} %get-tuple-element.42.own_ref), channel_id=1, source_target_pairs={{0,128},{64,192},{128,0},{192,64},{1,129},{65,193},{129,1},{193,65... | collective-permute-start | bytes 196616 | tf_op jit(solution)/shard_map/ppermute | solution.py:340
  71.2 0.0 collective-permute-start.13
  71.2 0.3 collective-permute-done.15.c_ref
  71.5 2.9 %collective-permute-done.14.b_ref = bf16[2,64,256]{2,1,0:T(8,128)(2,1)S(1)} collective-permute-done((bf16[2,64,256]{2,1,0:T(8,128)(2,1)S(1)}, bf16[2,64,256]{2,1,0:T(8,128)(2,1)S(1)}, u32[]{:S(2)}, u32[]{:S(2)}) %collective-permute-start.14) | collective-permute-done | bytes 65568 | tf_op jit(solution)/shard_map/ppermute | solution.py:340
  74.4 0.0 collective-permute-done.13.a_ref
  74.4 0.8 %shard_map.153 = (f32[256,256]{1,0:T(8,128)}, f32[256,256]{1,0:T(8,128)}) custom-call(bf16[2,64,256]{2,1,0:T(8,128)(2,1)S(1)} %get-tuple-element.42.own_ref, bf16[2,64,256]{2,1,0:T(8,128)(2,1)S(1)} %collective-permute-done.13.a_ref, bf16[2,64,256]{2,1,0:T(8,128)(2,1)S(1)} %collective-permute-done.14.b_ref, bf16[2,64,256]{2,1,0:T(8,128)(2,1)S(1)} %collective-permute-done.15.c_ref), custom_call_target="tpu_custom_call" | custom-call | tf_op jit(solution)/shard_map/pallas_call | solution.py:321
  (13 shorter events, 0.0 us)
Async XLA Ops:
  0.6 20.6 %copy-start = (bf16[256,768]{1,0:T(8,128)(2,1)S(1)}, bf16[256,768]{1,0:T(8,128)(2,1)}, u32[]{:S(2)}) copy-start(bf16[256,768]{1,0:T(8,128)(2,1)} %project_ref.3) | copy-start | bytes 1179652
  2.5 18.7 %copy-start.4 = (bf16[49,2048]{1,0:T(8,128)(2,1)S(1)}, bf16[49,2048]{1,0:T(8,128)(2,1)}, u32[]{:S(2)}) copy-start(bf16[49,2048]{1,0:T(8,128)(2,1)} %constant.17.clone.taps_ref) | copy-start | bytes 602116
  2.6 6.3 %collective-permute-start = (bf16[3,8,256]{2,1,0:T(8,128)(2,1)}, bf16[3,8,256]{2,1,0:T(8,128)(2,1)S(1)}, u32[]{:S(2)}, u32[]{:S(2)}) collective-permute-start(bf16[3,8,256]{2,1,0:T(8,128)(2,1)} %get-tuple-element.24), channel_id=1, source_target_pairs={{0,64},{64,0},{128,192},{192,128},{1,65},{65,1},{129,193},{193,129... | collective-permute-start | bytes 36872 | tf_op jit(solution)/shard_map/ppermute | solution.py:336
  5.9 5.5 %collective-permute-start.1 = (bf16[3,8,256]{2,1,0:T(8,128)(2,1)}, bf16[3,8,256]{2,1,0:T(8,128)(2,1)S(1)}, u32[]{:S(2)}, u32[]{:S(2)}) collective-permute-start(bf16[3,8,256]{2,1,0:T(8,128)(2,1)} %get-tuple-element.25), channel_id=1, source_target_pairs={{64,128},{128,64},{65,129},{129,65},{66,130},{130,66},{67,131},{13... | collective-permute-start | bytes 36872 | tf_op jit(solution)/shard_map/ppermute | solution.py:336
  7.8 16.3 %collective-permute-start.4 = (bf16[256,256]{1,0:T(8,128)(2,1)}, bf16[256,256]{1,0:T(8,128)(2,1)S(1)}, u32[]{:S(2)}, u32[]{:S(2)}) collective-permute-start(bf16[256,256]{1,0:T(8,128)(2,1)} %get-tuple-element.32.half_ref), channel_id=1, source_target_pairs={{0,1},{1,0},{2,3},{3,2},{4,5},{5,4},{6,7},{7,6},{8,9},{9,8},{10,11... | collective-permute-start | bytes 393224 | tf_op jit(solution)/shard_map/ppermute | solution.py:340
  12.2 9.0 %copy-start.1 = (bf16[16,8,256]{2,1,0:T(8,128)(2,1)S(1)}, bf16[16,8,256]{2,1,0:T(8,128)(2,1)}, u32[]{:S(2)}) copy-start(bf16[16,8,256]{2,1,0:T(8,128)(2,1)} %own_ref.1) | copy-start | bytes 196612
  12.3 9.0 %copy-start.8 = (bf16[16,8,256]{2,1,0:T(8,128)(2,1)S(1)}, bf16[16,8,256]{2,1,0:T(8,128)(2,1)}, u32[]{:S(2)}) copy-start(bf16[16,8,256]{2,1,0:T(8,128)(2,1)} %cot_ref.1) | copy-start | bytes 196612
  12.3 9.0 %copy-start.9 = (f32[1,2048]{1,0:T(1,128)S(1)}, f32[1,2048]{1,0:T(1,128)}, u32[]{:S(2)}) copy-start(f32[1,2048]{1,0:T(1,128)} %constant.18.clone.outside_ref) | copy-start | bytes 24580
  12.3 9.0 %copy-start.11 = (s32[1,1,16,8,1]{2,4,3,1,0:T(1,128)S(1)}, s32[1,1,16,8,1]{2,4,3,1,0:T(1,128)}, u32[]{:S(2)}) copy-start(s32[1,1,16,8,1]{2,4,3,1,0:T(1,128)} %param.16) | copy-start | bytes 1540
  12.3 9.0 %copy-start.13 = (f32[256]{0:T(256)S(1)}, f32[256]{0:T(256)}, u32[]{:S(2)}) copy-start(f32[256]{0:T(256)} %param.18) | copy-start | bytes 3076
  12.4 8.9 %copy-start.10 = (f32[8,49]{1,0:T(8,128)S(1)}, f32[8,49]{1,0:T(8,128)}, u32[]{:S(2)}) copy-start(f32[8,49]{1,0:T(8,128)} %pos_ref.1) | copy-start | bytes 4708
  12.4 8.9 %copy-start.7 = (s32[16,8]{0,1:T(8,128)S(1)}, s32[16,8]{0,1:T(8,128)}, u32[]{:S(2)}) copy-start(s32[16,8]{0,1:T(8,128)} %param.15) | copy-start | bytes 1540
  12.4 10.4 %collective-permute-start.3 = (bf16[22,4,256]{2,1,0:T(4,128)(2,1)S(1)}, bf16[22,4,256]{2,1,0:T(4,128)(2,1)S(1)}, u32[]{:S(2)}, u32[]{:S(2)}) collective-permute-start(bf16[22,4,256]{2,1,0:T(4,128)(2,1)S(1)} %get-tuple-element.50), channel_id=1, source_target_pairs={{1,2},{2,1},{3,4},{4,3},{5,6},{6,5},{7,8},{8,7},{9,10},{10,9},{11,... | collective-permute-start | bytes 135176 | tf_op jit(solution)/shard_map/ppermute | solution.py:336
  21.2 2.9 %collective-permute-start.2 = (bf16[22,4,256]{2,1,0:T(4,128)(2,1)S(1)}, bf16[22,4,256]{2,1,0:T(4,128)(2,1)S(1)}, u32[]{:S(2)}, u32[]{:S(2)}) collective-permute-start(bf16[22,4,256]{2,1,0:T(4,128)(2,1)S(1)} %get-tuple-element.51), channel_id=1, source_target_pairs={{0,1},{1,0},{2,3},{3,2},{4,5},{5,4},{6,7},{7,6},{8,9},{9,8},{10,11... | collective-permute-start | bytes 135176 | tf_op jit(solution)/shard_map/ppermute | solution.py:336
  21.2 0.7 copy-start.12
  21.9 2.2 %copy-start.5 = (bf16[256,256]{1,0:T(8,128)(2,1)S(1)}, bf16[256,256]{1,0:T(8,128)(2,1)}, u32[]{:S(2)}) copy-start(bf16[256,256]{1,0:T(8,128)(2,1)} %out_ref.1) | copy-start | bytes 393220
  21.9 2.2 %copy-start.6 = (bf16[256,256]{1,0:T(8,128)(2,1)S(1)}, bf16[256,256]{1,0:T(8,128)(2,1)}, u32[]{:S(2)}) copy-start(bf16[256,256]{1,0:T(8,128)(2,1)} %get-tuple-element.32.half_ref) | copy-start | bytes 393220
  27.5 12.4 %collective-permute-start.5 = (bf16[2,256,256]{2,1,0:T(8,128)(2,1)S(1)}, bf16[2,256,256]{2,1,0:T(8,128)(2,1)S(1)}, u32[]{:S(2)}, u32[]{:S(2)}) collective-permute-start(bf16[2,256,256]{2,1,0:T(8,128)(2,1)S(1)} %get-tuple-element.34), channel_id=1, source_target_pairs={{0,2},{1,3},{2,0},{3,1},{4,6},{5,7},{6,4},{7,5},{8,10},{9,11},{10,... | collective-permute-start | bytes 786440 | tf_op jit(solution)/shard_map/ppermute | solution.py:340
  27.5 14.2 %copy-start.2 = (bf16[256,256]{1,0:T(8,128)(2,1)S(1)}, bf16[256,256]{1,0:T(8,128)(2,1)}, u32[]{:S(2)}) copy-start(bf16[256,256]{1,0:T(8,128)(2,1)} %up_ref.1) | copy-start | bytes 393220
  27.5 14.2 %copy-start.3 = (bf16[256,256]{1,0:T(8,128)(2,1)S(1)}, bf16[256,256]{1,0:T(8,128)(2,1)}, u32[]{:S(2)}) copy-start(bf16[256,256]{1,0:T(8,128)(2,1)} %down_ref.1) | copy-start | bytes 393220
  27.5 14.2 %all-to-all-start = ((bf16[16,16,512]{2,1,0:T(8,128)(2,1)}), bf16[16,16,512]{2,1,0:T(8,128)(2,1)S(1)}, u32[]{:S(2)}, u32[]{:S(2)}) async-start(bf16[16,16,512]{2,1,0:T(8,128)(2,1)} %bitcast.5), calls=%async_computation | async-start | bytes 524288 | tf_op jit(solution)/shard_map/all_to_all | solution.py:356
  39.9 1.8 %collective-permute-start.7 = (bf16[2,256,256]{2,1,0:T(8,128)(2,1)S(1)}, bf16[2,256,256]{2,1,0:T(8,128)(2,1)S(1)}, u32[]{:S(2)}, u32[]{:S(2)}) collective-permute-start(bf16[2,256,256]{2,1,0:T(8,128)(2,1)S(1)} %collective-permute-done.5.mine2_ref), channel_id=1, source_target_pairs={{0,64},{64,0},{128,192},{192,128},{1,65},{65,1},{129,193},{193,129... | collective-permute-start | bytes 786440 | tf_op jit(solution)/shard_map/ppermute | solution.py:340
  40.4 1.3 %collective-permute-start.6 = (bf16[256,256]{1,0:T(8,128)(2,1)S(1)}, bf16[256,256]{1,0:T(8,128)(2,1)S(1)}, u32[]{:S(2)}, u32[]{:S(2)}) collective-permute-start(bf16[256,256]{1,0:T(8,128)(2,1)S(1)} %collective-permute-done.4.near_ref.mine1_ref), channel_id=1, source_target_pairs={{0,64},{64,0},{128,192},{192,128},{1,65},{65,1},{129,193},{193,129... | collective-permute-start | bytes 393224 | tf_op jit(solution)/shard_map/ppermute | solution.py:340
  43.9 6.2 %collective-permute-start.8 = (bf16[2,4,2,64,256]{4,3,2,1,0:T(8,128)(2,1)S(1)}, bf16[2,4,2,64,256]{4,3,2,1,0:T(8,128)(2,1)S(1)}, u32[]{:S(2)}, u32[]{:S(2)}) collective-permute-start(bf16[2,4,2,64,256]{4,3,2,1,0:T(8,128)(2,1)S(1)} %get-tuple-element.37), channel_id=1, source_target_pairs={{0,64},{64,0},{128,192},{192,128},{1,65},{65,1},{129,193},{193,129... | collective-permute-start | bytes 1572872 | tf_op jit(solution)/shard_map/ppermute | solution.py:340
  50.1 7.6 %collective-permute-start.9 = (bf16[4,2,64,256]{3,2,1,0:T(8,128)(2,1)S(1)}, bf16[4,2,64,256]{3,2,1,0:T(8,128)(2,1)S(1)}, u32[]{:S(2)}, u32[]{:S(2)}) collective-permute-start(bf16[4,2,64,256]{3,2,1,0:T(8,128)(2,1)S(1)} %fusion), channel_id=1, source_target_pairs={{0,128},{64,192},{128,0},{192,64},{1,129},{65,193},{129,1},{193,65... | collective-permute-start | bytes 786440 | tf_op jit(solution)/shard_map/ppermute | solution.py:340
  50.2 13.6 %all-to-all-start.1 = ((bf16[16,16,256]{2,1,0:T(8,128)(2,1)}), bf16[16,16,256]{2,1,0:T(8,128)(2,1)S(1)}, u32[]{:S(2)}, u32[]{:S(2)}) async-start(bf16[16,16,256]{2,1,0:T(8,128)(2,1)} %bitcast.8), calls=%async_computation.1 | async-start | bytes 262144 | tf_op jit(solution)/shard_map/all_to_all | solution.py:356
  57.9 6.0 %collective-permute-start.12 = (bf16[2,64,256]{2,1,0:T(8,128)(2,1)S(1)}, bf16[2,64,256]{2,1,0:T(8,128)(2,1)S(1)}, u32[]{:S(2)}, u32[]{:S(2)}) collective-permute-start(bf16[2,64,256]{2,1,0:T(8,128)(2,1)S(1)} %get-tuple-element.47), channel_id=1, source_target_pairs={{0,3},{1,2},{2,1},{3,0},{4,7},{5,6},{6,5},{7,4},{8,11},{9,10},{10,... | collective-permute-start | bytes 196616 | tf_op jit(solution)/shard_map/ppermute | solution.py:340
  58.0 9.0 %collective-permute-start.11 = (bf16[2,64,256]{2,1,0:T(8,128)(2,1)S(1)}, bf16[2,64,256]{2,1,0:T(8,128)(2,1)S(1)}, u32[]{:S(2)}, u32[]{:S(2)}) collective-permute-start(bf16[2,64,256]{2,1,0:T(8,128)(2,1)S(1)} %get-tuple-element.48), channel_id=1, source_target_pairs={{0,2},{1,3},{2,0},{3,1},{4,6},{5,7},{6,4},{7,5},{8,10},{9,11},{10,... | collective-permute-start | bytes 196616 | tf_op jit(solution)/shard_map/ppermute | solution.py:340
  62.6 4.3 %collective-permute-start.10 = (bf16[2,64,256]{2,1,0:T(8,128)(2,1)S(1)}, bf16[2,64,256]{2,1,0:T(8,128)(2,1)S(1)}, u32[]{:S(2)}, u32[]{:S(2)}) collective-permute-start(bf16[2,64,256]{2,1,0:T(8,128)(2,1)S(1)} %get-tuple-element.49), channel_id=1, source_target_pairs={{0,1},{1,0},{2,3},{3,2},{4,5},{5,4},{6,7},{7,6},{8,9},{9,8},{10,11... | collective-permute-start | bytes 196616 | tf_op jit(solution)/shard_map/ppermute | solution.py:340
  67.8 3.7 %collective-permute-start.15 = (bf16[2,64,256]{2,1,0:T(8,128)(2,1)S(1)}, bf16[2,64,256]{2,1,0:T(8,128)(2,1)S(1)}, u32[]{:S(2)}, u32[]{:S(2)}) collective-permute-start(bf16[2,64,256]{2,1,0:T(8,128)(2,1)S(1)} %get-tuple-element.42.own_ref), channel_id=1, source_target_pairs={{0,192},{64,128},{128,64},{192,0},{1,193},{65,129},{129,65},{193,1... | collective-permute-start | bytes 196616 | tf_op jit(solution)/shard_map/ppermute | solution.py:340
  69.6 4.9 %collective-permute-start.14 = (bf16[2,64,256]{2,1,0:T(8,128)(2,1)S(1)}, bf16[2,64,256]{2,1,0:T(8,128)(2,1)S(1)}, u32[]{:S(2)}, u32[]{:S(2)}) collective-permute-start(bf16[2,64,256]{2,1,0:T(8,128)(2,1)S(1)} %get-tuple-element.42.own_ref), channel_id=1, source_target_pairs={{0,128},{64,192},{128,0},{192,64},{1,129},{65,193},{129,1},{193,65... | collective-permute-start | bytes 196616 | tf_op jit(solution)/shard_map/ppermute | solution.py:340
  71.2 3.2 %collective-permute-start.13 = (bf16[2,64,256]{2,1,0:T(8,128)(2,1)S(1)}, bf16[2,64,256]{2,1,0:T(8,128)(2,1)S(1)}, u32[]{:S(2)}, u32[]{:S(2)}) collective-permute-start(bf16[2,64,256]{2,1,0:T(8,128)(2,1)S(1)} %get-tuple-element.42.own_ref), channel_id=1, source_target_pairs={{0,64},{64,0},{128,192},{192,128},{1,65},{65,1},{129,193},{193,129... | collective-permute-start | bytes 196616 | tf_op jit(solution)/shard_map/ppermute | solution.py:340

commit v3 on v2

--- a/solution.py
+++ b/solution.py
@@ -67,15 +67,19 @@
     return jnp.concatenate([table[:, i : i + 1] for i in range(ROWS)], axis=0)
 
 
-def mark_kernel(state_ref, land_ref, up_ref, down_ref, marked_ref, even_ref, odd_ref, half_ref):
+def mark_kernel(state_ref, land_ref, marked_ref, even_ref, odd_ref):
     even = lax.axis_index("lat") & 1 == 0
     land = column(land_ref[...]).reshape(ROWS, COLS, 1)
-    marked = jnp.where(land > 0, state_ref[...].astype(F32), LAND).astype(BF)
+    state = state_ref[...].astype(F32).reshape(ROWS, COLS, D)
+    marked = jnp.where(land > 0, state, LAND).astype(BF)
     marked_ref[...] = marked
     top, bottom = marked[:REACH], marked[ROWS - REACH :]
     even_ref[...] = jnp.where(even, bottom, top)
     odd_ref[...] = jnp.where(even, top, bottom)
-    half_ref[...] = jnp.where(even, up_ref[...], down_ref[...])
+
+
+def half_kernel(up_ref, down_ref, half_ref):
+    half_ref[...] = jnp.where(lax.axis_index("lat") & 1 == 0, up_ref[...], down_ref[...])
 
 
 def prepare_kernel(
@@ -255,22 +259,27 @@
     first_core = lat & 1 == 0
     inputs = got_ref[:, 0:D]
     tangents = got_ref[:, D : 2 * D]
-    outputs = jnp.zeros((SLOTS, D), F32)
+    ups, downs = [up_ref[...]], [down_ref[...]]
+    for mine, other in (
+        (mine1_ref[...], other1_ref[...]),
+        (mine2_ref[0], other2_ref[0]),
+        (mine2_ref[1], other2_ref[1]),
+    ):
+        ups.append(jnp.where(first_core, mine, other))
+        downs.append(jnp.where(first_core, other, mine))
+    hidden = [dot(inputs, up) for up in ups]
+    back = [dot_t(tangents, down) for down in downs]
+    active, pre_act = [], []
     for member in range(4):
-        if member:
-            mine = mine1_ref[...] if member == 1 else mine2_ref[member - 2]
-            other = other1_ref[...] if member == 1 else other2_ref[member - 2]
-            up = jnp.where(first_core, mine, other)
-            down = jnp.where(first_core, other, mine)
-        else:
-            up = up_ref[...]
-            down = down_ref[...]
-        active, slope = gelu_parts(dot(inputs, up))
-        active = active.astype(BF)
-        outputs = outputs + dot(active, down)
-        pre_act = (dot_t(tangents, down) * slope).astype(BF)
-        grad_ref[member, 0] = t_dot(inputs, pre_act)
-        grad_ref[member, 1] = t_dot(active, tangents)
+        value, slope = gelu_parts(hidden[member])
+        active.append(value.astype(BF))
+        pre_act.append((back[member] * slope).astype(BF))
+    for member in range(4):
+        grad_ref[member, 0] = t_dot(inputs, pre_act[member])
+        grad_ref[member, 1] = t_dot(active[member], tangents)
+    outputs = dot(active[0], downs[0])
+    for member in range(1, 4):
+        outputs = outputs + dot(active[member], downs[member])
     outputs_ref[...] = outputs.astype(BF)
     for far in range(2):
         for other in range(2):
@@ -372,12 +381,13 @@
     down_weight,
 ):
     land = land_sea.T
-    marked, even, odd, half = call(
+    marked, even, odd = call(
         mark_kernel,
-        [((ROWS, COLS, D), BF), ((REACH, COLS, D), BF), ((REACH, COLS, D), BF), ((D, UNITS), BF)],
-        (state, land, up_weight, down_weight),
-        fetch=4,
-    )
+        [((ROWS, COLS, D), BF), ((REACH, COLS, D), BF), ((REACH, COLS, D), BF)],
+        (state.reshape(CELLS, D), land),
+        fetch=2,
+    )
+    (half,) = call(half_kernel, [((D, UNITS), BF)], (up_weight, down_weight), fetch=2)
     lat_even = pair_up(even, "lat", 0, False)
     lat_odd = pair_up(odd, "lat", 1, False)
     at_even = lax.axis_index("lat") & 1 == 0

time: 75.6 us -> 75.1 us (level)
  Pallas kernels: 9.94 us -> 11.3 us
  starting transfers between devices: 37.6 us -> 36.3 us
  other arithmetic: 1.1 us -> 0.26 us
    ppermute x12, waiting for transfers between devices: 20.3 us -> 23.3 us  [swap(): lax.ppermute(value, axis, [(i, i ^ mask) for i in range(lax.axis_size(axi...]
    ppermute x4, waiting for transfers between devices: 3.78 us -> 1.8 us  [pair_up(): return lax.ppermute(value, axis, pairs)]
    pallas_call x6 -> x7, Pallas kernels: 9.94 us -> 11.3 us  [call(): pl.pallas_call(fetching if fetch else kernel, out_shape=[jax.ShapeDtypeSt...]
    ppermute x12, starting transfers between devices: 14.7 us -> 13.5 us  [swap(): lax.ppermute(value, axis, [(i, i ^ mask) for i in range(lax.axis_size(axi...]
    all_to_all x2, waiting for transfers between devices: 1.02 us -> 0.01 us  [exchange(): lax.all_to_all(value, ('lat', 'lon'), 0, 0, axis_index_groups=expert_grou...]
    concatenate x1, other arithmetic: 0.85 us -> 0.01 us  [on_device(): tall = jnp.concatenate([up, marked, down], axis=0)]
  transfers between devices with their start and end apart: 18 -> 18, of which waited for: 10 -> 10; matrix products, arithmetic and copies ran while one was open for 1% -> 0% of each run, Pallas kernels for 1% -> 3%
where the time goes in v3:
time: 75.1 us; the launch traced here: 74.7 us
  starting transfers between devices  36.3 us (48%)
  waiting for transfers between devices  25.1 us (33%)
  Pallas kernels  11.3 us (15%)
  between operations  0.91 us (1%)
    ppermute x12, waiting for transfers between devices, swap(): lax.ppermute(value, axis, [(i, i ^ mask) for i in range(lax.axis_size(axi...  23.3 us
    ppermute x4, starting transfers between devices, pair_up(): return lax.ppermute(value, axis, pairs)  14.2 us
    ppermute x12, starting transfers between devices, swap(): lax.ppermute(value, axis, [(i, i ^ mask) for i in range(lax.axis_size(axi...  13.5 us
    pallas_call x7, Pallas kernels, call(): pl.pallas_call(fetching if fetch else kernel, out_shape=[jax.ShapeDtypeSt...  11.3 us
    all_to_all x2, starting transfers between devices, exchange(): lax.all_to_all(value, ('lat', 'lon'), 0, 0, axis_index_groups=expert_grou...  8.61 us
    ppermute x4, waiting for transfers between devices, pair_up(): return lax.ppermute(value, axis, pairs)  1.8 us
  transfers between devices with their start and end apart: 18, of which 10 were waited for; matrix products, arithmetic and copies ran while one was open for 0% of the time, Pallas kernels for 3%

profile of v3, /device:TPU:1, one launch (start us, length us, event | category | flops | bytes accessed | tf_op | source)
XLA Modules:
  0.0 74.7 jit_solution(9701713179351341498)
XLA Ops:
  0.6 1.6 %shard_map.148 = (bf16[16,8,256]{2,1,0:T(8,128)(2,1)}, bf16[3,8,256]{2,1,0:T(8,128)(2,1)}, bf16[3,8,256]{2,1,0:T(8,128)(2,1)}) custom-call(bf16[128,256]{1,0:T(8,128)(2,1)} %bitcast.25, s32[8,16]{1,0:T(8,128)} %bitcast.27), custom_call_target="tpu_custom_call" | custom-call | tf_op jit(solution)/shard_map/pallas_call | solution.py:330
  2.3 0.0 copy-start.14
  2.3 3.3 %collective-permute-start = (bf16[3,8,256]{2,1,0:T(8,128)(2,1)}, bf16[3,8,256]{2,1,0:T(8,128)(2,1)S(1)}, u32[]{:S(2)}, u32[]{:S(2)}) collective-permute-start(bf16[3,8,256]{2,1,0:T(8,128)(2,1)} %get-tuple-element.23), channel_id=1, source_target_pairs={{0,64},{64,0},{128,192},{192,128},{1,65},{65,1},{129,193},{193,129... | collective-permute-start | bytes 36872 | tf_op jit(solution)/shard_map/ppermute | solution.py:345
  5.6 2.0 %collective-permute-start.1 = (bf16[3,8,256]{2,1,0:T(8,128)(2,1)}, bf16[3,8,256]{2,1,0:T(8,128)(2,1)S(1)}, u32[]{:S(2)}, u32[]{:S(2)}) collective-permute-start(bf16[3,8,256]{2,1,0:T(8,128)(2,1)} %get-tuple-element.24), channel_id=1, source_target_pairs={{64,128},{128,64},{65,129},{129,65},{66,130},{130,66},{67,131},{13... | collective-permute-start | bytes 36872 | tf_op jit(solution)/shard_map/ppermute | solution.py:345
  7.7 1.7 %shard_map.150.half_ref = bf16[256,256]{1,0:T(8,128)(2,1)} custom-call(bf16[256,256]{1,0:T(8,128)(2,1)} %up_ref.1, bf16[256,256]{1,0:T(8,128)(2,1)} %down_ref.1), custom_call_target="tpu_custom_call" | custom-call | tf_op jit(solution)/shard_map/pallas_call | solution.py:330
  9.3 0.0 copy-start.5
  9.4 1.1 %collective-permute-start.4 = (bf16[256,256]{1,0:T(8,128)(2,1)}, bf16[256,256]{1,0:T(8,128)(2,1)S(1)}, u32[]{:S(2)}, u32[]{:S(2)}) collective-permute-start(bf16[256,256]{1,0:T(8,128)(2,1)} %shard_map.150.half_ref), channel_id=1, source_target_pairs={{0,1},{1,0},{2,3},{3,2},{4,5},{5,4},{6,7},{7,6},{8,9},{9,8},{10,11... | collective-permute-start | bytes 393224 | tf_op jit(solution)/shard_map/ppermute | solution.py:349
  10.5 0.0 collective-permute-done.lat_even_ref
  10.5 0.5 collective-permute-done.1.lat_odd_ref
  11.0 0.0 copy-done.14
  11.0 0.0 copy-start.1
  11.0 0.0 copy-start.8
  11.0 0.0 copy-start.9
  11.0 0.0 copy-start.11
  11.1 0.0 copy-start.13
  11.1 0.1 broadcast_select_fusion
  11.1 0.0 copy-start.10
  11.1 0.0 copy-start.7
  11.2 8.9 %collective-permute-start.3 = (bf16[22,4,256]{2,1,0:T(4,128)(2,1)S(1)}, bf16[22,4,256]{2,1,0:T(4,128)(2,1)S(1)}, u32[]{:S(2)}, u32[]{:S(2)}) collective-permute-start(bf16[22,4,256]{2,1,0:T(4,128)(2,1)S(1)} %get-tuple-element.48), channel_id=1, source_target_pairs={{1,2},{2,1},{3,4},{4,3},{5,6},{6,5},{7,8},{8,7},{9,10},{10,9},{11,... | collective-permute-start | bytes 135176 | tf_op jit(solution)/shard_map/ppermute | solution.py:345
  20.0 0.0 collective-permute-start.2
  20.0 0.0 copy-done
  20.0 0.0 copy-done.5
  20.0 0.0 copy-done.1
  20.1 0.0 copy-done.8
  20.1 0.0 copy-done.9
  20.1 0.0 copy-done.11
  20.1 0.6 copy-done.12
  20.7 0.9 %shard_map.149 = (f32[128,128]{1,0:T(8,128)S(1)}, bf16[128,256]{1,0:T(8,128)(2,1)S(1)}, bf16[256,256]{1,0:T(8,128)(2,1)S(1)}, bf16[128,768]{1,0:T(8,128)(2,1)S(1)}, f32[2,256]{1,0:T(2,128)S(1)}) custom-call(f32[8,49]{1,0:T(8,128)S(1)} %copy-done.10, bf16[49,2048]{1,0:T(8,128)(2,1)S(1)} %copy-done.5, f32[1,2048]{1,0:T(1,128)S(1)} %copy-done.9, ...), custom_call_target="tpu_custom_call" | custom-call | tf_op jit(solution)/shard_map/pallas_call | solution.py:330
  21.6 0.0 collective-permute-done.3.lon_odd_ref
  21.6 1.3 %collective-permute-done.2.lon_even_ref = bf16[22,4,256]{2,1,0:T(4,128)(2,1)S(1)} collective-permute-done((bf16[22,4,256]{2,1,0:T(4,128)(2,1)S(1)}, bf16[22,4,256]{2,1,0:T(4,128)(2,1)S(1)}, u32[]{:S(2)}, u32[]{:S(2)}) %collective-permute-start.2) | collective-permute-done | bytes 45088 | tf_op jit(solution)/shard_map/ppermute | solution.py:345
  22.9 0.0 collective-permute-done.4.near_ref.mine1_ref
  22.9 0.0 copy-done.4
  22.9 3.4 %shard_map.151 = (bf16[128,256]{1,0:T(8,128)(2,1)S(1)}, bf16[256,512]{1,0:T(8,128)(2,1)}, bf16[2,256,256]{2,1,0:T(8,128)(2,1)S(1)}) custom-call(bf16[16,8,256]{2,1,0:T(8,128)(2,1)S(1)} %copy-done.1, bf16[3,8,256]{2,1,0:T(8,128)(2,1)S(1)} %collective-permute-done.lat_even_ref, bf16[3,8,256]{2,1,0:T(8,128)(2,1)S(1)} %collective-permute-done.1.lat_odd_ref, ...), custom_call_target="tpu_custom_call" | custom-call | tf_op jit(solution)/shard_map/pallas_call | solution.py:330
  26.3 0.0 collective-permute-start.5
  26.3 4.9 %all-to-all-start = ((bf16[16,16,512]{2,1,0:T(8,128)(2,1)}), bf16[16,16,512]{2,1,0:T(8,128)(2,1)S(1)}, u32[]{:S(2)}, u32[]{:S(2)}) async-start(bf16[16,16,512]{2,1,0:T(8,128)(2,1)} %bitcast.6), calls=%async_computation | async-start | bytes 524288 | tf_op jit(solution)/shard_map/all_to_all | solution.py:365
  31.2 9.5 %collective-permute-done.5.mine2_ref = bf16[2,256,256]{2,1,0:T(8,128)(2,1)S(1)} collective-permute-done((bf16[2,256,256]{2,1,0:T(8,128)(2,1)S(1)}, bf16[2,256,256]{2,1,0:T(8,128)(2,1)S(1)}, u32[]{:S(2)}, u32[]{:S(2)}) %collective-permute-start.5) | collective-permute-done | bytes 262176 | tf_op jit(solution)/shard_map/ppermute | solution.py:349
  40.7 0.5 collective-permute-start.7
  41.2 0.0 collective-permute-start.6
  41.3 1.3 %collective-permute-done.6.other1_ref = bf16[256,256]{1,0:T(8,128)(2,1)S(1)} collective-permute-done((bf16[256,256]{1,0:T(8,128)(2,1)S(1)}, bf16[256,256]{1,0:T(8,128)(2,1)S(1)}, u32[]{:S(2)}, u32[]{:S(2)}) %collective-permute-start.6) | collective-permute-done | bytes 131104 | tf_op jit(solution)/shard_map/ppermute | solution.py:349
  42.6 0.0 all-to-all-done
  42.6 0.0 collective-permute-done.7.other2_ref
  42.6 2.1 %shard_map.152 = (bf16[256,256]{1,0:T(8,128)(2,1)}, f32[2,4,2,64,256]{4,3,2,1,0:T(8,128)S(1)}, bf16[2,4,2,64,256]{4,3,2,1,0:T(8,128)(2,1)S(1)}) custom-call(bf16[256,512]{1,0:T(8,128)(2,1)S(1)} %bitcast.24, bf16[256,256]{1,0:T(8,128)(2,1)S(1)} %copy-done.2, bf16[256,256]{1,0:T(8,128)(2,1)S(1)} %copy-done.3, ...), custom_call_target="tpu_custom_call" | custom-call | tf_op jit(solution)/shard_map/pallas_call | solution.py:330
  44.7 3.3 %collective-permute-start.8 = (bf16[2,4,2,64,256]{4,3,2,1,0:T(8,128)(2,1)S(1)}, bf16[2,4,2,64,256]{4,3,2,1,0:T(8,128)(2,1)S(1)}, u32[]{:S(2)}, u32[]{:S(2)}) collective-permute-start(bf16[2,4,2,64,256]{4,3,2,1,0:T(8,128)(2,1)S(1)} %get-tuple-element.35), channel_id=1, source_target_pairs={{0,64},{64,0},{128,192},{192,128},{1,65},{65,1},{129,193},{193,129... | collective-permute-start | bytes 1572872 | tf_op jit(solution)/shard_map/ppermute | solution.py:349
  47.9 1.5 %collective-permute-done.8 = bf16[2,4,2,64,256]{4,3,2,1,0:T(8,128)(2,1)S(1)} collective-permute-done((bf16[2,4,2,64,256]{4,3,2,1,0:T(8,128)(2,1)S(1)}, bf16[2,4,2,64,256]{4,3,2,1,0:T(8,128)(2,1)S(1)}, u32[]{:S(2)}, u32[]{:S(2)}) %collective-permute-start.8) | collective-permute-done | bytes 524320 | tf_op jit(solution)/shard_map/ppermute | solution.py:349
  49.5 0.1 fusion
  49.5 0.1 collective-permute-start.9
  49.6 3.7 %all-to-all-start.1 = ((bf16[16,16,256]{2,1,0:T(8,128)(2,1)}), bf16[16,16,256]{2,1,0:T(8,128)(2,1)S(1)}, u32[]{:S(2)}, u32[]{:S(2)}) async-start(bf16[16,16,256]{2,1,0:T(8,128)(2,1)} %bitcast.9), calls=%async_computation.1 | async-start | bytes 262144 | tf_op jit(solution)/shard_map/all_to_all | solution.py:365
  53.4 3.8 %collective-permute-done.9 = bf16[4,2,64,256]{3,2,1,0:T(8,128)(2,1)S(1)} collective-permute-done((bf16[4,2,64,256]{3,2,1,0:T(8,128)(2,1)S(1)}, bf16[4,2,64,256]{3,2,1,0:T(8,128)(2,1)S(1)}, u32[]{:S(2)}, u32[]{:S(2)}) %collective-permute-start.9) | collective-permute-done | bytes 262176 | tf_op jit(solution)/shard_map/ppermute | solution.py:349
  57.2 0.1 fusion.1
  57.3 0.1 collective-permute-start.12
  57.4 4.6 %collective-permute-start.11 = (bf16[2,64,256]{2,1,0:T(8,128)(2,1)S(1)}, bf16[2,64,256]{2,1,0:T(8,128)(2,1)S(1)}, u32[]{:S(2)}, u32[]{:S(2)}) collective-permute-start(bf16[2,64,256]{2,1,0:T(8,128)(2,1)S(1)} %get-tuple-element.46), channel_id=1, source_target_pairs={{0,2},{1,3},{2,0},{3,1},{4,6},{5,7},{6,4},{7,5},{8,10},{9,11},{10,... | collective-permute-start | bytes 196616 | tf_op jit(solution)/shard_map/ppermute | solution.py:349
  62.0 0.2 collective-permute-start.10
  62.2 0.0 all-to-all-done.1
  62.2 0.3 collective-permute-done.12.c_ref
  62.6 3.7 %collective-permute-done.11.b_ref = bf16[2,64,256]{2,1,0:T(8,128)(2,1)S(1)} collective-permute-done((bf16[2,64,256]{2,1,0:T(8,128)(2,1)S(1)}, bf16[2,64,256]{2,1,0:T(8,128)(2,1)S(1)}, u32[]{:S(2)}, u32[]{:S(2)}) %collective-permute-start.11) | collective-permute-done | bytes 65568 | tf_op jit(solution)/shard_map/ppermute | solution.py:349
  66.2 0.0 collective-permute-done.10.a_ref
  66.2 0.8 %shard_map.153 = (bf16[16,8,256]{2,1,0:T(8,128)(2,1)}, bf16[2,64,256]{2,1,0:T(8,128)(2,1)S(1)}) custom-call(bf16[256,256]{1,0:T(8,128)(2,1)S(1)} %bitcast.26, bf16[128,256]{1,0:T(8,128)(2,1)S(1)} %get-tuple-element.29.place_ref, bf16[128,256]{1,0:T(8,128)(2,1)S(1)} %get-tuple-element.37.residual_ref, s32[8,16]{1,0:T(8,128)S(1)} %bitcast.30, ...), custom_call_target="tpu_custom_call" | custom-call | tf_op jit(solution)/shard_map/pallas_call | solution.py:330
  67.0 1.9 %collective-permute-start.15 = (bf16[2,64,256]{2,1,0:T(8,128)(2,1)S(1)}, bf16[2,64,256]{2,1,0:T(8,128)(2,1)S(1)}, u32[]{:S(2)}, u32[]{:S(2)}) collective-permute-start(bf16[2,64,256]{2,1,0:T(8,128)(2,1)S(1)} %get-tuple-element.40.own_ref), channel_id=1, source_target_pairs={{0,192},{64,128},{128,64},{192,0},{1,193},{65,129},{129,65},{193,1... | collective-permute-start | bytes 196616 | tf_op jit(solution)/shard_map/ppermute | solution.py:349
  69.0 1.7 %collective-permute-start.14 = (bf16[2,64,256]{2,1,0:T(8,128)(2,1)S(1)}, bf16[2,64,256]{2,1,0:T(8,128)(2,1)S(1)}, u32[]{:S(2)}, u32[]{:S(2)}) collective-permute-start(bf16[2,64,256]{2,1,0:T(8,128)(2,1)S(1)} %get-tuple-element.40.own_ref), channel_id=1, source_target_pairs={{0,128},{64,192},{128,0},{192,64},{1,129},{65,193},{129,1},{193,65... | collective-permute-start | bytes 196616 | tf_op jit(solution)/shard_map/ppermute | solution.py:349
  70.6 0.0 collective-permute-start.13
  70.6 0.3 collective-permute-done.15.c_ref
  70.9 2.9 %collective-permute-done.14.b_ref = bf16[2,64,256]{2,1,0:T(8,128)(2,1)S(1)} collective-permute-done((bf16[2,64,256]{2,1,0:T(8,128)(2,1)S(1)}, bf16[2,64,256]{2,1,0:T(8,128)(2,1)S(1)}, u32[]{:S(2)}, u32[]{:S(2)}) %collective-permute-start.14) | collective-permute-done | bytes 65568 | tf_op jit(solution)/shard_map/ppermute | solution.py:349
  73.8 0.0 collective-permute-done.13.a_ref
  73.8 0.8 %shard_map.154 = (f32[256,256]{1,0:T(8,128)}, f32[256,256]{1,0:T(8,128)}) custom-call(bf16[2,64,256]{2,1,0:T(8,128)(2,1)S(1)} %get-tuple-element.40.own_ref, bf16[2,64,256]{2,1,0:T(8,128)(2,1)S(1)} %collective-permute-done.13.a_ref, bf16[2,64,256]{2,1,0:T(8,128)(2,1)S(1)} %collective-permute-done.14.b_ref, bf16[2,64,256]{2,1,0:T(8,128)(2,1)S(1)} %collective-permute-done.15.c_ref), custom_call_target="tpu_custom_call" | custom-call | tf_op jit(solution)/shard_map/pallas_call | solution.py:330
  (16 shorter events, 0.1 us)
Async XLA Ops:
  2.3 8.7 %copy-start.14 = (bf16[16,8,256]{2,1,0:T(8,128)(2,1)S(1)}, bf16[16,8,256]{2,1,0:T(8,128)(2,1)}, u32[]{:S(2)}) copy-start(bf16[16,8,256]{2,1,0:T(8,128)(2,1)} %get-tuple-element.25) | copy-start | bytes 196612
  2.3 8.2 %collective-permute-start = (bf16[3,8,256]{2,1,0:T(8,128)(2,1)}, bf16[3,8,256]{2,1,0:T(8,128)(2,1)S(1)}, u32[]{:S(2)}, u32[]{:S(2)}) collective-permute-start(bf16[3,8,256]{2,1,0:T(8,128)(2,1)} %get-tuple-element.23), channel_id=1, source_target_pairs={{0,64},{64,0},{128,192},{192,128},{1,65},{65,1},{129,193},{193,129... | collective-permute-start | bytes 36872 | tf_op jit(solution)/shard_map/ppermute | solution.py:345
  5.6 14.4 %copy-start = (bf16[256,768]{1,0:T(8,128)(2,1)S(1)}, bf16[256,768]{1,0:T(8,128)(2,1)}, u32[]{:S(2)}) copy-start(bf16[256,768]{1,0:T(8,128)(2,1)} %project_ref.3) | copy-start | bytes 1179652
  5.6 5.3 %collective-permute-start.1 = (bf16[3,8,256]{2,1,0:T(8,128)(2,1)}, bf16[3,8,256]{2,1,0:T(8,128)(2,1)S(1)}, u32[]{:S(2)}, u32[]{:S(2)}) collective-permute-start(bf16[3,8,256]{2,1,0:T(8,128)(2,1)} %get-tuple-element.24), channel_id=1, source_target_pairs={{64,128},{128,64},{65,129},{129,65},{66,130},{130,66},{67,131},{13... | collective-permute-start | bytes 36872 | tf_op jit(solution)/shard_map/ppermute | solution.py:345
  9.3 10.7 %copy-start.5 = (bf16[49,2048]{1,0:T(8,128)(2,1)S(1)}, bf16[49,2048]{1,0:T(8,128)(2,1)}, u32[]{:S(2)}) copy-start(bf16[49,2048]{1,0:T(8,128)(2,1)} %constant.17.clone.taps_ref) | copy-start | bytes 602116
  9.4 13.6 %collective-permute-start.4 = (bf16[256,256]{1,0:T(8,128)(2,1)}, bf16[256,256]{1,0:T(8,128)(2,1)S(1)}, u32[]{:S(2)}, u32[]{:S(2)}) collective-permute-start(bf16[256,256]{1,0:T(8,128)(2,1)} %shard_map.150.half_ref), channel_id=1, source_target_pairs={{0,1},{1,0},{2,3},{3,2},{4,5},{5,4},{6,7},{7,6},{8,9},{9,8},{10,11... | collective-permute-start | bytes 393224 | tf_op jit(solution)/shard_map/ppermute | solution.py:349
  11.0 9.0 %copy-start.1 = (bf16[16,8,256]{2,1,0:T(8,128)(2,1)S(1)}, bf16[16,8,256]{2,1,0:T(8,128)(2,1)}, u32[]{:S(2)}) copy-start(bf16[16,8,256]{2,1,0:T(8,128)(2,1)} %own_ref.1) | copy-start | bytes 196612
  11.0 9.0 %copy-start.8 = (bf16[16,8,256]{2,1,0:T(8,128)(2,1)S(1)}, bf16[16,8,256]{2,1,0:T(8,128)(2,1)}, u32[]{:S(2)}) copy-start(bf16[16,8,256]{2,1,0:T(8,128)(2,1)} %cot_ref.1) | copy-start | bytes 196612
  11.0 9.0 %copy-start.9 = (f32[1,2048]{1,0:T(1,128)S(1)}, f32[1,2048]{1,0:T(1,128)}, u32[]{:S(2)}) copy-start(f32[1,2048]{1,0:T(1,128)} %constant.18.clone.outside_ref) | copy-start | bytes 24580
  11.0 9.0 %copy-start.11 = (s32[1,1,16,8,1]{2,4,3,1,0:T(1,128)S(1)}, s32[1,1,16,8,1]{2,4,3,1,0:T(1,128)}, u32[]{:S(2)}) copy-start(s32[1,1,16,8,1]{2,4,3,1,0:T(1,128)} %param.16) | copy-start | bytes 1540
  11.1 9.0 %copy-start.13 = (f32[256]{0:T(256)S(1)}, f32[256]{0:T(256)}, u32[]{:S(2)}) copy-start(f32[256]{0:T(256)} %param.18) | copy-start | bytes 3076
  11.1 9.0 %copy-start.10 = (f32[8,49]{1,0:T(8,128)S(1)}, f32[8,49]{1,0:T(8,128)}, u32[]{:S(2)}) copy-start(f32[8,49]{1,0:T(8,128)} %pos_ref.1) | copy-start | bytes 4708
  11.1 9.0 %copy-start.7 = (s32[16,8]{0,1:T(8,128)S(1)}, s32[16,8]{0,1:T(8,128)}, u32[]{:S(2)}) copy-start(s32[16,8]{0,1:T(8,128)} %param.15) | copy-start | bytes 1540
  11.2 10.5 %collective-permute-start.3 = (bf16[22,4,256]{2,1,0:T(4,128)(2,1)S(1)}, bf16[22,4,256]{2,1,0:T(4,128)(2,1)S(1)}, u32[]{:S(2)}, u32[]{:S(2)}) collective-permute-start(bf16[22,4,256]{2,1,0:T(4,128)(2,1)S(1)} %get-tuple-element.48), channel_id=1, source_target_pairs={{1,2},{2,1},{3,4},{4,3},{5,6},{6,5},{7,8},{8,7},{9,10},{10,9},{11,... | collective-permute-start | bytes 135176 | tf_op jit(solution)/shard_map/ppermute | solution.py:345
  20.0 2.9 %collective-permute-start.2 = (bf16[22,4,256]{2,1,0:T(4,128)(2,1)S(1)}, bf16[22,4,256]{2,1,0:T(4,128)(2,1)S(1)}, u32[]{:S(2)}, u32[]{:S(2)}) collective-permute-start(bf16[22,4,256]{2,1,0:T(4,128)(2,1)S(1)} %get-tuple-element.49), channel_id=1, source_target_pairs={{0,1},{1,0},{2,3},{3,2},{4,5},{5,4},{6,7},{7,6},{8,9},{9,8},{10,11... | collective-permute-start | bytes 135176 | tf_op jit(solution)/shard_map/ppermute | solution.py:345
  20.0 0.7 copy-start.12
  20.7 2.2 %copy-start.4 = (bf16[256,256]{1,0:T(8,128)(2,1)S(1)}, bf16[256,256]{1,0:T(8,128)(2,1)}, u32[]{:S(2)}) copy-start(bf16[256,256]{1,0:T(8,128)(2,1)} %shard_map.150.half_ref) | copy-start | bytes 393220
  20.7 2.2 %copy-start.6 = (bf16[256,256]{1,0:T(8,128)(2,1)S(1)}, bf16[256,256]{1,0:T(8,128)(2,1)}, u32[]{:S(2)}) copy-start(bf16[256,256]{1,0:T(8,128)(2,1)} %out_ref.1) | copy-start | bytes 393220
  26.3 14.4 %collective-permute-start.5 = (bf16[2,256,256]{2,1,0:T(8,128)(2,1)S(1)}, bf16[2,256,256]{2,1,0:T(8,128)(2,1)S(1)}, u32[]{:S(2)}, u32[]{:S(2)}) collective-permute-start(bf16[2,256,256]{2,1,0:T(8,128)(2,1)S(1)} %get-tuple-element.32), channel_id=1, source_target_pairs={{0,2},{1,3},{2,0},{3,1},{4,6},{5,7},{6,4},{7,5},{8,10},{9,11},{10,... | collective-permute-start | bytes 786440 | tf_op jit(solution)/shard_map/ppermute | solution.py:349
  26.3 16.3 %copy-start.2 = (bf16[256,256]{1,0:T(8,128)(2,1)S(1)}, bf16[256,256]{1,0:T(8,128)(2,1)}, u32[]{:S(2)}) copy-start(bf16[256,256]{1,0:T(8,128)(2,1)} %up_ref.1) | copy-start | bytes 393220
  26.3 16.3 %copy-start.3 = (bf16[256,256]{1,0:T(8,128)(2,1)S(1)}, bf16[256,256]{1,0:T(8,128)(2,1)}, u32[]{:S(2)}) copy-start(bf16[256,256]{1,0:T(8,128)(2,1)} %down_ref.1) | copy-start | bytes 393220
  26.3 16.2 %all-to-all-start = ((bf16[16,16,512]{2,1,0:T(8,128)(2,1)}), bf16[16,16,512]{2,1,0:T(8,128)(2,1)S(1)}, u32[]{:S(2)}, u32[]{:S(2)}) async-start(bf16[16,16,512]{2,1,0:T(8,128)(2,1)} %bitcast.6), calls=%async_computation | async-start | bytes 524288 | tf_op jit(solution)/shard_map/all_to_all | solution.py:365
  40.7 1.8 %collective-permute-start.7 = (bf16[2,256,256]{2,1,0:T(8,128)(2,1)S(1)}, bf16[2,256,256]{2,1,0:T(8,128)(2,1)S(1)}, u32[]{:S(2)}, u32[]{:S(2)}) collective-permute-start(bf16[2,256,256]{2,1,0:T(8,128)(2,1)S(1)} %collective-permute-done.5.mine2_ref), channel_id=1, source_target_pairs={{0,64},{64,0},{128,192},{192,128},{1,65},{65,1},{129,193},{193,129... | collective-permute-start | bytes 786440 | tf_op jit(solution)/shard_map/ppermute | solution.py:349
  41.2 1.3 %collective-permute-start.6 = (bf16[256,256]{1,0:T(8,128)(2,1)S(1)}, bf16[256,256]{1,0:T(8,128)(2,1)S(1)}, u32[]{:S(2)}, u32[]{:S(2)}) collective-permute-start(bf16[256,256]{1,0:T(8,128)(2,1)S(1)} %collective-permute-done.4.near_ref.mine1_ref), channel_id=1, source_target_pairs={{0,64},{64,0},{128,192},{192,128},{1,65},{65,1},{129,193},{193,129... | collective-permute-start | bytes 393224 | tf_op jit(solution)/shard_map/ppermute | solution.py:349
  44.7 4.8 %collective-permute-start.8 = (bf16[2,4,2,64,256]{4,3,2,1,0:T(8,128)(2,1)S(1)}, bf16[2,4,2,64,256]{4,3,2,1,0:T(8,128)(2,1)S(1)}, u32[]{:S(2)}, u32[]{:S(2)}) collective-permute-start(bf16[2,4,2,64,256]{4,3,2,1,0:T(8,128)(2,1)S(1)} %get-tuple-element.35), channel_id=1, source_target_pairs={{0,64},{64,0},{128,192},{192,128},{1,65},{65,1},{129,193},{193,129... | collective-permute-start | bytes 1572872 | tf_op jit(solution)/shard_map/ppermute | solution.py:349
  49.5 7.6 %collective-permute-start.9 = (bf16[4,2,64,256]{3,2,1,0:T(8,128)(2,1)S(1)}, bf16[4,2,64,256]{3,2,1,0:T(8,128)(2,1)S(1)}, u32[]{:S(2)}, u32[]{:S(2)}) collective-permute-start(bf16[4,2,64,256]{3,2,1,0:T(8,128)(2,1)S(1)} %fusion), channel_id=1, source_target_pairs={{0,128},{64,192},{128,0},{192,64},{1,129},{65,193},{129,1},{193,65... | collective-permute-start | bytes 786440 | tf_op jit(solution)/shard_map/ppermute | solution.py:349
  49.6 12.6 %all-to-all-start.1 = ((bf16[16,16,256]{2,1,0:T(8,128)(2,1)}), bf16[16,16,256]{2,1,0:T(8,128)(2,1)S(1)}, u32[]{:S(2)}, u32[]{:S(2)}) async-start(bf16[16,16,256]{2,1,0:T(8,128)(2,1)} %bitcast.9), calls=%async_computation.1 | async-start | bytes 262144 | tf_op jit(solution)/shard_map/all_to_all | solution.py:365
  57.3 5.3 %collective-permute-start.12 = (bf16[2,64,256]{2,1,0:T(8,128)(2,1)S(1)}, bf16[2,64,256]{2,1,0:T(8,128)(2,1)S(1)}, u32[]{:S(2)}, u32[]{:S(2)}) collective-permute-start(bf16[2,64,256]{2,1,0:T(8,128)(2,1)S(1)} %get-tuple-element.45), channel_id=1, source_target_pairs={{0,3},{1,2},{2,1},{3,0},{4,7},{5,6},{6,5},{7,4},{8,11},{9,10},{10,... | collective-permute-start | bytes 196616 | tf_op jit(solution)/shard_map/ppermute | solution.py:349
  57.4 8.8 %collective-permute-start.11 = (bf16[2,64,256]{2,1,0:T(8,128)(2,1)S(1)}, bf16[2,64,256]{2,1,0:T(8,128)(2,1)S(1)}, u32[]{:S(2)}, u32[]{:S(2)}) collective-permute-start(bf16[2,64,256]{2,1,0:T(8,128)(2,1)S(1)} %get-tuple-element.46), channel_id=1, source_target_pairs={{0,2},{1,3},{2,0},{3,1},{4,6},{5,7},{6,4},{7,5},{8,10},{9,11},{10,... | collective-permute-start | bytes 196616 | tf_op jit(solution)/shard_map/ppermute | solution.py:349
  62.0 4.2 %collective-permute-start.10 = (bf16[2,64,256]{2,1,0:T(8,128)(2,1)S(1)}, bf16[2,64,256]{2,1,0:T(8,128)(2,1)S(1)}, u32[]{:S(2)}, u32[]{:S(2)}) collective-permute-start(bf16[2,64,256]{2,1,0:T(8,128)(2,1)S(1)} %get-tuple-element.47), channel_id=1, source_target_pairs={{0,1},{1,0},{2,3},{3,2},{4,5},{5,4},{6,7},{7,6},{8,9},{9,8},{10,11... | collective-permute-start | bytes 196616 | tf_op jit(solution)/shard_map/ppermute | solution.py:349
  67.0 3.9 %collective-permute-start.15 = (bf16[2,64,256]{2,1,0:T(8,128)(2,1)S(1)}, bf16[2,64,256]{2,1,0:T(8,128)(2,1)S(1)}, u32[]{:S(2)}, u32[]{:S(2)}) collective-permute-start(bf16[2,64,256]{2,1,0:T(8,128)(2,1)S(1)} %get-tuple-element.40.own_ref), channel_id=1, source_target_pairs={{0,192},{64,128},{128,64},{192,0},{1,193},{65,129},{129,65},{193,1... | collective-permute-start | bytes 196616 | tf_op jit(solution)/shard_map/ppermute | solution.py:349
  69.0 4.9 %collective-permute-start.14 = (bf16[2,64,256]{2,1,0:T(8,128)(2,1)S(1)}, bf16[2,64,256]{2,1,0:T(8,128)(2,1)S(1)}, u32[]{:S(2)}, u32[]{:S(2)}) collective-permute-start(bf16[2,64,256]{2,1,0:T(8,128)(2,1)S(1)} %get-tuple-element.40.own_ref), channel_id=1, source_target_pairs={{0,128},{64,192},{128,0},{192,64},{1,129},{65,193},{129,1},{193,65... | collective-permute-start | bytes 196616 | tf_op jit(solution)/shard_map/ppermute | solution.py:349
  70.6 3.2 %collective-permute-start.13 = (bf16[2,64,256]{2,1,0:T(8,128)(2,1)S(1)}, bf16[2,64,256]{2,1,0:T(8,128)(2,1)S(1)}, u32[]{:S(2)}, u32[]{:S(2)}) collective-permute-start(bf16[2,64,256]{2,1,0:T(8,128)(2,1)S(1)} %get-tuple-element.40.own_ref), channel_id=1, source_target_pairs={{0,64},{64,0},{128,192},{192,128},{1,65},{65,1},{129,193},{193,129... | collective-permute-start | bytes 196616 | tf_op jit(solution)/shard_map/ppermute | solution.py:349

commit v4 on v3

--- a/solution.py
+++ b/solution.py
@@ -291,16 +291,17 @@
                 keep_ref[far] = chunk
 
 
-def combine_kernel(
-    returned_ref, place_ref, residual_ref, land_ref, part_ref, a_ref, b_ref, c_ref, block_ref, total_ref
-):
+def total_kernel(returned_ref, part_ref, a_ref, b_ref, c_ref, total_ref):
+    total = part_ref[...] + a_ref[...].astype(F32)
+    total_ref[...] = (total + b_ref[...].astype(F32) + c_ref[...].astype(F32)).astype(BF)
+
+
+def combine_kernel(returned_ref, place_ref, residual_ref, land_ref, block_ref):
     rows = dot(place_ref[...], returned_ref[...])
     land = column(land_ref[...]).astype(F32)
     block_ref[...] = (
         (land * (residual_ref[...].astype(F32) + rows)).astype(BF).reshape(ROWS, COLS, D)
     )
-    total = part_ref[...] + a_ref[...].astype(F32)
-    total_ref[...] = (total + b_ref[...].astype(F32) + c_ref[...].astype(F32)).astype(BF)
 
 
 def gather_kernel(own_ref, a_ref, b_ref, c_ref, up_ref, down_ref):
@@ -468,10 +469,9 @@
     far = swap(sent, "lat", 2)
     part = keep[0] + near[0].astype(F32) + far.astype(F32)
     others = [swap(part[mask].astype(BF), "lon", mask) for mask in (1, 2, 3)]
-    block, total = call(
-        combine_kernel,
-        [((ROWS, COLS, D), BF), ((2, 64, D), BF)],
-        (returned, place, residual, land, part[0], *others),
+    (total,) = call(total_kernel, [((2, 64, D), BF)], (returned, part[0], *others))
+    (block,) = call(
+        combine_kernel, [((ROWS, COLS, D), BF)], (returned, place, residual, land)
     )
     grad_up, grad_down = call(
         gather_kernel,

time: 75.1 us -> 74.5 us (level)
    pallas_call x7 -> x8, Pallas kernels: 11.3 us -> 11.3 us  [call(): pl.pallas_call(fetching if fetch else kernel, out_shape=[jax.ShapeDtypeSt...]
  transfers between devices with their start and end apart: 18 -> 18, of which waited for: 10 -> 9; matrix products, arithmetic and copies ran while one was open for 0% -> 0% of each run, Pallas kernels for 3% -> 5%
where the time goes in v4:
time: 74.5 us; the launch traced here: 74.1 us
  starting transfers between devices  36.4 us (49%)
  waiting for transfers between devices  24.4 us (33%)
  Pallas kernels  11.3 us (15%)
  between operations  0.92 us (1%)
    ppermute x12, waiting for transfers between devices, swap(): lax.ppermute(value, axis, [(i, i ^ mask) for i in range(lax.axis_size(axi...  22.6 us
    ppermute x4, starting transfers between devices, pair_up(): return lax.ppermute(value, axis, pairs)  14.2 us
    ppermute x12, starting transfers between devices, swap(): lax.ppermute(value, axis, [(i, i ^ mask) for i in range(lax.axis_size(axi...  13.6 us
    pallas_call x8, Pallas kernels, call(): pl.pallas_call(fetching if fetch else kernel, out_shape=[jax.ShapeDtypeSt...  11.3 us
    all_to_all x2, starting transfers between devices, exchange(): lax.all_to_all(value, ('lat', 'lon'), 0, 0, axis_index_groups=expert_grou...  8.61 us
    ppermute x4, waiting for transfers between devices, pair_up(): return lax.ppermute(value, axis, pairs)  1.8 us
  transfers between devices with their start and end apart: 18, of which 9 were waited for; matrix products, arithmetic and copies ran while one was open for 0% of the time, Pallas kernels for 5%

profile of v4, /device:TPU:1, one launch (start us, length us, event | category | flops | bytes accessed | tf_op | source)
XLA Modules:
  0.0 74.1 jit_solution(10372478833355028772)
XLA Ops:
  0.6 1.6 %shard_map.148 = (bf16[16,8,256]{2,1,0:T(8,128)(2,1)}, bf16[3,8,256]{2,1,0:T(8,128)(2,1)}, bf16[3,8,256]{2,1,0:T(8,128)(2,1)}) custom-call(bf16[128,256]{1,0:T(8,128)(2,1)} %bitcast.27, s32[8,16]{1,0:T(8,128)} %bitcast.28), custom_call_target="tpu_custom_call" | custom-call | tf_op jit(solution)/shard_map/pallas_call | solution.py:331
  2.3 0.0 copy-start.14
  2.3 3.3 %collective-permute-start = (bf16[3,8,256]{2,1,0:T(8,128)(2,1)}, bf16[3,8,256]{2,1,0:T(8,128)(2,1)S(1)}, u32[]{:S(2)}, u32[]{:S(2)}) collective-permute-start(bf16[3,8,256]{2,1,0:T(8,128)(2,1)} %get-tuple-element.21), channel_id=1, source_target_pairs={{0,64},{64,0},{128,192},{192,128},{1,65},{65,1},{129,193},{193,129... | collective-permute-start | bytes 36872 | tf_op jit(solution)/shard_map/ppermute | solution.py:346
  5.6 2.0 %collective-permute-start.1 = (bf16[3,8,256]{2,1,0:T(8,128)(2,1)}, bf16[3,8,256]{2,1,0:T(8,128)(2,1)S(1)}, u32[]{:S(2)}, u32[]{:S(2)}) collective-permute-start(bf16[3,8,256]{2,1,0:T(8,128)(2,1)} %get-tuple-element.22), channel_id=1, source_target_pairs={{64,128},{128,64},{65,129},{129,65},{66,130},{130,66},{67,131},{13... | collective-permute-start | bytes 36872 | tf_op jit(solution)/shard_map/ppermute | solution.py:346
  7.7 1.7 %shard_map.150.half_ref = bf16[256,256]{1,0:T(8,128)(2,1)} custom-call(bf16[256,256]{1,0:T(8,128)(2,1)} %up_ref.1, bf16[256,256]{1,0:T(8,128)(2,1)} %down_ref.1), custom_call_target="tpu_custom_call" | custom-call | tf_op jit(solution)/shard_map/pallas_call | solution.py:331
  9.3 0.0 copy-start.5
  9.4 1.1 %collective-permute-start.4 = (bf16[256,256]{1,0:T(8,128)(2,1)}, bf16[256,256]{1,0:T(8,128)(2,1)S(1)}, u32[]{:S(2)}, u32[]{:S(2)}) collective-permute-start(bf16[256,256]{1,0:T(8,128)(2,1)} %shard_map.150.half_ref), channel_id=1, source_target_pairs={{0,1},{1,0},{2,3},{3,2},{4,5},{5,4},{6,7},{7,6},{8,9},{9,8},{10,11... | collective-permute-start | bytes 393224 | tf_op jit(solution)/shard_map/ppermute | solution.py:350
  10.5 0.0 collective-permute-done.lat_even_ref
  10.5 0.5 collective-permute-done.1.lat_odd_ref
  11.0 0.0 copy-start.1
  11.0 0.0 copy-start.8
  11.0 0.0 copy-start.9
  11.0 0.0 copy-start.11
  11.1 0.0 copy-start.13
  11.1 0.1 broadcast_select_fusion
  11.1 0.0 copy-start.10
  11.1 0.0 copy-start.7
  11.2 8.9 %collective-permute-start.3 = (bf16[22,4,256]{2,1,0:T(4,128)(2,1)S(1)}, bf16[22,4,256]{2,1,0:T(4,128)(2,1)S(1)}, u32[]{:S(2)}, u32[]{:S(2)}) collective-permute-start(bf16[22,4,256]{2,1,0:T(4,128)(2,1)S(1)} %get-tuple-element.44), channel_id=1, source_target_pairs={{1,2},{2,1},{3,4},{4,3},{5,6},{6,5},{7,8},{8,7},{9,10},{10,9},{11,... | collective-permute-start | bytes 135176 | tf_op jit(solution)/shard_map/ppermute | solution.py:346
  20.0 0.0 collective-permute-start.2
  20.0 0.0 copy-done.5
  20.0 0.0 copy-done.1
  20.1 0.0 copy-done.8
  20.1 0.0 copy-done.9
  20.1 0.0 copy-done.11
  20.1 0.0 copy-done.13
  20.1 0.0 copy-done.10
  20.1 0.0 copy-done.7
  20.1 0.6 copy-done.12
  20.7 0.9 %shard_map.149 = (f32[128,128]{1,0:T(8,128)S(1)}, bf16[128,256]{1,0:T(8,128)(2,1)S(1)}, bf16[256,256]{1,0:T(8,128)(2,1)S(1)}, bf16[128,768]{1,0:T(8,128)(2,1)S(1)}, f32[2,256]{1,0:T(2,128)S(1)}) custom-call(f32[8,49]{1,0:T(8,128)S(1)} %copy-done.10, bf16[49,2048]{1,0:T(8,128)(2,1)S(1)} %copy-done.5, f32[1,2048]{1,0:T(1,128)S(1)} %copy-done.9, ...), custom_call_target="tpu_custom_call" | custom-call | tf_op jit(solution)/shard_map/pallas_call | solution.py:331
  21.6 0.0 collective-permute-done.3.lon_odd_ref
  21.6 1.3 %collective-permute-done.2.lon_even_ref = bf16[22,4,256]{2,1,0:T(4,128)(2,1)S(1)} collective-permute-done((bf16[22,4,256]{2,1,0:T(4,128)(2,1)S(1)}, bf16[22,4,256]{2,1,0:T(4,128)(2,1)S(1)}, u32[]{:S(2)}, u32[]{:S(2)}) %collective-permute-start.2) | collective-permute-done | bytes 45088 | tf_op jit(solution)/shard_map/ppermute | solution.py:346
  22.9 0.0 collective-permute-done.4.near_ref.mine1_ref
  22.9 3.4 %shard_map.151 = (bf16[128,256]{1,0:T(8,128)(2,1)S(1)}, bf16[256,512]{1,0:T(8,128)(2,1)}, bf16[2,256,256]{2,1,0:T(8,128)(2,1)S(1)}) custom-call(bf16[16,8,256]{2,1,0:T(8,128)(2,1)S(1)} %copy-done.1, bf16[3,8,256]{2,1,0:T(8,128)(2,1)S(1)} %collective-permute-done.lat_even_ref, bf16[3,8,256]{2,1,0:T(8,128)(2,1)S(1)} %collective-permute-done.1.lat_odd_ref, ...), custom_call_target="tpu_custom_call" | custom-call | tf_op jit(solution)/shard_map/pallas_call | solution.py:331
  26.3 0.0 collective-permute-start.5
  26.3 4.9 %all-to-all-start = ((bf16[16,16,512]{2,1,0:T(8,128)(2,1)}), bf16[16,16,512]{2,1,0:T(8,128)(2,1)S(1)}, u32[]{:S(2)}, u32[]{:S(2)}) async-start(bf16[16,16,512]{2,1,0:T(8,128)(2,1)} %bitcast.6), calls=%async_computation | async-start | bytes 524288 | tf_op jit(solution)/shard_map/all_to_all | solution.py:366
  31.2 9.5 %collective-permute-done.5.mine2_ref = bf16[2,256,256]{2,1,0:T(8,128)(2,1)S(1)} collective-permute-done((bf16[2,256,256]{2,1,0:T(8,128)(2,1)S(1)}, bf16[2,256,256]{2,1,0:T(8,128)(2,1)S(1)}, u32[]{:S(2)}, u32[]{:S(2)}) %collective-permute-start.5) | collective-permute-done | bytes 262176 | tf_op jit(solution)/shard_map/ppermute | solution.py:350
  40.7 0.5 collective-permute-start.7
  41.2 0.0 collective-permute-start.6
  41.3 1.3 %collective-permute-done.6.other1_ref = bf16[256,256]{1,0:T(8,128)(2,1)S(1)} collective-permute-done((bf16[256,256]{1,0:T(8,128)(2,1)S(1)}, bf16[256,256]{1,0:T(8,128)(2,1)S(1)}, u32[]{:S(2)}, u32[]{:S(2)}) %collective-permute-start.6) | collective-permute-done | bytes 131104 | tf_op jit(solution)/shard_map/ppermute | solution.py:350
  42.6 0.0 all-to-all-done
  42.6 0.0 collective-permute-done.7.other2_ref
  42.6 2.1 %shard_map.152 = (bf16[256,256]{1,0:T(8,128)(2,1)}, f32[2,4,2,64,256]{4,3,2,1,0:T(8,128)S(1)}, bf16[2,4,2,64,256]{4,3,2,1,0:T(8,128)(2,1)S(1)}) custom-call(bf16[256,512]{1,0:T(8,128)(2,1)S(1)} %bitcast.26, bf16[256,256]{1,0:T(8,128)(2,1)S(1)} %copy-done.2, bf16[256,256]{1,0:T(8,128)(2,1)S(1)} %copy-done.3, ...), custom_call_target="tpu_custom_call" | custom-call | tf_op jit(solution)/shard_map/pallas_call | solution.py:331
  44.7 3.3 %collective-permute-start.8 = (bf16[2,4,2,64,256]{4,3,2,1,0:T(8,128)(2,1)S(1)}, bf16[2,4,2,64,256]{4,3,2,1,0:T(8,128)(2,1)S(1)}, u32[]{:S(2)}, u32[]{:S(2)}) collective-permute-start(bf16[2,4,2,64,256]{4,3,2,1,0:T(8,128)(2,1)S(1)} %get-tuple-element.33), channel_id=1, source_target_pairs={{0,64},{64,0},{128,192},{192,128},{1,65},{65,1},{129,193},{193,129... | collective-permute-start | bytes 1572872 | tf_op jit(solution)/shard_map/ppermute | solution.py:350
  47.9 1.5 %collective-permute-done.8 = bf16[2,4,2,64,256]{4,3,2,1,0:T(8,128)(2,1)S(1)} collective-permute-done((bf16[2,4,2,64,256]{4,3,2,1,0:T(8,128)(2,1)S(1)}, bf16[2,4,2,64,256]{4,3,2,1,0:T(8,128)(2,1)S(1)}, u32[]{:S(2)}, u32[]{:S(2)}) %collective-permute-start.8) | collective-permute-done | bytes 524320 | tf_op jit(solution)/shard_map/ppermute | solution.py:350
  49.5 0.1 fusion
  49.5 0.1 collective-permute-start.9
  49.6 3.7 %all-to-all-start.1 = ((bf16[16,16,256]{2,1,0:T(8,128)(2,1)}), bf16[16,16,256]{2,1,0:T(8,128)(2,1)S(1)}, u32[]{:S(2)}, u32[]{:S(2)}) async-start(bf16[16,16,256]{2,1,0:T(8,128)(2,1)} %bitcast.9), calls=%async_computation.1 | async-start | bytes 262144 | tf_op jit(solution)/shard_map/all_to_all | solution.py:366
  53.4 3.8 %collective-permute-done.9 = bf16[4,2,64,256]{3,2,1,0:T(8,128)(2,1)S(1)} collective-permute-done((bf16[4,2,64,256]{3,2,1,0:T(8,128)(2,1)S(1)}, bf16[4,2,64,256]{3,2,1,0:T(8,128)(2,1)S(1)}, u32[]{:S(2)}, u32[]{:S(2)}) %collective-permute-start.9) | collective-permute-done | bytes 262176 | tf_op jit(solution)/shard_map/ppermute | solution.py:350
  57.2 0.1 fusion.1
  57.3 0.1 collective-permute-start.12
  57.4 4.6 %collective-permute-start.11 = (bf16[2,64,256]{2,1,0:T(8,128)(2,1)S(1)}, bf16[2,64,256]{2,1,0:T(8,128)(2,1)S(1)}, u32[]{:S(2)}, u32[]{:S(2)}) collective-permute-start(bf16[2,64,256]{2,1,0:T(8,128)(2,1)S(1)} %get-tuple-element.42), channel_id=1, source_target_pairs={{0,2},{1,3},{2,0},{3,1},{4,6},{5,7},{6,4},{7,5},{8,10},{9,11},{10,... | collective-permute-start | bytes 196616 | tf_op jit(solution)/shard_map/ppermute | solution.py:350
  62.0 0.2 collective-permute-start.10
  62.2 0.0 all-to-all-done.1
  62.2 0.3 collective-permute-done.12.c_ref
  62.6 3.7 %collective-permute-done.11.b_ref = bf16[2,64,256]{2,1,0:T(8,128)(2,1)S(1)} collective-permute-done((bf16[2,64,256]{2,1,0:T(8,128)(2,1)S(1)}, bf16[2,64,256]{2,1,0:T(8,128)(2,1)S(1)}, u32[]{:S(2)}, u32[]{:S(2)}) %collective-permute-start.11) | collective-permute-done | bytes 65568 | tf_op jit(solution)/shard_map/ppermute | solution.py:350
  66.2 0.0 collective-permute-done.10.a_ref
  66.3 2.0 %collective-permute-start.15 = (bf16[2,64,256]{2,1,0:T(8,128)(2,1)S(1)}, bf16[2,64,256]{2,1,0:T(8,128)(2,1)S(1)}, u32[]{:S(2)}, u32[]{:S(2)}) collective-permute-start(bf16[2,64,256]{2,1,0:T(8,128)(2,1)S(1)} %shard_map.154.own_ref), channel_id=1, source_target_pairs={{0,192},{64,128},{128,64},{192,0},{1,193},{65,129},{129,65},{193,1... | collective-permute-start | bytes 196616 | tf_op jit(solution)/shard_map/ppermute | solution.py:350
  68.3 1.7 %collective-permute-start.14 = (bf16[2,64,256]{2,1,0:T(8,128)(2,1)S(1)}, bf16[2,64,256]{2,1,0:T(8,128)(2,1)S(1)}, u32[]{:S(2)}, u32[]{:S(2)}) collective-permute-start(bf16[2,64,256]{2,1,0:T(8,128)(2,1)S(1)} %shard_map.154.own_ref), channel_id=1, source_target_pairs={{0,128},{64,192},{128,0},{192,64},{1,129},{65,193},{129,1},{193,65... | collective-permute-start | bytes 196616 | tf_op jit(solution)/shard_map/ppermute | solution.py:350
  70.0 0.0 collective-permute-start.13
  70.0 0.8 %shard_map.153 = bf16[16,8,256]{2,1,0:T(8,128)(2,1)} custom-call(bf16[256,256]{1,0:T(8,128)(2,1)S(1)} %bitcast.25, bf16[128,256]{1,0:T(8,128)(2,1)S(1)} %get-tuple-element.27.place_ref, bf16[128,256]{1,0:T(8,128)(2,1)S(1)} %get-tuple-element.35.residual_ref, s32[8,16]{1,0:T(8,128)S(1)} %bitcast.31), custom_call_target="tpu_custom_call" | custom-call | tf_op jit(solution)/shard_map/pallas_call | solution.py:331
  70.8 0.0 collective-permute-done.15.c_ref
  70.8 2.5 %collective-permute-done.14.b_ref = bf16[2,64,256]{2,1,0:T(8,128)(2,1)S(1)} collective-permute-done((bf16[2,64,256]{2,1,0:T(8,128)(2,1)S(1)}, bf16[2,64,256]{2,1,0:T(8,128)(2,1)S(1)}, u32[]{:S(2)}, u32[]{:S(2)}) %collective-permute-start.14) | collective-permute-done | bytes 65568 | tf_op jit(solution)/shard_map/ppermute | solution.py:350
  73.2 0.0 collective-permute-done.13.a_ref
  73.2 0.8 %shard_map.155 = (f32[256,256]{1,0:T(8,128)}, f32[256,256]{1,0:T(8,128)}) custom-call(bf16[2,64,256]{2,1,0:T(8,128)(2,1)S(1)} %shard_map.154.own_ref, bf16[2,64,256]{2,1,0:T(8,128)(2,1)S(1)} %collective-permute-done.13.a_ref, bf16[2,64,256]{2,1,0:T(8,128)(2,1)S(1)} %collective-permute-done.14.b_ref, bf16[2,64,256]{2,1,0:T(8,128)(2,1)S(1)} %collective-permute-done.15.c_ref), custom_call_target="tpu_custom_call" | custom-call | tf_op jit(solution)/shard_map/pallas_call | solution.py:331
  (17 shorter events, 0.1 us)
Async XLA Ops:
  2.3 8.7 %copy-start.14 = (bf16[16,8,256]{2,1,0:T(8,128)(2,1)S(1)}, bf16[16,8,256]{2,1,0:T(8,128)(2,1)}, u32[]{:S(2)}) copy-start(bf16[16,8,256]{2,1,0:T(8,128)(2,1)} %get-tuple-element.23) | copy-start | bytes 196612
  2.3 8.2 %collective-permute-start = (bf16[3,8,256]{2,1,0:T(8,128)(2,1)}, bf16[3,8,256]{2,1,0:T(8,128)(2,1)S(1)}, u32[]{:S(2)}, u32[]{:S(2)}) collective-permute-start(bf16[3,8,256]{2,1,0:T(8,128)(2,1)} %get-tuple-element.21), channel_id=1, source_target_pairs={{0,64},{64,0},{128,192},{192,128},{1,65},{65,1},{129,193},{193,129... | collective-permute-start | bytes 36872 | tf_op jit(solution)/shard_map/ppermute | solution.py:346
  5.6 14.4 %copy-start = (bf16[256,768]{1,0:T(8,128)(2,1)S(1)}, bf16[256,768]{1,0:T(8,128)(2,1)}, u32[]{:S(2)}) copy-start(bf16[256,768]{1,0:T(8,128)(2,1)} %project_ref.3) | copy-start | bytes 1179652
  5.6 5.3 %collective-permute-start.1 = (bf16[3,8,256]{2,1,0:T(8,128)(2,1)}, bf16[3,8,256]{2,1,0:T(8,128)(2,1)S(1)}, u32[]{:S(2)}, u32[]{:S(2)}) collective-permute-start(bf16[3,8,256]{2,1,0:T(8,128)(2,1)} %get-tuple-element.22), channel_id=1, source_target_pairs={{64,128},{128,64},{65,129},{129,65},{66,130},{130,66},{67,131},{13... | collective-permute-start | bytes 36872 | tf_op jit(solution)/shard_map/ppermute | solution.py:346
  9.3 10.7 %copy-start.5 = (bf16[49,2048]{1,0:T(8,128)(2,1)S(1)}, bf16[49,2048]{1,0:T(8,128)(2,1)}, u32[]{:S(2)}) copy-start(bf16[49,2048]{1,0:T(8,128)(2,1)} %constant.17.clone.taps_ref) | copy-start | bytes 602116
  9.4 13.6 %collective-permute-start.4 = (bf16[256,256]{1,0:T(8,128)(2,1)}, bf16[256,256]{1,0:T(8,128)(2,1)S(1)}, u32[]{:S(2)}, u32[]{:S(2)}) collective-permute-start(bf16[256,256]{1,0:T(8,128)(2,1)} %shard_map.150.half_ref), channel_id=1, source_target_pairs={{0,1},{1,0},{2,3},{3,2},{4,5},{5,4},{6,7},{7,6},{8,9},{9,8},{10,11... | collective-permute-start | bytes 393224 | tf_op jit(solution)/shard_map/ppermute | solution.py:350
  11.0 9.0 %copy-start.1 = (bf16[16,8,256]{2,1,0:T(8,128)(2,1)S(1)}, bf16[16,8,256]{2,1,0:T(8,128)(2,1)}, u32[]{:S(2)}) copy-start(bf16[16,8,256]{2,1,0:T(8,128)(2,1)} %own_ref.1) | copy-start | bytes 196612
  11.0 9.0 %copy-start.8 = (bf16[16,8,256]{2,1,0:T(8,128)(2,1)S(1)}, bf16[16,8,256]{2,1,0:T(8,128)(2,1)}, u32[]{:S(2)}) copy-start(bf16[16,8,256]{2,1,0:T(8,128)(2,1)} %cot_ref.1) | copy-start | bytes 196612
  11.0 9.0 %copy-start.9 = (f32[1,2048]{1,0:T(1,128)S(1)}, f32[1,2048]{1,0:T(1,128)}, u32[]{:S(2)}) copy-start(f32[1,2048]{1,0:T(1,128)} %constant.18.clone.outside_ref) | copy-start | bytes 24580
  11.0 9.0 %copy-start.11 = (s32[1,1,16,8,1]{2,4,3,1,0:T(1,128)S(1)}, s32[1,1,16,8,1]{2,4,3,1,0:T(1,128)}, u32[]{:S(2)}) copy-start(s32[1,1,16,8,1]{2,4,3,1,0:T(1,128)} %param.16) | copy-start | bytes 1540
  11.1 9.0 %copy-start.13 = (f32[256]{0:T(256)S(1)}, f32[256]{0:T(256)}, u32[]{:S(2)}) copy-start(f32[256]{0:T(256)} %param.18) | copy-start | bytes 3076
  11.1 9.0 %copy-start.10 = (f32[8,49]{1,0:T(8,128)S(1)}, f32[8,49]{1,0:T(8,128)}, u32[]{:S(2)}) copy-start(f32[8,49]{1,0:T(8,128)} %pos_ref.1) | copy-start | bytes 4708
  11.1 9.0 %copy-start.7 = (s32[16,8]{0,1:T(8,128)S(1)}, s32[16,8]{0,1:T(8,128)}, u32[]{:S(2)}) copy-start(s32[16,8]{0,1:T(8,128)} %param.15) | copy-start | bytes 1540
  11.2 10.5 %collective-permute-start.3 = (bf16[22,4,256]{2,1,0:T(4,128)(2,1)S(1)}, bf16[22,4,256]{2,1,0:T(4,128)(2,1)S(1)}, u32[]{:S(2)}, u32[]{:S(2)}) collective-permute-start(bf16[22,4,256]{2,1,0:T(4,128)(2,1)S(1)} %get-tuple-element.44), channel_id=1, source_target_pairs={{1,2},{2,1},{3,4},{4,3},{5,6},{6,5},{7,8},{8,7},{9,10},{10,9},{11,... | collective-permute-start | bytes 135176 | tf_op jit(solution)/shard_map/ppermute | solution.py:346
  20.0 2.9 %collective-permute-start.2 = (bf16[22,4,256]{2,1,0:T(4,128)(2,1)S(1)}, bf16[22,4,256]{2,1,0:T(4,128)(2,1)S(1)}, u32[]{:S(2)}, u32[]{:S(2)}) collective-permute-start(bf16[22,4,256]{2,1,0:T(4,128)(2,1)S(1)} %get-tuple-element.45), channel_id=1, source_target_pairs={{0,1},{1,0},{2,3},{3,2},{4,5},{5,4},{6,7},{7,6},{8,9},{9,8},{10,11... | collective-permute-start | bytes 135176 | tf_op jit(solution)/shard_map/ppermute | solution.py:346
  20.0 0.7 copy-start.12
  20.7 2.2 %copy-start.4 = (bf16[256,256]{1,0:T(8,128)(2,1)S(1)}, bf16[256,256]{1,0:T(8,128)(2,1)}, u32[]{:S(2)}) copy-start(bf16[256,256]{1,0:T(8,128)(2,1)} %shard_map.150.half_ref) | copy-start | bytes 393220
  20.7 2.2 %copy-start.6 = (bf16[256,256]{1,0:T(8,128)(2,1)S(1)}, bf16[256,256]{1,0:T(8,128)(2,1)}, u32[]{:S(2)}) copy-start(bf16[256,256]{1,0:T(8,128)(2,1)} %out_ref.1) | copy-start | bytes 393220
  26.3 14.4 %collective-permute-start.5 = (bf16[2,256,256]{2,1,0:T(8,128)(2,1)S(1)}, bf16[2,256,256]{2,1,0:T(8,128)(2,1)S(1)}, u32[]{:S(2)}, u32[]{:S(2)}) collective-permute-start(bf16[2,256,256]{2,1,0:T(8,128)(2,1)S(1)} %get-tuple-element.30), channel_id=1, source_target_pairs={{0,2},{1,3},{2,0},{3,1},{4,6},{5,7},{6,4},{7,5},{8,10},{9,11},{10,... | collective-permute-start | bytes 786440 | tf_op jit(solution)/shard_map/ppermute | solution.py:350
  26.3 16.3 %copy-start.2 = (bf16[256,256]{1,0:T(8,128)(2,1)S(1)}, bf16[256,256]{1,0:T(8,128)(2,1)}, u32[]{:S(2)}) copy-start(bf16[256,256]{1,0:T(8,128)(2,1)} %up_ref.1) | copy-start | bytes 393220
  26.3 16.3 %copy-start.3 = (bf16[256,256]{1,0:T(8,128)(2,1)S(1)}, bf16[256,256]{1,0:T(8,128)(2,1)}, u32[]{:S(2)}) copy-start(bf16[256,256]{1,0:T(8,128)(2,1)} %down_ref.1) | copy-start | bytes 393220
  26.3 16.2 %all-to-all-start = ((bf16[16,16,512]{2,1,0:T(8,128)(2,1)}), bf16[16,16,512]{2,1,0:T(8,128)(2,1)S(1)}, u32[]{:S(2)}, u32[]{:S(2)}) async-start(bf16[16,16,512]{2,1,0:T(8,128)(2,1)} %bitcast.6), calls=%async_computation | async-start | bytes 524288 | tf_op jit(solution)/shard_map/all_to_all | solution.py:366
  40.7 1.8 %collective-permute-start.7 = (bf16[2,256,256]{2,1,0:T(8,128)(2,1)S(1)}, bf16[2,256,256]{2,1,0:T(8,128)(2,1)S(1)}, u32[]{:S(2)}, u32[]{:S(2)}) collective-permute-start(bf16[2,256,256]{2,1,0:T(8,128)(2,1)S(1)} %collective-permute-done.5.mine2_ref), channel_id=1, source_target_pairs={{0,64},{64,0},{128,192},{192,128},{1,65},{65,1},{129,193},{193,129... | collective-permute-start | bytes 786440 | tf_op jit(solution)/shard_map/ppermute | solution.py:350
  41.2 1.3 %collective-permute-start.6 = (bf16[256,256]{1,0:T(8,128)(2,1)S(1)}, bf16[256,256]{1,0:T(8,128)(2,1)S(1)}, u32[]{:S(2)}, u32[]{:S(2)}) collective-permute-start(bf16[256,256]{1,0:T(8,128)(2,1)S(1)} %collective-permute-done.4.near_ref.mine1_ref), channel_id=1, source_target_pairs={{0,64},{64,0},{128,192},{192,128},{1,65},{65,1},{129,193},{193,129... | collective-permute-start | bytes 393224 | tf_op jit(solution)/shard_map/ppermute | solution.py:350
  44.7 4.8 %collective-permute-start.8 = (bf16[2,4,2,64,256]{4,3,2,1,0:T(8,128)(2,1)S(1)}, bf16[2,4,2,64,256]{4,3,2,1,0:T(8,128)(2,1)S(1)}, u32[]{:S(2)}, u32[]{:S(2)}) collective-permute-start(bf16[2,4,2,64,256]{4,3,2,1,0:T(8,128)(2,1)S(1)} %get-tuple-element.33), channel_id=1, source_target_pairs={{0,64},{64,0},{128,192},{192,128},{1,65},{65,1},{129,193},{193,129... | collective-permute-start | bytes 1572872 | tf_op jit(solution)/shard_map/ppermute | solution.py:350
  49.5 7.6 %collective-permute-start.9 = (bf16[4,2,64,256]{3,2,1,0:T(8,128)(2,1)S(1)}, bf16[4,2,64,256]{3,2,1,0:T(8,128)(2,1)S(1)}, u32[]{:S(2)}, u32[]{:S(2)}) collective-permute-start(bf16[4,2,64,256]{3,2,1,0:T(8,128)(2,1)S(1)} %fusion), channel_id=1, source_target_pairs={{0,128},{64,192},{128,0},{192,64},{1,129},{65,193},{129,1},{193,65... | collective-permute-start | bytes 786440 | tf_op jit(solution)/shard_map/ppermute | solution.py:350
  49.6 12.6 %all-to-all-start.1 = ((bf16[16,16,256]{2,1,0:T(8,128)(2,1)}), bf16[16,16,256]{2,1,0:T(8,128)(2,1)S(1)}, u32[]{:S(2)}, u32[]{:S(2)}) async-start(bf16[16,16,256]{2,1,0:T(8,128)(2,1)} %bitcast.9), calls=%async_computation.1 | async-start | bytes 262144 | tf_op jit(solution)/shard_map/all_to_all | solution.py:366
  57.3 5.3 %collective-permute-start.12 = (bf16[2,64,256]{2,1,0:T(8,128)(2,1)S(1)}, bf16[2,64,256]{2,1,0:T(8,128)(2,1)S(1)}, u32[]{:S(2)}, u32[]{:S(2)}) collective-permute-start(bf16[2,64,256]{2,1,0:T(8,128)(2,1)S(1)} %get-tuple-element.41), channel_id=1, source_target_pairs={{0,3},{1,2},{2,1},{3,0},{4,7},{5,6},{6,5},{7,4},{8,11},{9,10},{10,... | collective-permute-start | bytes 196616 | tf_op jit(solution)/shard_map/ppermute | solution.py:350
  57.4 8.8 %collective-permute-start.11 = (bf16[2,64,256]{2,1,0:T(8,128)(2,1)S(1)}, bf16[2,64,256]{2,1,0:T(8,128)(2,1)S(1)}, u32[]{:S(2)}, u32[]{:S(2)}) collective-permute-start(bf16[2,64,256]{2,1,0:T(8,128)(2,1)S(1)} %get-tuple-element.42), channel_id=1, source_target_pairs={{0,2},{1,3},{2,0},{3,1},{4,6},{5,7},{6,4},{7,5},{8,10},{9,11},{10,... | collective-permute-start | bytes 196616 | tf_op jit(solution)/shard_map/ppermute | solution.py:350
  62.0 4.2 %collective-permute-start.10 = (bf16[2,64,256]{2,1,0:T(8,128)(2,1)S(1)}, bf16[2,64,256]{2,1,0:T(8,128)(2,1)S(1)}, u32[]{:S(2)}, u32[]{:S(2)}) collective-permute-start(bf16[2,64,256]{2,1,0:T(8,128)(2,1)S(1)} %get-tuple-element.43), channel_id=1, source_target_pairs={{0,1},{1,0},{2,3},{3,2},{4,5},{5,4},{6,7},{7,6},{8,9},{9,8},{10,11... | collective-permute-start | bytes 196616 | tf_op jit(solution)/shard_map/ppermute | solution.py:350
  66.3 4.5 %collective-permute-start.15 = (bf16[2,64,256]{2,1,0:T(8,128)(2,1)S(1)}, bf16[2,64,256]{2,1,0:T(8,128)(2,1)S(1)}, u32[]{:S(2)}, u32[]{:S(2)}) collective-permute-start(bf16[2,64,256]{2,1,0:T(8,128)(2,1)S(1)} %shard_map.154.own_ref), channel_id=1, source_target_pairs={{0,192},{64,128},{128,64},{192,0},{1,193},{65,129},{129,65},{193,1... | collective-permute-start | bytes 196616 | tf_op jit(solution)/shard_map/ppermute | solution.py:350
  68.3 4.9 %collective-permute-start.14 = (bf16[2,64,256]{2,1,0:T(8,128)(2,1)S(1)}, bf16[2,64,256]{2,1,0:T(8,128)(2,1)S(1)}, u32[]{:S(2)}, u32[]{:S(2)}) collective-permute-start(bf16[2,64,256]{2,1,0:T(8,128)(2,1)S(1)} %shard_map.154.own_ref), channel_id=1, source_target_pairs={{0,128},{64,192},{128,0},{192,64},{1,129},{65,193},{129,1},{193,65... | collective-permute-start | bytes 196616 | tf_op jit(solution)/shard_map/ppermute | solution.py:350
  70.0 3.3 %collective-permute-start.13 = (bf16[2,64,256]{2,1,0:T(8,128)(2,1)S(1)}, bf16[2,64,256]{2,1,0:T(8,128)(2,1)S(1)}, u32[]{:S(2)}, u32[]{:S(2)}) collective-permute-start(bf16[2,64,256]{2,1,0:T(8,128)(2,1)S(1)} %shard_map.154.own_ref), channel_id=1, source_target_pairs={{0,64},{64,0},{128,192},{192,128},{1,65},{65,1},{129,193},{193,129... | collective-permute-start | bytes 196616 | tf_op jit(solution)/shard_map/ppermute | solution.py:350
